TPU v7x, 32 devices: a whole 2x2x4 slice. The times are simulated.
32 devices in a mesh: seq: 8 (over z, y), tp: 4 (over x, core).
Axes of the slice: x: 2, y: 2, z: 4, core: 2. Of those that a mesh axis runs over, the one named last changes fastest.
Arguments:
- residual: bfloat16 [2048, 2048], P('seq', 'tp'), may hold values from -6 to 6
- query_vectors: bfloat16 [2048, 2048], P('seq', 'tp'), may hold values from -6 to 6
- key_vectors: bfloat16 [2048, 2048], P('seq', 'tp'), may hold values from -6 to 6
- value_vectors: bfloat16 [2048, 2048], P('seq', 'tp'), may hold values from -6 to 6
- log_decay: float32 [16, 2048], P('tp', 'seq'), may hold values from -1 to 0, as said below
- norm_gain: float32 [2048], P('tp'), may hold values from 0.5 to 1.5
- out_weight: bfloat16 [2048, 2048], P('tp'), may hold values from -0.125 to 0.125
Outputs:
- mixed: bfloat16 [2048, 2048], P('seq', 'tp')
Inputs may be any that keep to these rules, and one draw needn't show every extreme that they name: `log_decay`: Log-decays are never positive.
All inputs are finite; a program needn't handle non-finite values.
Results may differ from a plain program's by a relative error of at most 0.005.
Values may be sent and summed in bfloat16 or wider, within the bound.
No kernel may reach another device: no remote copies, remote signals or barrier semaphores. Data moves between devices by JAX's collectives and lax.ppermute only.
A program may use at most 128 MiB of HBM per device.

v0:
```python
import functools

import jax
import jax.numpy as jnp
from jax import lax
from jax.experimental import pallas as pl
from jax.experimental.pallas import tpu as pltpu
from jax.sharding import PartitionSpec as P

HEAD_DIM = 128
GROUP = 256
SCALE = HEAD_DIM ** (-0.5)
F32 = jnp.float32
BF16 = jnp.bfloat16
VMEM = pl.BlockSpec(memory_space=pltpu.VMEM)
HBM = pl.BlockSpec(memory_space=pltpu.HBM)
ANY = pl.BlockSpec(memory_space=pl.ANY)
DECAY_ROWS = 16
MEMBERS = 4
PARAMS = pltpu.CompilerParams(vmem_limit_bytes=24 * 1024 * 1024)


def state_rows(j):
    return slice(j * HEAD_DIM, (j + 1) * HEAD_DIM)


def place():
    return lax.rem(lax.axis_index("seq"), MEMBERS)


def side():
    return lax.rem(lax.axis_index("seq"), 2)


def half_at(owner, size):
    return pl.ds(pl.multiple_of(owner * size, size), size)


def pick(owner, values, axis):
    half = values.shape[axis] // 2
    low = lax.slice_in_dim(values, 0, half, axis=axis)
    high = lax.slice_in_dim(values, half, 2 * half, axis=axis)
    return jnp.where(owner == 0, low, high)


def contract(a, b):
    return lax.dot_general(a, b, (((1,), (1,)), ((), ())), preferred_element_type=F32)


def positions():
    shape = (GROUP, GROUP)
    return lax.broadcasted_iota(jnp.int32, shape, 0), lax.broadcasted_iota(jnp.int32, shape, 1)


def three_terms(values):
    first = values.astype(BF16).astype(F32)
    second = (values - first).astype(BF16).astype(F32)
    third = values - first - second
    return jnp.concatenate([first, second, third], axis=0).astype(BF16)


def sums_down(mask, decays):
    heads = decays.shape[0]
    terms = contract(mask, three_terms(decays))
    return terms[:, :heads] + terms[:, heads : 2 * heads] + terms[:, 2 * heads :]


def sums_across(mask, decays):
    heads = decays.shape[0]
    terms = contract(three_terms(decays), mask)
    return terms[:heads] + terms[heads : 2 * heads] + terms[2 * heads :]


def decays_to_rows(decays):
    each = DECAY_ROWS // (2 * len(decays))
    wide = jnp.concatenate([jnp.broadcast_to(d, (each, HEAD_DIM)) for d in decays], axis=0)
    coarse = wide.astype(BF16).astype(F32)
    return jnp.concatenate([coarse, wide - coarse], axis=0).astype(BF16)


def rows_to_decays(rows, count):
    rows = rows.astype(F32)
    each = DECAY_ROWS // (2 * count)
    both = rows[: DECAY_ROWS // 2] + rows[DECAY_ROWS // 2 :]
    return [both[j * each : j * each + 1] for j in range(count)]


def state_kernel(half, *refs):
    sources, outs, held, sems = refs[:5], refs[5:7], refs[7:12], refs[12]
    copies = [
        pltpu.make_async_copy(source, target, sems.at[i])
        for i, (source, target) in enumerate(zip(sources, held))
    ]
    for copy in copies:
        copy.start()
    decay_ref, key_ref, value_ref = held[:3]
    me = side()
    row, col = positions()
    later = jnp.where(col > row, 1.0, 0.0).astype(BF16)
    copies[0].wait()
    decays = decay_ref[...]
    tail = jnp.exp(sums_across(later, decays))
    whole = jnp.exp(jnp.sum(decays, axis=1, keepdims=True))
    copies[1].wait()
    copies[2].wait()
    decay_rows = decays_to_rows([whole[h : h + 1] for h in range(2 * half)])
    for owner, out_ref in zip((1 - me, me), outs):
        factors = pick(owner, tail, 0)
        for j in range(half):
            at = half_at(owner * half + j, HEAD_DIM)
            weighted = (key_ref[:, at].T.astype(F32) * factors[j : j + 1, :]).astype(BF16)
            update = jnp.dot(weighted, value_ref[:, at], preferred_element_type=F32)
            out_ref[state_rows(j), :] = update.astype(BF16)
        out_ref[half * HEAD_DIM :, :] = decay_rows
    for copy in copies[3:]:
        copy.wait()


def local_kernel(heads, decay_ref, query_ref, key_ref, value_ref, intra_ref, own_ref):
    row, col = positions()
    causal = col <= row
    upto = jnp.where(causal, 1.0, 0.0).astype(BF16)
    decays = decay_ref[...]
    down = sums_down(upto, decays)
    across = sums_across(upto, decays)
    own_ref[...] = jnp.exp(down) * SCALE
    for h in range(heads):
        at = slice(h * HEAD_DIM, (h + 1) * HEAD_DIM)
        scores = contract(query_ref[:, at], key_ref[:, at])
        gaps = down[:, h : h + 1] - across[h : h + 1, :]
        weights = jnp.where(causal, jnp.exp(gaps), 0.0)
        probs = (scores * SCALE * weights).astype(BF16)
        intra_ref[:, at] = jnp.dot(probs, value_ref[:, at], preferred_element_type=F32)


def gather_kernel(half, steps, *refs):
    received, (before_ref, sent_ref, through_ref, total_ref, again_ref, held_ref) = (
        refs[: len(steps)],
        refs[len(steps) :],
    )
    me, upper = place(), side() == 1
    for step, message_ref in zip(steps, received):
        held_ref[me ^ step] = message_ref[...]
    later_pair = me >= 2
    decays = [rows_to_decays(held_ref[m, half * HEAD_DIM :, :], 2 * half) for m in range(MEMBERS)]
    totals = []
    for j in range(2 * half):
        low, high = (j, half + j) if j < half else (j, j - half)
        decay = [jnp.where(upper, d[high], d[low]) for d in decays]
        through = [jnp.ones((1, HEAD_DIM), F32)]
        for m in range(MEMBERS):
            through.append(through[m] * decay[m])
        first, last = [jnp.where(later_pair, through[2 + i], through[i]) for i in range(2)]
        factor = jnp.where(upper, last, first)
        through_ref[j * 8 : (j + 1) * 8, :] = jnp.broadcast_to(factor, (8, HEAD_DIM))
        if j >= half:
            continue
        at = state_rows(j)
        held = [jnp.zeros((HEAD_DIM, HEAD_DIM), F32)]
        for m in range(MEMBERS):
            held.append(held[m] * decay[m] + held_ref[m, at, :].astype(F32))
        first, last = [jnp.where(later_pair, held[2 + i], held[i]) for i in range(2)]
        before_ref[at, :] = jnp.where(upper, last, first)
        sent_ref[at, :] = jnp.where(upper, first, last).astype(BF16)
        total_ref[at, :] = held[MEMBERS].astype(BF16)
        again_ref[at, :] = held[MEMBERS].astype(BF16)
        totals.append(through[MEMBERS])
    total_ref[half * HEAD_DIM :, :] = decays_to_rows(totals)


def start_kernel(half, before_ref, through_ref, inside_ref, earlier_ref, _, *outs):
    mine_ref, rest_ref, factor_ref = outs
    started = lax.axis_index("seq") >= MEMBERS
    for j in range(half):
        at = state_rows(j)
        earlier = jnp.where(started, earlier_ref[at, :].astype(F32), 0.0)
        held = before_ref[at, :] + through_ref[8 * j : 8 * j + 1, :] * earlier
        mine_ref[at, :] = held.astype(BF16)
    rest_ref[...] = inside_ref[...]
    factor_ref[...] = through_ref[8 * half :, :]


def start_other_kernel(half, rest_ref, factor_ref, earlier_ref, _, out_ref):
    for j in range(half):
        at = state_rows(j)
        earlier = factor_ref[8 * j : 8 * j + 1, :] * earlier_ref[at, :].astype(F32)
        out_ref[at, :] = (rest_ref[at, :].astype(F32) + earlier).astype(BF16)


def norm_kernel(half, halves, rows, query_ref, intra_ref, own_ref, gain_ref, *refs):
    states, out_ref = refs[: len(halves)], refs[-1]
    for i, (mine, state_ref) in enumerate(zip(halves, states)):
        owner = side() if mine else 1 - side()
        own = pick(owner, own_ref[rows, :], 1)
        for j in range(half):
            at = half_at(owner * half + j, HEAD_DIM)
            state = state_ref[state_rows(j), :]
            inter = jnp.dot(query_ref[rows, at], state, preferred_element_type=F32)
            attended = intra_ref[rows, at] + own[:, j : j + 1] * inter
            mean_square = jnp.mean(attended * attended, axis=-1, keepdims=True)
            normed = (attended * lax.rsqrt(mean_square + 1e-06) * gain_ref[:, at]).astype(BF16)
            to = (i * half + j) * HEAD_DIM
            out_ref[:, to : to + HEAD_DIM] = normed


def share(halves, pair, weights):
    rows = weights[0].shape[0] // 2
    total = None
    for i, mine in enumerate(halves):
        at = half_at(side() if mine else 1 - side(), rows)
        for normed_ref, weight_ref in zip(pair, weights):
            normed = normed_ref[:, i * rows : (i + 1) * rows]
            part = jnp.dot(normed, weight_ref[at, :], preferred_element_type=F32)
            total = part if total is None else total + part
    return total


def fetch(step, whole, held, sems):
    copies = []
    for i, (weight, ref) in enumerate(zip(whole, held)):
        at = half_at(lax.axis_index("tp") ^ step, ref.shape[1])
        copies.append(pltpu.make_async_copy(weight.at[:, at], ref, sems.at[i]))
        copies[i].start()
    return copies


def fetch_kernel(weight_hbm, other_weight_hbm, _, weight_ref, other_weight_ref, sems):
    for copy in fetch(2, (weight_hbm, other_weight_hbm), (weight_ref, other_weight_ref), sems):
        copy.wait()


def far_mine_kernel(chunks, weight_ref, other_weight_ref, *refs):
    for i, rows in enumerate(chunks):
        pair = refs[2 * i : 2 * i + 2]
        refs[-1][rows, :] = share((True,), pair, (weight_ref, other_weight_ref))


def far_kernel(rows, begun_ref, mine_ref, other_ref, weight_ref, other_weight_ref, out_ref):
    rest = share((False,), (mine_ref, other_ref), (weight_ref, other_weight_ref))
    out_ref[...] = (begun_ref[rows, :] + rest).astype(BF16)


def far_all_kernel(mine_ref, other_ref, weight_ref, other_weight_ref, out_ref):
    pair, weights = (mine_ref, other_ref), (weight_ref, other_weight_ref)
    out_ref[...] = share((True, False), pair, weights).astype(BF16)


def near_kernel(chunks, passes, residual_hbm, weight_hbm, other_weight_hbm, *refs):
    out_ref, residual_ref, *weights, sems = refs[-5:]
    copies = fetch(0, (weight_hbm, other_weight_hbm), weights, sems)
    copies.append(pltpu.make_async_copy(residual_hbm, residual_ref, sems.at[2]))
    copies[2].start()
    for copy in copies:
        copy.wait()
    pairs = iter(zip(refs[0:-5:2], refs[1:-5:2]))
    for rows in chunks:
        near = residual_ref[rows, :].astype(F32)
        for halves in passes:
            near = near + share(halves, next(pairs), weights)
        out_ref[rows, :] = near


def nothing_kernel(out_hbm):
    pass


def add_kernel(chunks, near_ref, *refs):
    far, (out_hbm, out_ref, sems) = refs[: len(chunks)], refs[-3:]
    copies = []
    for i, rows in enumerate(chunks):
        out_ref[rows, :] = (near_ref[rows, :] + far[i][...].astype(F32)).astype(BF16)
        copies.append(
            pltpu.make_async_copy(out_ref.at[rows, :], out_hbm.at[rows, :], sems.at[i])
        )
        copies[-1].start()
    for copy in copies:
        copy.wait()


def call(kernel, out_shape, in_specs, name, out_specs=None, scratch=(), cost=0, aliases={}):
    single = isinstance(out_shape, jax.ShapeDtypeStruct)
    if out_specs is None:
        out_specs = VMEM if single else (VMEM,) * len(out_shape)
    cost = pl.CostEstimate(
        flops=cost, bytes_accessed=2_000_000 if cost else 0, transcendentals=0
    )
    return pl.pallas_call(
        kernel,
        out_shape=out_shape,
        in_specs=in_specs,
        out_specs=out_specs,
        scratch_shapes=scratch,
        input_output_aliases=aliases,
        compiler_params=PARAMS,
        cost_estimate=cost,
        name=name,
    )


def earlier_groups(total, again, half, devices):
    groups = devices // MEMBERS

    def swap(message, step):
        return lax.ppermute(message, "seq", [(i, i ^ step) for i in range(devices)])

    if groups == 2:
        return swap(total, MEMBERS), swap(again, MEMBERS + 1)

    def shift(message, by):
        moves = [(i, i + by * MEMBERS) for i in range(devices - by * MEMBERS)]
        return lax.ppermute(message, "seq", moves)

    rows = half * HEAD_DIM
    held = shift(total, 1)
    by = 1
    while by < groups - 1:
        before = shift(held, by)
        decays = rows_to_decays(held[rows:], half)
        factor = jnp.concatenate([jnp.broadcast_to(d, (HEAD_DIM, HEAD_DIM)) for d in decays])
        state = held[:rows].astype(F32) + factor * before[:rows].astype(F32)
        through = [a * b for a, b in zip(decays, rows_to_decays(before[rows:], half))]
        held = jnp.concatenate([state.astype(BF16), decays_to_rows(through)], axis=0)
        by *= 2
    return held, swap(held, 1)


def on_device(
    residual, query_vectors, key_vectors, value_vectors, log_decay, norm_gain, out_weight
):
    tokens, width = residual.shape
    heads = log_decay.shape[0]
    half = heads // 2
    devices = lax.axis_size("seq")
    tp = lax.axis_size("tp")
    wide = (tokens, heads * HEAD_DIM)
    out_width = out_weight.shape[1] // tp
    states = (half * HEAD_DIM, HEAD_DIM)
    near_pairs = [(i, i ^ 1) for i in range(tp)]
    far_pairs = [(i, i ^ 2) for i in range(tp)]
    shape = jax.ShapeDtypeStruct
    message = shape((half * HEAD_DIM + DECAY_ROWS, HEAD_DIM), BF16)

    def swap(piece, step):
        return lax.ppermute(piece, "seq", [(i, i ^ step) for i in range(devices)])

    other_weight = lax.ppermute(out_weight, "tp", near_pairs)
    arguments = (log_decay, key_vectors, value_vectors, query_vectors, norm_gain.reshape(1, -1))
    theirs, mine, decays, keys, values, queries, gain = call(
        functools.partial(state_kernel, half),
        (message, message) + tuple(shape(a.shape, a.dtype) for a in arguments),
        [HBM] * 5,
        "states",
        scratch=[pltpu.SemaphoreType.DMA((5,))],
    )(*(pltpu.with_memory_space_constraint(a, pltpu.HBM) for a in arguments))
    steps = (3, 1, 2, 0)
    received = [swap(theirs, 3), swap(theirs, 1), swap(mine, 2), mine]
    state = shape(states, BF16)
    before, sent, through, total, again = call(
        functools.partial(gather_kernel, half, steps),
        (shape(states, F32), state, shape((heads * 8, HEAD_DIM), F32), message, state),
        [VMEM] * len(steps),
        "gather_states",
        scratch=[pltpu.VMEM((MEMBERS,) + message.shape, BF16)],
    )(*received)
    earlier, other_earlier = earlier_groups(total, again, half, devices)
    inside = swap(sent, 1)
    intra, own = call(
        functools.partial(local_kernel, heads),
        (shape(wide, F32), shape((tokens, heads), F32)),
        [VMEM] * 4,
        "local",
        cost=4 * tokens * tokens * heads * HEAD_DIM,
    )(decays, queries, keys, values)
    block = (out_weight.shape[0], out_width)
    weights = (out_weight, other_weight)
    far_weights = call(
        fetch_kernel,
        (shape(block, BF16),) * 2,
        [ANY] * 2 + [VMEM],
        "fetch_far",
        scratch=[pltpu.SemaphoreType.DMA((2,))],
    )(*weights, own)
    mine, rest, factor = call(
        functools.partial(start_kernel, half),
        (state, state, shape((half * 8, HEAD_DIM), F32)),
        [VMEM] * 5,
        "start_states",
    )(before, through, inside, earlier, far_weights[0])
    chunks = [slice(0, tokens // 2), slice(tokens // 2, tokens)]

    def normed(name, halves, rows, *states):
        part = call(
            functools.partial(norm_kernel, half, halves, rows),
            shape((rows.stop - rows.start, len(halves) * half * HEAD_DIM), BF16),
            [VMEM] * (4 + len(states)),
            name,
        )(queries, intra, own, gain, *states)
        return part, lax.ppermute(part, "tp", near_pairs)

    def send_far(name, kernel, rows, *operands):
        part = call(
            kernel,
            shape((rows.stop - rows.start, out_width), BF16),
            [VMEM] * (len(operands) + 2),
            name,
        )(*operands, *far_weights)
        return lax.ppermute(part, "tp", far_pairs)

    def add(passes, pairs, far, out=()):
        near = call(
            functools.partial(near_kernel, chunks, passes),
            shape((tokens, out_width), F32),
            [ANY] * 3 + [VMEM] * (2 * len(pairs)),
            "project_near",
            scratch=[
                pltpu.VMEM(residual.shape, BF16),
                pltpu.VMEM(block, BF16),
                pltpu.VMEM(block, BF16),
                pltpu.SemaphoreType.DMA((3,)),
            ],
        )(residual, *weights, *(a for pair in pairs for a in pair))
        return call(
            functools.partial(add_kernel, chunks),
            pltpu.HBM((tokens, out_width), BF16),
            [VMEM] * (1 + len(chunks)) + [HBM] * len(out),
            "add",
            out_specs=HBM,
            scratch=[
                pltpu.VMEM((tokens, out_width), BF16),
                pltpu.SemaphoreType.DMA((len(chunks),)),
            ],
            aliases={1 + len(chunks): 0} if out else {},
        )(near, *far, *out)

    def first_group():
        both = (True, False)
        pairs = [normed(f"norm_{i}", both, rows, mine, rest) for i, rows in enumerate(chunks)]
        far = [
            send_far(f"project_far_{i}", far_all_kernel, rows, *pairs[i])
            for i, rows in enumerate(chunks)
        ]
        return add((both,), pairs, far)

    def not_yet():
        return call(
            nothing_kernel, pltpu.HBM((tokens, out_width), BF16), [], "nothing", out_specs=HBM
        )()

    def later_group(out):
        begun = [normed(f"norm_mine_{i}", (True,), rows, mine) for i, rows in enumerate(chunks)]
        far_begun = call(
            functools.partial(far_mine_kernel, chunks),
            shape((tokens, out_width), F32),
            [VMEM] * (2 + 2 * len(chunks)),
            "project_far_mine",
        )(*far_weights, *(a for pair in begun for a in pair))
        other = call(functools.partial(start_other_kernel, half), state, [VMEM] * 4, "start_other")(
            rest, factor, other_earlier, far_begun
        )
        parts = [normed(f"norm_{i}", (False,), rows, other) for i, rows in enumerate(chunks)]
        far = [
            send_far(
                f"project_far_{i}", functools.partial(far_kernel, rows), rows, far_begun, *parts[i]
            )
            for i, rows in enumerate(chunks)
        ]
        pairs = [pair for i in range(len(chunks)) for pair in (begun[i], parts[i])]
        return add(((True,), (False,)), pairs, far, (out,))

    first = lax.axis_index("seq") < MEMBERS
    out = lax.cond(first, first_group, not_yet)
    return lax.cond(first, lambda out: out, later_group, out)


def solution(mesh):
    return jax.shard_map(
        on_device,
        mesh=mesh,
        in_specs=(
            P("seq", "tp"),
            P("seq", "tp"),
            P("seq", "tp"),
            P("seq", "tp"),
            P("tp", "seq"),
            P("tp"),
            P("tp", None),
        ),
        out_specs=P("seq", "tp"),
        check_vma=False,
    )
```

profile of v0, /device:TPU:24, one launch (start us, length us, event | category | flops | bytes accessed | tf_op | source)
XLA Modules:
  0.0 31.7 jit_solution(8386368902352813201)
XLA Ops:
  0.0 1.4 %states.1 = (bf16[272,128]{1,0:T(8,128)(2,1)S(1)}, bf16[272,128]{1,0:T(8,128)(2,1)S(1)}, f32[4,256]{1,0:T(4,128)S(1)}, bf16[256,512]{1,0:T(8,128)(2,1)S(1)}, bf1...) custom-call(f32[4,256]{1,0:T(4,128)} %refs_0_.1, bf16[256,512]{1,0:T(8,128)(2,1)} %refs_1_.1, ...), custom_call_target="tpu_custom_call" | custom-call | tf_op jit(solution)/shard_map/states/pallas_call | solution.py:348
  1.4 1.5 %collective-permute-start.10 = (bf16[272,128]{1,0:T(8,128)(2,1)S(1)}, bf16[272,128]{1,0:T(8,128)(2,1)S(1)}, u32[]{:S(2)}, u32[]{:S(2)}) collective-permute-start(bf16[272,128]{1,0:T(8,128)(2,1)S(1)} %get-tuple-element.113), channel_id=1, source_target_pairs={{0,12},{4,8},{8,4},{12,0},{16,28},{20,24},{24,20},{28,16},{1,13},{... | collective-permute-start | bytes 208904 | tf_op jit(solution)/shard_map/ppermute | solution.py:344
  2.9 0.5 %collective-permute-start.11 = (bf16[272,128]{1,0:T(8,128)(2,1)S(1)}, bf16[272,128]{1,0:T(8,128)(2,1)S(1)}, u32[]{:S(2)}, u32[]{:S(2)}) collective-permute-start(bf16[272,128]{1,0:T(8,128)(2,1)S(1)} %get-tuple-element.113), channel_id=1, source_target_pairs={{0,4},{4,0},{8,12},{12,8},{16,20},{20,16},{24,28},{28,24},{1,5},{5... | collective-permute-start | bytes 208904 | tf_op jit(solution)/shard_map/ppermute | solution.py:344
  3.4 1.6 %collective-permute-start.12 = (bf16[272,128]{1,0:T(8,128)(2,1)S(1)}, bf16[272,128]{1,0:T(8,128)(2,1)S(1)}, u32[]{:S(2)}, u32[]{:S(2)}) collective-permute-start(bf16[272,128]{1,0:T(8,128)(2,1)S(1)} %get-tuple-element.114.refs_3_), channel_id=1, source_target_pairs={{0,8},{4,12},{8,0},{12,4},{16,24},{20,28},{24,16},{28,20},{1,9},{5... | collective-permute-start | bytes 208904 | tf_op jit(solution)/shard_map/ppermute | solution.py:344
  4.9 2.1 %collective-permute-done.10.refs_0_ = bf16[272,128]{1,0:T(8,128)(2,1)S(1)} collective-permute-done((bf16[272,128]{1,0:T(8,128)(2,1)S(1)}, bf16[272,128]{1,0:T(8,128)(2,1)S(1)}, u32[]{:S(2)}, u32[]{:S(2)}) %collective-permute-start.10) | collective-permute-done | bytes 69664 | tf_op jit(solution)/shard_map/ppermute | solution.py:344
  7.0 1.4 %collective-permute-done.11.refs_1_ = bf16[272,128]{1,0:T(8,128)(2,1)S(1)} collective-permute-done((bf16[272,128]{1,0:T(8,128)(2,1)S(1)}, bf16[272,128]{1,0:T(8,128)(2,1)S(1)}, u32[]{:S(2)}, u32[]{:S(2)}) %collective-permute-start.11) | collective-permute-done | bytes 69664 | tf_op jit(solution)/shard_map/ppermute | solution.py:344
  8.7 0.4 %collective-permute-start.14 = (bf16[272,128]{1,0:T(8,128)(2,1)S(1)}, bf16[272,128]{1,0:T(8,128)(2,1)S(1)}, u32[]{:S(2)}, u32[]{:S(2)}) collective-permute-start(bf16[272,128]{1,0:T(8,128)(2,1)S(1)} %get-tuple-element.118), channel_id=1, source_target_pairs={{0,16},{4,20},{8,24},{12,28},{16,0},{20,4},{24,8},{28,12},{1,17},{... | collective-permute-start | bytes 208904 | tf_op jit(solution)/shard_map/ppermute | solution.py:304
  9.1 0.7 %collective-permute-start.13 = (bf16[256,128]{1,0:T(8,128)(2,1)S(1)}, bf16[256,128]{1,0:T(8,128)(2,1)S(1)}, u32[]{:S(2)}, u32[]{:S(2)}) collective-permute-start(bf16[256,128]{1,0:T(8,128)(2,1)S(1)} %get-tuple-element.117), channel_id=1, source_target_pairs={{0,4},{4,0},{8,12},{12,8},{16,20},{20,16},{24,28},{28,24},{1,5},{5... | collective-permute-start | bytes 196616 | tf_op jit(solution)/shard_map/ppermute | solution.py:344
  9.7 3.4 %collective-permute-start.16 = (bf16[256,128]{1,0:T(8,128)(2,1)S(1)}, bf16[256,128]{1,0:T(8,128)(2,1)S(1)}, u32[]{:S(2)}, u32[]{:S(2)}) collective-permute-start(bf16[256,128]{1,0:T(8,128)(2,1)S(1)} %get-tuple-element.124), channel_id=1, source_target_pairs={{0,20},{4,16},{8,28},{12,24},{16,4},{20,0},{24,12},{28,8},{1,21},{... | collective-permute-start | bytes 196616 | tf_op jit(solution)/shard_map/ppermute | solution.py:304
  13.1 0.7 %local.1 = (f32[256,512]{1,0:T(8,128)S(1)}, f32[256,4]{1,0:T(8,128)S(1)}) custom-call(f32[4,256]{1,0:T(4,128)S(1)} %get-tuple-element.107.decay_ref, bf16[256,512]{1,0:T(8,128)(2,1)S(1)} %get-tuple-element.106.query_ref, bf16[256,512]{1,0:T(8,128)(2,1)S(1)} %get-tuple-element.108.key_ref, bf16[256,512]{1,0:T(8,128)(2,1)S(1)} %get-tuple-element.109.value_ref), custom_call_target="tpu_custom_call" | custom-call | flops 134217728 | bytes 2000000 | tf_op jit(solution)/shard_map/local/pallas_call | solution.py:367
  13.9 1.3 %fetch_far.1 = (bf16[512,512]{1,0:T(8,128)(2,1)S(1)}, bf16[512,512]{1,0:T(8,128)(2,1)S(1)}) custom-call(bf16[512,2048]{1,0:T(8,128)(2,1)} %weight_hbm.1, bf16[512,2048]{1,0:T(8,128)(2,1)} %collective-permute-done.15.other_weight_hbm, f32[256,4]{1,0:T(8,128)S(1)} %get-tuple-element.111._), custom_call_target="tpu_custom_call" | custom-call | tf_op jit(solution)/shard_map/fetch_far/pallas_call | solution.py:376
  15.2 1.5 %collective-permute-done.14.earlier_ref = bf16[272,128]{1,0:T(8,128)(2,1)S(1)} collective-permute-done((bf16[272,128]{1,0:T(8,128)(2,1)S(1)}, bf16[272,128]{1,0:T(8,128)(2,1)S(1)}, u32[]{:S(2)}, u32[]{:S(2)}) %collective-permute-start.14) | collective-permute-done | bytes 69664 | tf_op jit(solution)/shard_map/ppermute | solution.py:304
  16.7 1.3 %collective-permute-done.16 = bf16[256,128]{1,0:T(8,128)(2,1)S(1)} collective-permute-done((bf16[256,128]{1,0:T(8,128)(2,1)S(1)}, bf16[256,128]{1,0:T(8,128)(2,1)S(1)}, u32[]{:S(2)}, u32[]{:S(2)}) %collective-permute-start.16) | collective-permute-done | bytes 65568 | tf_op jit(solution)/shard_map/ppermute | solution.py:304
  18.1 13.7 %conditional.3 = (bf16[256,512]{1,0:T(8,128)(2,1)}) conditional(s32[]{:T(128)} %convert_element_type.4, (bf16[256,512]{1,0:T(8,128)(2,1)S(1)}, f32[256,512]{1,0:T(8,128)S(1)}, f32[256,4]{1,0:T(8,128)S(1)}, f32[1,512]{1,0:T(1,128)S(1)}, bf16[256,128]{1,0:T(8,128)(2,1)S(1)}, /*index=5*/bf16[512,512]{1,0:T(8,128)(2,1)S(1)}, ...), branch_computations={%region_2.0_spmd, %region_3.0_spmd} | conditional | bytes 10486036 | solution.py:472
  18.7 0.6 %collective-permute-start.5 = (bf16[128,256]{1,0:T(8,128)(2,1)S(1)}, bf16[128,256]{1,0:T(8,128)(2,1)S(1)}, u32[]{:S(2)}, u32[]{:S(2)}) collective-permute-start(bf16[128,256]{1,0:T(8,128)(2,1)S(1)} %norm_mine_1.1.refs_2_.refs_4_), channel_id=1, source_target_pairs={{0,1},{1,0},{2,3},{3,2},{4,5},{5,4},{6,7},{7,6},{8,9},{9,8},{10,11... | collective-permute-start | bytes 196616 | tf_op jit(solution)/shard_map/cond/branch_0_fun/ppermute | solution.py:398
  19.3 0.4 %collective-permute-done.4.refs_1_ = bf16[128,256]{1,0:T(8,128)(2,1)S(1)} collective-permute-done((bf16[128,256]{1,0:T(8,128)(2,1)S(1)}, bf16[128,256]{1,0:T(8,128)(2,1)S(1)}, u32[]{:S(2)}, u32[]{:S(2)}) %collective-permute-start.4) | collective-permute-done | bytes 65568 | tf_op jit(solution)/shard_map/cond/branch_0_fun/ppermute | solution.py:398
  19.7 0.5 %collective-permute-done.5.refs_3_.refs_5_ = bf16[128,256]{1,0:T(8,128)(2,1)S(1)} collective-permute-done((bf16[128,256]{1,0:T(8,128)(2,1)S(1)}, bf16[128,256]{1,0:T(8,128)(2,1)S(1)}, u32[]{:S(2)}, u32[]{:S(2)}) %collective-permute-start.5) | collective-permute-done | bytes 65568 | tf_op jit(solution)/shard_map/cond/branch_0_fun/ppermute | solution.py:398
  20.8 0.4 %collective-permute-start.7 = (bf16[128,256]{1,0:T(8,128)(2,1)S(1)}, bf16[128,256]{1,0:T(8,128)(2,1)S(1)}, u32[]{:S(2)}, u32[]{:S(2)}) collective-permute-start(bf16[128,256]{1,0:T(8,128)(2,1)S(1)} %norm_1.3.refs_6_.mine_ref), channel_id=1, source_target_pairs={{0,1},{1,0},{2,3},{3,2},{4,5},{5,4},{6,7},{7,6},{8,9},{9,8},{10,11... | collective-permute-start | bytes 196616 | tf_op jit(solution)/shard_map/cond/branch_0_fun/ppermute | solution.py:398
  22.4 1.6 %collective-permute-start.9 = (bf16[128,512]{1,0:T(8,128)(2,1)S(1)}, bf16[128,512]{1,0:T(8,128)(2,1)S(1)}, u32[]{:S(2)}, u32[]{:S(2)}) collective-permute-start(bf16[128,512]{1,0:T(8,128)(2,1)S(1)} %project_far_1.3), channel_id=1, source_target_pairs={{0,2},{1,3},{2,0},{3,1},{4,6},{5,7},{6,4},{7,5},{8,10},{9,11},{10,... | collective-permute-start | bytes 393224 | tf_op jit(solution)/shard_map/cond/branch_0_fun/ppermute | solution.py:407
  24.2 0.6 %collective-permute-start.8 = (bf16[128,512]{1,0:T(8,128)(2,1)S(1)}, bf16[128,512]{1,0:T(8,128)(2,1)S(1)}, u32[]{:S(2)}, u32[]{:S(2)}) collective-permute-start(bf16[128,512]{1,0:T(8,128)(2,1)S(1)} %project_far_0.3), channel_id=1, source_target_pairs={{0,2},{1,3},{2,0},{3,1},{4,6},{5,7},{6,4},{7,5},{8,10},{9,11},{10,... | collective-permute-start | bytes 393224 | tf_op jit(solution)/shard_map/cond/branch_0_fun/ppermute | solution.py:407
  24.8 1.6 %project_near.3.near_ref = f32[256,512]{1,0:T(8,128)S(1)} custom-call(bf16[256,512]{1,0:T(8,128)(2,1)S(1)} %get-tuple-element.73.residual_hbm, bf16[512,2048]{1,0:T(8,128)(2,1)S(1)} %copy-done.1, bf16[512,2048]{1,0:T(8,128)(2,1)} %get-tuple-element.75.other_weight_hbm, bf16[128,256]{1,0:T(8,128)(2,1)S(1)} %norm_mine_0.1.refs_0_, ...), custom_call_target="tpu_custom_call" | custom-call | tf_op jit(solution)/shard_map/cond/branch_0_fun/project_near/pallas_call | solution.py:410
  26.4 2.4 %collective-permute-done.9.refs_1_ = bf16[128,512]{1,0:T(8,128)(2,1)S(1)} collective-permute-done((bf16[128,512]{1,0:T(8,128)(2,1)S(1)}, bf16[128,512]{1,0:T(8,128)(2,1)S(1)}, u32[]{:S(2)}, u32[]{:S(2)}) %collective-permute-start.9) | collective-permute-done | bytes 131104 | tf_op jit(solution)/shard_map/cond/branch_0_fun/ppermute | solution.py:407
  28.7 2.2 %collective-permute-done.8.refs_0_ = bf16[128,512]{1,0:T(8,128)(2,1)S(1)} collective-permute-done((bf16[128,512]{1,0:T(8,128)(2,1)S(1)}, bf16[128,512]{1,0:T(8,128)(2,1)S(1)}, u32[]{:S(2)}, u32[]{:S(2)}) %collective-permute-start.8) | collective-permute-done | bytes 131104 | tf_op jit(solution)/shard_map/cond/branch_0_fun/ppermute | solution.py:407
  31.0 0.7 %add.3 = bf16[256,512]{1,0:T(8,128)(2,1)} custom-call(f32[256,512]{1,0:T(8,128)S(1)} %project_near.3.near_ref, bf16[128,512]{1,0:T(8,128)(2,1)S(1)} %collective-permute-done.8.refs_0_, bf16[128,512]{1,0:T(8,128)(2,1)S(1)} %collective-permute-done.9.refs_1_, bf16[256,512]{1,0:T(8,128)(2,1)} %get-tuple-element.86.refs_2_), custom_call_target="tpu_custom_call", output_to_operand_aliasing={{}: (3, {})} | custom-call | tf_op jit(solution)/shard_map/cond/branch_0_fun/add/pallas_call | solution.py:422
  (24 shorter events, 2.9 us)
Async XLA Ops:
  0.0 13.9 %collective-permute-start.15 = (bf16[512,2048]{1,0:T(8,128)(2,1)}, bf16[512,2048]{1,0:T(8,128)(2,1)}, u32[]{:S(2)}, u32[]{:S(2)}) collective-permute-start(bf16[512,2048]{1,0:T(8,128)(2,1)} %weight_hbm.1), channel_id=1, source_target_pairs={{0,1},{1,0},{2,3},{3,2},{4,5},{5,4},{6,7},{7,6},{8,9},{9,8},{10,11... | collective-permute-start | bytes 6291464 | tf_op jit(solution)/shard_map/ppermute | solution.py:346
  1.4 5.7 %collective-permute-start.10 = (bf16[272,128]{1,0:T(8,128)(2,1)S(1)}, bf16[272,128]{1,0:T(8,128)(2,1)S(1)}, u32[]{:S(2)}, u32[]{:S(2)}) collective-permute-start(bf16[272,128]{1,0:T(8,128)(2,1)S(1)} %get-tuple-element.113), channel_id=1, source_target_pairs={{0,12},{4,8},{8,4},{12,0},{16,28},{20,24},{24,20},{28,16},{1,13},{... | collective-permute-start | bytes 208904 | tf_op jit(solution)/shard_map/ppermute | solution.py:344
  2.9 5.6 %collective-permute-start.11 = (bf16[272,128]{1,0:T(8,128)(2,1)S(1)}, bf16[272,128]{1,0:T(8,128)(2,1)S(1)}, u32[]{:S(2)}, u32[]{:S(2)}) collective-permute-start(bf16[272,128]{1,0:T(8,128)(2,1)S(1)} %get-tuple-element.113), channel_id=1, source_target_pairs={{0,4},{4,0},{8,12},{12,8},{16,20},{20,16},{24,28},{28,24},{1,5},{5... | collective-permute-start | bytes 208904 | tf_op jit(solution)/shard_map/ppermute | solution.py:344
  3.4 5.2 %collective-permute-start.12 = (bf16[272,128]{1,0:T(8,128)(2,1)S(1)}, bf16[272,128]{1,0:T(8,128)(2,1)S(1)}, u32[]{:S(2)}, u32[]{:S(2)}) collective-permute-start(bf16[272,128]{1,0:T(8,128)(2,1)S(1)} %get-tuple-element.114.refs_3_), channel_id=1, source_target_pairs={{0,8},{4,12},{8,0},{12,4},{16,24},{20,28},{24,16},{28,20},{1,9},{5... | collective-permute-start | bytes 208904 | tf_op jit(solution)/shard_map/ppermute | solution.py:344
  8.7 8.0 %collective-permute-start.14 = (bf16[272,128]{1,0:T(8,128)(2,1)S(1)}, bf16[272,128]{1,0:T(8,128)(2,1)S(1)}, u32[]{:S(2)}, u32[]{:S(2)}) collective-permute-start(bf16[272,128]{1,0:T(8,128)(2,1)S(1)} %get-tuple-element.118), channel_id=1, source_target_pairs={{0,16},{4,20},{8,24},{12,28},{16,0},{20,4},{24,8},{28,12},{1,17},{... | collective-permute-start | bytes 208904 | tf_op jit(solution)/shard_map/ppermute | solution.py:304
  9.1 6.1 %collective-permute-start.13 = (bf16[256,128]{1,0:T(8,128)(2,1)S(1)}, bf16[256,128]{1,0:T(8,128)(2,1)S(1)}, u32[]{:S(2)}, u32[]{:S(2)}) collective-permute-start(bf16[256,128]{1,0:T(8,128)(2,1)S(1)} %get-tuple-element.117), channel_id=1, source_target_pairs={{0,4},{4,0},{8,12},{12,8},{16,20},{20,16},{24,28},{28,24},{1,5},{5... | collective-permute-start | bytes 196616 | tf_op jit(solution)/shard_map/ppermute | solution.py:344
  9.7 8.3 %collective-permute-start.16 = (bf16[256,128]{1,0:T(8,128)(2,1)S(1)}, bf16[256,128]{1,0:T(8,128)(2,1)S(1)}, u32[]{:S(2)}, u32[]{:S(2)}) collective-permute-start(bf16[256,128]{1,0:T(8,128)(2,1)S(1)} %get-tuple-element.124), channel_id=1, source_target_pairs={{0,20},{4,16},{8,28},{12,24},{16,4},{20,0},{24,12},{28,8},{1,21},{... | collective-permute-start | bytes 196616 | tf_op jit(solution)/shard_map/ppermute | solution.py:304
  13.9 2.8 %copy-start.2 = (bf16[256,512]{1,0:T(8,128)(2,1)S(1)}, bf16[256,512]{1,0:T(8,128)(2,1)}, u32[]{:S(2)}) copy-start(bf16[256,512]{1,0:T(8,128)(2,1)} %param.11) | copy-start | bytes 786436
  18.3 1.3 %collective-permute-start.4 = (bf16[128,256]{1,0:T(8,128)(2,1)S(1)}, bf16[128,256]{1,0:T(8,128)(2,1)S(1)}, u32[]{:S(2)}, u32[]{:S(2)}) collective-permute-start(bf16[128,256]{1,0:T(8,128)(2,1)S(1)} %norm_mine_0.1.refs_0_), channel_id=1, source_target_pairs={{0,1},{1,0},{2,3},{3,2},{4,5},{5,4},{6,7},{7,6},{8,9},{9,8},{10,11... | collective-permute-start | bytes 196616 | tf_op jit(solution)/shard_map/cond/branch_0_fun/ppermute | solution.py:398
  18.7 1.5 %collective-permute-start.5 = (bf16[128,256]{1,0:T(8,128)(2,1)S(1)}, bf16[128,256]{1,0:T(8,128)(2,1)S(1)}, u32[]{:S(2)}, u32[]{:S(2)}) collective-permute-start(bf16[128,256]{1,0:T(8,128)(2,1)S(1)} %norm_mine_1.1.refs_2_.refs_4_), channel_id=1, source_target_pairs={{0,1},{1,0},{2,3},{3,2},{4,5},{5,4},{6,7},{7,6},{8,9},{9,8},{10,11... | collective-permute-start | bytes 196616 | tf_op jit(solution)/shard_map/cond/branch_0_fun/ppermute | solution.py:398
  20.8 1.3 %collective-permute-start.7 = (bf16[128,256]{1,0:T(8,128)(2,1)S(1)}, bf16[128,256]{1,0:T(8,128)(2,1)S(1)}, u32[]{:S(2)}, u32[]{:S(2)}) collective-permute-start(bf16[128,256]{1,0:T(8,128)(2,1)S(1)} %norm_1.3.refs_6_.mine_ref), channel_id=1, source_target_pairs={{0,1},{1,0},{2,3},{3,2},{4,5},{5,4},{6,7},{7,6},{8,9},{9,8},{10,11... | collective-permute-start | bytes 196616 | tf_op jit(solution)/shard_map/cond/branch_0_fun/ppermute | solution.py:398
  21.5 3.3 %copy-start.1 = (bf16[512,2048]{1,0:T(8,128)(2,1)S(1)}, bf16[512,2048]{1,0:T(8,128)(2,1)}, u32[]{:S(2)}) copy-start(bf16[512,2048]{1,0:T(8,128)(2,1)} %get-tuple-element.74.weight_hbm) | copy-start | bytes 6291460 | tf_op jit(solution)/shard_map/cond
  21.5 2.4 %collective-permute-start.6 = (bf16[128,256]{1,0:T(8,128)(2,1)S(1)}, bf16[128,256]{1,0:T(8,128)(2,1)S(1)}, u32[]{:S(2)}, u32[]{:S(2)}) collective-permute-start(bf16[128,256]{1,0:T(8,128)(2,1)S(1)} %norm_0.3.refs_2_.mine_ref), channel_id=1, source_target_pairs={{0,1},{1,0},{2,3},{3,2},{4,5},{5,4},{6,7},{7,6},{8,9},{9,8},{10,11... | collective-permute-start | bytes 196616 | tf_op jit(solution)/shard_map/cond/branch_0_fun/ppermute | solution.py:398
  22.4 6.4 %collective-permute-start.9 = (bf16[128,512]{1,0:T(8,128)(2,1)S(1)}, bf16[128,512]{1,0:T(8,128)(2,1)S(1)}, u32[]{:S(2)}, u32[]{:S(2)}) collective-permute-start(bf16[128,512]{1,0:T(8,128)(2,1)S(1)} %project_far_1.3), channel_id=1, source_target_pairs={{0,2},{1,3},{2,0},{3,1},{4,6},{5,7},{6,4},{7,5},{8,10},{9,11},{10,... | collective-permute-start | bytes 393224 | tf_op jit(solution)/shard_map/cond/branch_0_fun/ppermute | solution.py:407
  24.2 6.8 %collective-permute-start.8 = (bf16[128,512]{1,0:T(8,128)(2,1)S(1)}, bf16[128,512]{1,0:T(8,128)(2,1)S(1)}, u32[]{:S(2)}, u32[]{:S(2)}) collective-permute-start(bf16[128,512]{1,0:T(8,128)(2,1)S(1)} %project_far_0.3), channel_id=1, source_target_pairs={{0,2},{1,3},{2,0},{3,1},{4,6},{5,7},{6,4},{7,5},{8,10},{9,11},{10,... | collective-permute-start | bytes 393224 | tf_op jit(solution)/shard_map/cond/branch_0_fun/ppermute | solution.py:407
where the time goes:
time: 31.9 us; the launch traced here: 31.7 us
  waiting for transfers between devices  12.3 us (39%)
  starting transfers between devices  11.4 us (36%)
  Pallas kernels  7.76 us (24%)
    ppermute x2, waiting for transfers between devices, send_far(): return lax.ppermute(part, 'tp', far_pairs)  4.62 us
    ppermute x4, starting transfers between devices, swap(): return lax.ppermute(piece, 'seq', [(i, i ^ step) for i in range(devices)])  4.21 us
    ppermute x2, starting transfers between devices, swap(): return lax.ppermute(message, 'seq', [(i, i ^ step) for i in range(devices)])  3.8 us
    ppermute x4, waiting for transfers between devices, swap(): return lax.ppermute(piece, 'seq', [(i, i ^ step) for i in range(devices)])  3.6 us
    ppermute x2, waiting for transfers between devices, swap(): return lax.ppermute(message, 'seq', [(i, i ^ step) for i in range(devices)])  2.82 us
    ppermute x2, starting transfers between devices, send_far(): return lax.ppermute(part, 'tp', far_pairs)  2.16 us
    pallas_call x1, Pallas kernels, add(): call(functools.partial(near_kernel, chunks, passes), shape((tokens, out_w...  1.59 us
    pallas_call x1, Pallas kernels, on_device(): call(functools.partial(state_kernel, half), (message, message) + tuple((s...  1.37 us
  transfers between devices with their start and end apart: 13, of which 10 were waited for; matrix products, arithmetic and copies ran while one was open for 0% of the time, Pallas kernels for 19%

commit v1 on v0

--- a/solution.py
+++ b/solution.py
@@ -180,17 +180,17 @@
     factor_ref[...] = through_ref[8 * half :, :]
 
 
-def start_other_kernel(half, rest_ref, factor_ref, earlier_ref, _, out_ref):
+def start_other_kernel(half, rest_ref, factor_ref, earlier_ref, out_ref):
     for j in range(half):
         at = state_rows(j)
         earlier = factor_ref[8 * j : 8 * j + 1, :] * earlier_ref[at, :].astype(F32)
         out_ref[at, :] = (rest_ref[at, :].astype(F32) + earlier).astype(BF16)
 
 
-def norm_kernel(half, halves, rows, query_ref, intra_ref, own_ref, gain_ref, *refs):
-    states, out_ref = refs[: len(halves)], refs[-1]
-    for i, (mine, state_ref) in enumerate(zip(halves, states)):
-        owner = side() if mine else 1 - side()
+def norm_kernel(
+    half, rows, query_ref, intra_ref, own_ref, gain_ref, mine_ref, other_ref, out_ref
+):
+    for i, (owner, state_ref) in enumerate(zip((side(), 1 - side()), (mine_ref, other_ref))):
         own = pick(owner, own_ref[rows, :], 1)
         for j in range(half):
             at = half_at(owner * half + j, HEAD_DIM)
@@ -203,11 +203,11 @@
             out_ref[:, to : to + HEAD_DIM] = normed
 
 
-def share(halves, pair, weights):
+def share(pair, weights):
     rows = weights[0].shape[0] // 2
     total = None
-    for i, mine in enumerate(halves):
-        at = half_at(side() if mine else 1 - side(), rows)
+    for i, owner in enumerate((side(), 1 - side())):
+        at = half_at(owner, rows)
         for normed_ref, weight_ref in zip(pair, weights):
             normed = normed_ref[:, i * rows : (i + 1) * rows]
             part = jnp.dot(normed, weight_ref[at, :], preferred_element_type=F32)
@@ -229,35 +229,20 @@
         copy.wait()
 
 
-def far_mine_kernel(chunks, weight_ref, other_weight_ref, *refs):
-    for i, rows in enumerate(chunks):
-        pair = refs[2 * i : 2 * i + 2]
-        refs[-1][rows, :] = share((True,), pair, (weight_ref, other_weight_ref))
-
-
-def far_kernel(rows, begun_ref, mine_ref, other_ref, weight_ref, other_weight_ref, out_ref):
-    rest = share((False,), (mine_ref, other_ref), (weight_ref, other_weight_ref))
-    out_ref[...] = (begun_ref[rows, :] + rest).astype(BF16)
-
-
-def far_all_kernel(mine_ref, other_ref, weight_ref, other_weight_ref, out_ref):
-    pair, weights = (mine_ref, other_ref), (weight_ref, other_weight_ref)
-    out_ref[...] = share((True, False), pair, weights).astype(BF16)
-
-
-def near_kernel(chunks, passes, residual_hbm, weight_hbm, other_weight_hbm, *refs):
+def far_kernel(mine_ref, other_ref, weight_ref, other_weight_ref, out_ref):
+    out_ref[...] = share((mine_ref, other_ref), (weight_ref, other_weight_ref)).astype(BF16)
+
+
+def near_kernel(chunks, residual_hbm, weight_hbm, other_weight_hbm, *refs):
     out_ref, residual_ref, *weights, sems = refs[-5:]
     copies = fetch(0, (weight_hbm, other_weight_hbm), weights, sems)
     copies.append(pltpu.make_async_copy(residual_hbm, residual_ref, sems.at[2]))
     copies[2].start()
     for copy in copies:
         copy.wait()
-    pairs = iter(zip(refs[0:-5:2], refs[1:-5:2]))
-    for rows in chunks:
-        near = residual_ref[rows, :].astype(F32)
-        for halves in passes:
-            near = near + share(halves, next(pairs), weights)
-        out_ref[rows, :] = near
+    for i, rows in enumerate(chunks):
+        near = share(refs[2 * i : 2 * i + 2], weights)
+        out_ref[rows, :] = residual_ref[rows, :].astype(F32) + near
 
 
 def nothing_kernel(out_hbm):
@@ -388,29 +373,28 @@
     )(before, through, inside, earlier, far_weights[0])
     chunks = [slice(0, tokens // 2), slice(tokens // 2, tokens)]
 
-    def normed(name, halves, rows, *states):
-        part = call(
-            functools.partial(norm_kernel, half, halves, rows),
-            shape((rows.stop - rows.start, len(halves) * half * HEAD_DIM), BF16),
-            [VMEM] * (4 + len(states)),
-            name,
-        )(queries, intra, own, gain, *states)
-        return part, lax.ppermute(part, "tp", near_pairs)
-
-    def send_far(name, kernel, rows, *operands):
-        part = call(
-            kernel,
-            shape((rows.stop - rows.start, out_width), BF16),
-            [VMEM] * (len(operands) + 2),
-            name,
-        )(*operands, *far_weights)
-        return lax.ppermute(part, "tp", far_pairs)
-
-    def add(passes, pairs, far, out=()):
+    def finish(mine, other, out=()):
+        pairs, far = [], []
+        for i, rows in enumerate(chunks):
+            part = call(
+                functools.partial(norm_kernel, half, rows),
+                shape((rows.stop - rows.start, heads * HEAD_DIM), BF16),
+                [VMEM] * 6,
+                f"norm_{i}",
+            )(queries, intra, own, gain, mine, other)
+            pairs.append((part, lax.ppermute(part, "tp", near_pairs)))
+        for i, rows in enumerate(chunks):
+            part = call(
+                far_kernel,
+                shape((rows.stop - rows.start, out_width), BF16),
+                [VMEM] * 4,
+                f"project_far_{i}",
+            )(*pairs[i], *far_weights)
+            far.append(lax.ppermute(part, "tp", far_pairs))
         near = call(
-            functools.partial(near_kernel, chunks, passes),
+            functools.partial(near_kernel, chunks),
             shape((tokens, out_width), F32),
-            [ANY] * 3 + [VMEM] * (2 * len(pairs)),
+            [ANY] * 3 + [VMEM] * (2 * len(chunks)),
             "project_near",
             scratch=[
                 pltpu.VMEM(residual.shape, BF16),
@@ -432,43 +416,19 @@
             aliases={1 + len(chunks): 0} if out else {},
         )(near, *far, *out)
 
-    def first_group():
-        both = (True, False)
-        pairs = [normed(f"norm_{i}", both, rows, mine, rest) for i, rows in enumerate(chunks)]
-        far = [
-            send_far(f"project_far_{i}", far_all_kernel, rows, *pairs[i])
-            for i, rows in enumerate(chunks)
-        ]
-        return add((both,), pairs, far)
-
     def not_yet():
         return call(
             nothing_kernel, pltpu.HBM((tokens, out_width), BF16), [], "nothing", out_specs=HBM
         )()
 
     def later_group(out):
-        begun = [normed(f"norm_mine_{i}", (True,), rows, mine) for i, rows in enumerate(chunks)]
-        far_begun = call(
-            functools.partial(far_mine_kernel, chunks),
-            shape((tokens, out_width), F32),
-            [VMEM] * (2 + 2 * len(chunks)),
-            "project_far_mine",
-        )(*far_weights, *(a for pair in begun for a in pair))
-        other = call(functools.partial(start_other_kernel, half), state, [VMEM] * 4, "start_other")(
-            rest, factor, other_earlier, far_begun
+        other = call(functools.partial(start_other_kernel, half), state, [VMEM] * 3, "start_other")(
+            rest, factor, other_earlier
         )
-        parts = [normed(f"norm_{i}", (False,), rows, other) for i, rows in enumerate(chunks)]
-        far = [
-            send_far(
-                f"project_far_{i}", functools.partial(far_kernel, rows), rows, far_begun, *parts[i]
-            )
-            for i, rows in enumerate(chunks)
-        ]
-        pairs = [pair for i in range(len(chunks)) for pair in (begun[i], parts[i])]
-        return add(((True,), (False,)), pairs, far, (out,))
+        return finish(mine, other, (out,))
 
     first = lax.axis_index("seq") < MEMBERS
-    out = lax.cond(first, first_group, not_yet)
+    out = lax.cond(first, lambda: finish(mine, rest), not_yet)
     return lax.cond(first, lambda out: out, later_group, out)
 
 

time: 31.9 us -> 32.6 us (1.022)
  Pallas kernels: 7.76 us -> 12.8 us
  waiting for transfers between devices: 12.3 us -> 8.49 us
  starting transfers between devices: 11.4 us -> 10.9 us
    pallas_call x10 -> x7, Pallas kernels: 4.23 us -> 6.92 us  [the longest x2 3.03 us: finish(): call(functools.partial(norm_kernel, half, rows), shape((rows.stop - rows....]
    ppermute x2, waiting for transfers between devices: 2.82 us -> 0.36 us  [swap(): return lax.ppermute(message, 'seq', [(i, i ^ step) for i in range(devices)])]
    ppermute x6 -> x4, waiting for transfers between devices: 5.91 us -> 4.17 us  [the longest x2 4.17 us: finish(): far.append(lax.ppermute(part, 'tp', far_pairs))]
    pallas_call x1, Pallas kernels: 1.27 us -> 2.18 us  [on_device(): call(fetch_kernel, (shape(block, BF16),) * 2, [ANY] * 2 + [VMEM], 'fetch_...]
    pallas_call x1, Pallas kernels: 0.73 us -> 1.54 us  [on_device(): call(functools.partial(local_kernel, heads), (shape(wide, F32), shape((to...]
    ppermute x2, starting transfers between devices: 3.8 us -> 3.1 us  [swap(): return lax.ppermute(message, 'seq', [(i, i ^ step) for i in range(devices)])]
    ppermute x4, starting transfers between devices: 4.21 us -> 4.9 us  [swap(): return lax.ppermute(piece, 'seq', [(i, i ^ step) for i in range(devices)])]
    pallas_call x1, Pallas kernels: 0.03 us -> 0.63 us  [on_device(): call(functools.partial(start_kernel, half), (state, state, shape((half *...]
  transfers between devices with their start and end apart: 13 -> 11, of which waited for: 10 -> 5; matrix products, arithmetic and copies ran while one was open for 0% -> 0% of each run, Pallas kernels for 19% -> 30%
where the time goes in v1:
time: 32.6 us; the launch traced here: 32.3 us
  Pallas kernels  12.8 us (39%)
  starting transfers between devices  10.9 us (33%)
  waiting for transfers between devices  8.49 us (26%)
    ppermute x4, starting transfers between devices, swap(): return lax.ppermute(piece, 'seq', [(i, i ^ step) for i in range(devices)])  4.9 us
    ppermute x2, waiting for transfers between devices, finish(): far.append(lax.ppermute(part, 'tp', far_pairs))  4.17 us
    ppermute x4, waiting for transfers between devices, swap(): return lax.ppermute(piece, 'seq', [(i, i ^ step) for i in range(devices)])  3.95 us
    ppermute x2, starting transfers between devices, swap(): return lax.ppermute(message, 'seq', [(i, i ^ step) for i in range(devices)])  3.1 us
    pallas_call x2, Pallas kernels, finish(): call(functools.partial(norm_kernel, half, rows), shape((rows.stop - rows....  3.03 us
    ppermute x2, starting transfers between devices, finish(): far.append(lax.ppermute(part, 'tp', far_pairs))  2.24 us
    pallas_call x1, Pallas kernels, on_device(): call(fetch_kernel, (shape(block, BF16),) * 2, [ANY] * 2 + [VMEM], 'fetch_...  2.18 us
    pallas_call x1, Pallas kernels, finish(): call(functools.partial(near_kernel, chunks), shape((tokens, out_width), F...  1.59 us
  transfers between devices with their start and end apart: 11, of which 5 were waited for; matrix products, arithmetic and copies ran while one was open for 0% of the time, Pallas kernels for 30%

profile of v1, /device:TPU:24, one launch (start us, length us, event | category | flops | bytes accessed | tf_op | source)
XLA Modules:
  0.0 32.3 jit_solution(16670332071560280039)
XLA Ops:
  0.0 1.4 %states.1 = (bf16[272,128]{1,0:T(8,128)(2,1)S(1)}, bf16[272,128]{1,0:T(8,128)(2,1)S(1)}, f32[4,256]{1,0:T(4,128)S(1)}, bf16[256,512]{1,0:T(8,128)(2,1)S(1)}, bf1...) custom-call(f32[4,256]{1,0:T(4,128)} %refs_0_.1, bf16[256,512]{1,0:T(8,128)(2,1)} %refs_1_.1, ...), custom_call_target="tpu_custom_call" | custom-call | tf_op jit(solution)/shard_map/states/pallas_call | solution.py:333
  1.4 1.6 %collective-permute-start.9 = (bf16[272,128]{1,0:T(8,128)(2,1)S(1)}, bf16[272,128]{1,0:T(8,128)(2,1)S(1)}, u32[]{:S(2)}, u32[]{:S(2)}) collective-permute-start(bf16[272,128]{1,0:T(8,128)(2,1)S(1)} %get-tuple-element.106), channel_id=1, source_target_pairs={{0,4},{4,0},{8,12},{12,8},{16,20},{20,16},{24,28},{28,24},{1,5},{5... | collective-permute-start | bytes 208904 | tf_op jit(solution)/shard_map/ppermute | solution.py:329
  3.0 0.4 %collective-permute-start.8 = (bf16[272,128]{1,0:T(8,128)(2,1)S(1)}, bf16[272,128]{1,0:T(8,128)(2,1)S(1)}, u32[]{:S(2)}, u32[]{:S(2)}) collective-permute-start(bf16[272,128]{1,0:T(8,128)(2,1)S(1)} %get-tuple-element.106), channel_id=1, source_target_pairs={{0,12},{4,8},{8,4},{12,0},{16,28},{20,24},{24,20},{28,16},{1,13},{... | collective-permute-start | bytes 208904 | tf_op jit(solution)/shard_map/ppermute | solution.py:329
  3.4 1.6 %collective-permute-start.10 = (bf16[272,128]{1,0:T(8,128)(2,1)S(1)}, bf16[272,128]{1,0:T(8,128)(2,1)S(1)}, u32[]{:S(2)}, u32[]{:S(2)}) collective-permute-start(bf16[272,128]{1,0:T(8,128)(2,1)S(1)} %get-tuple-element.107.refs_3_), channel_id=1, source_target_pairs={{0,8},{4,12},{8,0},{12,4},{16,24},{20,28},{24,16},{28,20},{1,9},{5... | collective-permute-start | bytes 208904 | tf_op jit(solution)/shard_map/ppermute | solution.py:329
  4.9 1.1 %collective-permute-done.9.refs_1_ = bf16[272,128]{1,0:T(8,128)(2,1)S(1)} collective-permute-done((bf16[272,128]{1,0:T(8,128)(2,1)S(1)}, bf16[272,128]{1,0:T(8,128)(2,1)S(1)}, u32[]{:S(2)}, u32[]{:S(2)}) %collective-permute-start.9) | collective-permute-done | bytes 69664 | tf_op jit(solution)/shard_map/ppermute | solution.py:329
  6.1 2.8 %collective-permute-done.8.refs_0_ = bf16[272,128]{1,0:T(8,128)(2,1)S(1)} collective-permute-done((bf16[272,128]{1,0:T(8,128)(2,1)S(1)}, bf16[272,128]{1,0:T(8,128)(2,1)S(1)}, u32[]{:S(2)}, u32[]{:S(2)}) %collective-permute-start.8) | collective-permute-done | bytes 69664 | tf_op jit(solution)/shard_map/ppermute | solution.py:329
  9.0 0.4 %collective-permute-start.12 = (bf16[272,128]{1,0:T(8,128)(2,1)S(1)}, bf16[272,128]{1,0:T(8,128)(2,1)S(1)}, u32[]{:S(2)}, u32[]{:S(2)}) collective-permute-start(bf16[272,128]{1,0:T(8,128)(2,1)S(1)} %get-tuple-element.111), channel_id=1, source_target_pairs={{0,16},{4,20},{8,24},{12,28},{16,0},{20,4},{24,8},{28,12},{1,17},{... | collective-permute-start | bytes 208904 | tf_op jit(solution)/shard_map/ppermute | solution.py:289
  9.4 1.3 %collective-permute-start.11 = (bf16[256,128]{1,0:T(8,128)(2,1)S(1)}, bf16[256,128]{1,0:T(8,128)(2,1)S(1)}, u32[]{:S(2)}, u32[]{:S(2)}) collective-permute-start(bf16[256,128]{1,0:T(8,128)(2,1)S(1)} %get-tuple-element.110), channel_id=1, source_target_pairs={{0,4},{4,0},{8,12},{12,8},{16,20},{20,16},{24,28},{28,24},{1,5},{5... | collective-permute-start | bytes 196616 | tf_op jit(solution)/shard_map/ppermute | solution.py:329
  10.8 2.7 %collective-permute-start.14 = (bf16[256,128]{1,0:T(8,128)(2,1)S(1)}, bf16[256,128]{1,0:T(8,128)(2,1)}, u32[]{:S(2)}, u32[]{:S(2)}) collective-permute-start(bf16[256,128]{1,0:T(8,128)(2,1)S(1)} %get-tuple-element.120), channel_id=1, source_target_pairs={{0,20},{4,16},{8,28},{12,24},{16,4},{20,0},{24,12},{28,8},{1,21},{... | collective-permute-start | bytes 196616 | tf_op jit(solution)/shard_map/ppermute | solution.py:289
  13.5 1.5 %local.1 = (f32[256,512]{1,0:T(8,128)}, f32[256,4]{1,0:T(8,128)S(1)}) custom-call(f32[4,256]{1,0:T(4,128)S(1)} %get-tuple-element.112.decay_ref, bf16[256,512]{1,0:T(8,128)(2,1)S(1)} %get-tuple-element.113.query_ref, bf16[256,512]{1,0:T(8,128)(2,1)S(1)} %get-tuple-element.114.key_ref, bf16[256,512]{1,0:T(8,128)(2,1)S(1)} %get-tuple-element.115.value_ref), custom_call_target="tpu_custom_call" | custom-call | flops 134217728 | bytes 2000000 | tf_op jit(solution)/shard_map/local/pallas_call | solution.py:352
  15.0 2.2 %fetch_far.1 = (bf16[512,512]{1,0:T(8,128)(2,1)S(1)}, bf16[512,512]{1,0:T(8,128)(2,1)}) custom-call(bf16[512,2048]{1,0:T(8,128)(2,1)} %weight_hbm.1, bf16[512,2048]{1,0:T(8,128)(2,1)} %collective-permute-done.13.other_weight_hbm, f32[256,4]{1,0:T(8,128)S(1)} %get-tuple-element.116._), custom_call_target="tpu_custom_call" | custom-call | tf_op jit(solution)/shard_map/fetch_far/pallas_call | solution.py:361
  17.2 0.6 %start_states.1 = (bf16[256,128]{1,0:T(8,128)(2,1)S(1)}, bf16[256,128]{1,0:T(8,128)(2,1)}, f32[16,128]{1,0:T(8,128)S(1)}) custom-call(f32[256,128]{1,0:T(8,128)S(1)} %get-tuple-element.108.before_ref, f32[32,128]{1,0:T(8,128)S(1)} %get-tuple-element.109.through_ref, bf16[256,128]{1,0:T(8,128)(2,1)S(1)} %collective-permute-done.11.inside_ref, ...), custom_call_target="tpu_custom_call" | custom-call | tf_op jit(solution)/shard_map/start_states/pallas_call | solution.py:368
  17.9 0.4 %collective-permute-done.14 = bf16[256,128]{1,0:T(8,128)(2,1)} collective-permute-done((bf16[256,128]{1,0:T(8,128)(2,1)S(1)}, bf16[256,128]{1,0:T(8,128)(2,1)}, u32[]{:S(2)}, u32[]{:S(2)}) %collective-permute-start.14) | collective-permute-done | bytes 65568 | tf_op jit(solution)/shard_map/ppermute | solution.py:289
  18.2 14.0 %conditional.3 = (bf16[256,512]{1,0:T(8,128)(2,1)}) conditional(s32[]{:T(128)} %convert_element_type.4, (bf16[256,128]{1,0:T(8,128)(2,1)}, f32[16,128]{1,0:T(8,128)S(1)}, bf16[256,128]{1,0:T(8,128)(2,1)}, bf16[256,512]{1,0:T(8,128)(2,1)S(1)}, f32[256,512]{1,0:T(8,128)}, /*index=5*/f32[256,4]{1,0:T(8,128)S(1)}, f32[1,512]{1,0:T(1,128)S(1)}, ...), branch_computations={%region_2.0_spmd, %region_3.0_spmd} | conditional | bytes 5243104 | solution.py:432
  18.2 1.0 %start_other.1.other_ref = bf16[256,128]{1,0:T(8,128)(2,1)S(1)} custom-call(bf16[256,128]{1,0:T(8,128)(2,1)} %get-tuple-element.81.rest_ref, f32[16,128]{1,0:T(8,128)S(1)} %get-tuple-element.82.factor_ref, bf16[256,128]{1,0:T(8,128)(2,1)} %get-tuple-element.83.earlier_ref), custom_call_target="tpu_custom_call" | custom-call | tf_op jit(solution)/shard_map/cond/branch_0_fun/start_other/pallas_call | solution.py:425
  19.2 1.5 %norm_0.3.refs_0_.mine_ref = bf16[128,512]{1,0:T(8,128)(2,1)S(1)} custom-call(bf16[256,512]{1,0:T(8,128)(2,1)S(1)} %get-tuple-element.76.query_ref, f32[256,512]{1,0:T(8,128)} %get-tuple-element.77.intra_ref, f32[256,4]{1,0:T(8,128)S(1)} %get-tuple-element.78.own_ref, f32[1,512]{1,0:T(1,128)S(1)} %get-tuple-element.79.gain_ref, ...), custom_call_target="tpu_custom_call" | custom-call | tf_op jit(solution)/shard_map/cond/branch_0_fun/norm_0/pallas_call | solution.py:379
  20.8 1.5 %norm_1.3.refs_2_.mine_ref = bf16[128,512]{1,0:T(8,128)(2,1)S(1)} custom-call(bf16[256,512]{1,0:T(8,128)(2,1)S(1)} %get-tuple-element.76.query_ref, f32[256,512]{1,0:T(8,128)} %get-tuple-element.77.intra_ref, f32[256,4]{1,0:T(8,128)S(1)} %get-tuple-element.78.own_ref, f32[1,512]{1,0:T(1,128)S(1)} %get-tuple-element.79.gain_ref, ...), custom_call_target="tpu_custom_call" | custom-call | tf_op jit(solution)/shard_map/cond/branch_0_fun/norm_1/pallas_call | solution.py:379
  22.3 0.6 %collective-permute-start.5 = (bf16[128,512]{1,0:T(8,128)(2,1)S(1)}, bf16[128,512]{1,0:T(8,128)(2,1)S(1)}, u32[]{:S(2)}, u32[]{:S(2)}) collective-permute-start(bf16[128,512]{1,0:T(8,128)(2,1)S(1)} %norm_1.3.refs_2_.mine_ref), channel_id=1, source_target_pairs={{0,1},{1,0},{2,3},{3,2},{4,5},{5,4},{6,7},{7,6},{8,9},{9,8},{10,11... | collective-permute-start | bytes 393224 | tf_op jit(solution)/shard_map/cond/branch_0_fun/ppermute | solution.py:385
  23.2 1.6 %collective-permute-start.6 = (bf16[128,512]{1,0:T(8,128)(2,1)S(1)}, bf16[128,512]{1,0:T(8,128)(2,1)S(1)}, u32[]{:S(2)}, u32[]{:S(2)}) collective-permute-start(bf16[128,512]{1,0:T(8,128)(2,1)S(1)} %project_far_0.3), channel_id=1, source_target_pairs={{0,2},{1,3},{2,0},{3,1},{4,6},{5,7},{6,4},{7,5},{8,10},{9,11},{10,... | collective-permute-start | bytes 393224 | tf_op jit(solution)/shard_map/cond/branch_0_fun/ppermute | solution.py:393
  25.1 0.7 %collective-permute-start.7 = (bf16[128,512]{1,0:T(8,128)(2,1)S(1)}, bf16[128,512]{1,0:T(8,128)(2,1)S(1)}, u32[]{:S(2)}, u32[]{:S(2)}) collective-permute-start(bf16[128,512]{1,0:T(8,128)(2,1)S(1)} %project_far_1.3), channel_id=1, source_target_pairs={{0,2},{1,3},{2,0},{3,1},{4,6},{5,7},{6,4},{7,5},{8,10},{9,11},{10,... | collective-permute-start | bytes 393224 | tf_op jit(solution)/shard_map/cond/branch_0_fun/ppermute | solution.py:393
  25.7 1.6 %project_near.3.near_ref = f32[256,512]{1,0:T(8,128)S(1)} custom-call(bf16[256,512]{1,0:T(8,128)(2,1)S(1)} %copy-done.4, bf16[512,2048]{1,0:T(8,128)(2,1)S(1)} %get-tuple-element.74.weight_hbm, bf16[512,2048]{1,0:T(8,128)(2,1)} %get-tuple-element.75.other_weight_hbm, bf16[128,512]{1,0:T(8,128)(2,1)S(1)} %norm_0.3.refs_0_.mine_ref, ...), custom_call_target="tpu_custom_call" | custom-call | tf_op jit(solution)/shard_map/cond/branch_0_fun/project_near/pallas_call | solution.py:394
  27.3 2.3 %collective-permute-done.6.refs_0_ = bf16[128,512]{1,0:T(8,128)(2,1)S(1)} collective-permute-done((bf16[128,512]{1,0:T(8,128)(2,1)S(1)}, bf16[128,512]{1,0:T(8,128)(2,1)S(1)}, u32[]{:S(2)}, u32[]{:S(2)}) %collective-permute-start.6) | collective-permute-done | bytes 131104 | tf_op jit(solution)/shard_map/cond/branch_0_fun/ppermute | solution.py:393
  29.6 1.9 %collective-permute-done.7.refs_1_ = bf16[128,512]{1,0:T(8,128)(2,1)S(1)} collective-permute-done((bf16[128,512]{1,0:T(8,128)(2,1)S(1)}, bf16[128,512]{1,0:T(8,128)(2,1)S(1)}, u32[]{:S(2)}, u32[]{:S(2)}) %collective-permute-start.7) | collective-permute-done | bytes 131104 | tf_op jit(solution)/shard_map/cond/branch_0_fun/ppermute | solution.py:393
  31.5 0.7 %add.3 = bf16[256,512]{1,0:T(8,128)(2,1)} custom-call(f32[256,512]{1,0:T(8,128)S(1)} %project_near.3.near_ref, bf16[128,512]{1,0:T(8,128)(2,1)S(1)} %collective-permute-done.6.refs_0_, bf16[128,512]{1,0:T(8,128)(2,1)S(1)} %collective-permute-done.7.refs_1_, bf16[256,512]{1,0:T(8,128)(2,1)} %get-tuple-element.86.refs_2_), custom_call_target="tpu_custom_call", output_to_operand_aliasing={{}: (3, {})} | custom-call | tf_op jit(solution)/shard_map/cond/branch_0_fun/add/pallas_call | solution.py:406
  (19 shorter events, 0.8 us)
Async XLA Ops:
  0.0 15.0 %collective-permute-start.13 = (bf16[512,2048]{1,0:T(8,128)(2,1)}, bf16[512,2048]{1,0:T(8,128)(2,1)}, u32[]{:S(2)}, u32[]{:S(2)}) collective-permute-start(bf16[512,2048]{1,0:T(8,128)(2,1)} %weight_hbm.1), channel_id=1, source_target_pairs={{0,1},{1,0},{2,3},{3,2},{4,5},{5,4},{6,7},{7,6},{8,9},{9,8},{10,11... | collective-permute-start | bytes 6291464 | tf_op jit(solution)/shard_map/ppermute | solution.py:331
  1.4 4.7 %collective-permute-start.9 = (bf16[272,128]{1,0:T(8,128)(2,1)S(1)}, bf16[272,128]{1,0:T(8,128)(2,1)S(1)}, u32[]{:S(2)}, u32[]{:S(2)}) collective-permute-start(bf16[272,128]{1,0:T(8,128)(2,1)S(1)} %get-tuple-element.106), channel_id=1, source_target_pairs={{0,4},{4,0},{8,12},{12,8},{16,20},{20,16},{24,28},{28,24},{1,5},{5... | collective-permute-start | bytes 208904 | tf_op jit(solution)/shard_map/ppermute | solution.py:329
  3.0 5.9 %collective-permute-start.8 = (bf16[272,128]{1,0:T(8,128)(2,1)S(1)}, bf16[272,128]{1,0:T(8,128)(2,1)S(1)}, u32[]{:S(2)}, u32[]{:S(2)}) collective-permute-start(bf16[272,128]{1,0:T(8,128)(2,1)S(1)} %get-tuple-element.106), channel_id=1, source_target_pairs={{0,12},{4,8},{8,4},{12,0},{16,28},{20,24},{24,20},{28,16},{1,13},{... | collective-permute-start | bytes 208904 | tf_op jit(solution)/shard_map/ppermute | solution.py:329
  3.4 5.5 %collective-permute-start.10 = (bf16[272,128]{1,0:T(8,128)(2,1)S(1)}, bf16[272,128]{1,0:T(8,128)(2,1)S(1)}, u32[]{:S(2)}, u32[]{:S(2)}) collective-permute-start(bf16[272,128]{1,0:T(8,128)(2,1)S(1)} %get-tuple-element.107.refs_3_), channel_id=1, source_target_pairs={{0,8},{4,12},{8,0},{12,4},{16,24},{20,28},{24,16},{28,20},{1,9},{5... | collective-permute-start | bytes 208904 | tf_op jit(solution)/shard_map/ppermute | solution.py:329
  9.0 8.2 %collective-permute-start.12 = (bf16[272,128]{1,0:T(8,128)(2,1)S(1)}, bf16[272,128]{1,0:T(8,128)(2,1)S(1)}, u32[]{:S(2)}, u32[]{:S(2)}) collective-permute-start(bf16[272,128]{1,0:T(8,128)(2,1)S(1)} %get-tuple-element.111), channel_id=1, source_target_pairs={{0,16},{4,20},{8,24},{12,28},{16,0},{20,4},{24,8},{28,12},{1,17},{... | collective-permute-start | bytes 208904 | tf_op jit(solution)/shard_map/ppermute | solution.py:289
  9.4 7.8 %collective-permute-start.11 = (bf16[256,128]{1,0:T(8,128)(2,1)S(1)}, bf16[256,128]{1,0:T(8,128)(2,1)S(1)}, u32[]{:S(2)}, u32[]{:S(2)}) collective-permute-start(bf16[256,128]{1,0:T(8,128)(2,1)S(1)} %get-tuple-element.110), channel_id=1, source_target_pairs={{0,4},{4,0},{8,12},{12,8},{16,20},{20,16},{24,28},{28,24},{1,5},{5... | collective-permute-start | bytes 196616 | tf_op jit(solution)/shard_map/ppermute | solution.py:329
  10.8 7.5 %collective-permute-start.14 = (bf16[256,128]{1,0:T(8,128)(2,1)S(1)}, bf16[256,128]{1,0:T(8,128)(2,1)}, u32[]{:S(2)}, u32[]{:S(2)}) collective-permute-start(bf16[256,128]{1,0:T(8,128)(2,1)S(1)} %get-tuple-element.120), channel_id=1, source_target_pairs={{0,20},{4,16},{8,28},{12,24},{16,4},{20,0},{24,12},{28,8},{1,21},{... | collective-permute-start | bytes 196616 | tf_op jit(solution)/shard_map/ppermute | solution.py:289
  15.0 2.8 %copy-start = (bf16[512,2048]{1,0:T(8,128)(2,1)S(1)}, bf16[512,2048]{1,0:T(8,128)(2,1)}, u32[]{:S(2)}) copy-start(bf16[512,2048]{1,0:T(8,128)(2,1)} %weight_hbm.1) | copy-start | bytes 6291460
  18.2 4.7 %copy-start.2 = (bf16[512,512]{1,0:T(8,128)(2,1)S(1)}, bf16[512,512]{1,0:T(8,128)(2,1)}, u32[]{:S(2)}) copy-start(bf16[512,512]{1,0:T(8,128)(2,1)} %get-tuple-element.85.other_weight_ref) | copy-start | bytes 1572868 | tf_op jit(solution)/shard_map/cond
  20.7 5.0 %copy-start.4 = (bf16[256,512]{1,0:T(8,128)(2,1)S(1)}, bf16[256,512]{1,0:T(8,128)(2,1)}, u32[]{:S(2)}) copy-start(bf16[256,512]{1,0:T(8,128)(2,1)} %get-tuple-element.73.residual_hbm) | copy-start | bytes 786436 | tf_op jit(solution)/shard_map/cond
  20.7 2.2 %collective-permute-start.4 = (bf16[128,512]{1,0:T(8,128)(2,1)S(1)}, bf16[128,512]{1,0:T(8,128)(2,1)S(1)}, u32[]{:S(2)}, u32[]{:S(2)}) collective-permute-start(bf16[128,512]{1,0:T(8,128)(2,1)S(1)} %norm_0.3.refs_0_.mine_ref), channel_id=1, source_target_pairs={{0,1},{1,0},{2,3},{3,2},{4,5},{5,4},{6,7},{7,6},{8,9},{9,8},{10,11... | collective-permute-start | bytes 393224 | tf_op jit(solution)/shard_map/cond/branch_0_fun/ppermute | solution.py:385
  22.3 2.4 %collective-permute-start.5 = (bf16[128,512]{1,0:T(8,128)(2,1)S(1)}, bf16[128,512]{1,0:T(8,128)(2,1)S(1)}, u32[]{:S(2)}, u32[]{:S(2)}) collective-permute-start(bf16[128,512]{1,0:T(8,128)(2,1)S(1)} %norm_1.3.refs_2_.mine_ref), channel_id=1, source_target_pairs={{0,1},{1,0},{2,3},{3,2},{4,5},{5,4},{6,7},{7,6},{8,9},{9,8},{10,11... | collective-permute-start | bytes 393224 | tf_op jit(solution)/shard_map/cond/branch_0_fun/ppermute | solution.py:385
  23.2 6.4 %collective-permute-start.6 = (bf16[128,512]{1,0:T(8,128)(2,1)S(1)}, bf16[128,512]{1,0:T(8,128)(2,1)S(1)}, u32[]{:S(2)}, u32[]{:S(2)}) collective-permute-start(bf16[128,512]{1,0:T(8,128)(2,1)S(1)} %project_far_0.3), channel_id=1, source_target_pairs={{0,2},{1,3},{2,0},{3,1},{4,6},{5,7},{6,4},{7,5},{8,10},{9,11},{10,... | collective-permute-start | bytes 393224 | tf_op jit(solution)/shard_map/cond/branch_0_fun/ppermute | solution.py:393
  25.1 6.5 %collective-permute-start.7 = (bf16[128,512]{1,0:T(8,128)(2,1)S(1)}, bf16[128,512]{1,0:T(8,128)(2,1)S(1)}, u32[]{:S(2)}, u32[]{:S(2)}) collective-permute-start(bf16[128,512]{1,0:T(8,128)(2,1)S(1)} %project_far_1.3), channel_id=1, source_target_pairs={{0,2},{1,3},{2,0},{3,1},{4,6},{5,7},{6,4},{7,5},{8,10},{9,11},{10,... | collective-permute-start | bytes 393224 | tf_op jit(solution)/shard_map/cond/branch_0_fun/ppermute | solution.py:393

commit v2 on v1

--- a/solution.py
+++ b/solution.py
@@ -116,21 +116,23 @@
         copy.wait()
 
 
-def local_kernel(heads, decay_ref, query_ref, key_ref, value_ref, intra_ref, own_ref):
+def local_kernel(heads, decay_ref, query_ref, key_ref, value_ref, intra_ref, scaled_ref):
     row, col = positions()
     causal = col <= row
     upto = jnp.where(causal, 1.0, 0.0).astype(BF16)
     decays = decay_ref[...]
     down = sums_down(upto, decays)
     across = sums_across(upto, decays)
-    own_ref[...] = jnp.exp(down) * SCALE
+    own = jnp.exp(down) * SCALE
     for h in range(heads):
         at = slice(h * HEAD_DIM, (h + 1) * HEAD_DIM)
+        scaled_ref[:, at] = (query_ref[:, at].astype(F32) * own[:, h : h + 1]).astype(BF16)
         scores = contract(query_ref[:, at], key_ref[:, at])
         gaps = down[:, h : h + 1] - across[h : h + 1, :]
         weights = jnp.where(causal, jnp.exp(gaps), 0.0)
         probs = (scores * SCALE * weights).astype(BF16)
-        intra_ref[:, at] = jnp.dot(probs, value_ref[:, at], preferred_element_type=F32)
+        intra = jnp.dot(probs, value_ref[:, at], preferred_element_type=F32)
+        intra_ref[:, at] = intra.astype(BF16)
 
 
 def gather_kernel(half, steps, *refs):
@@ -187,16 +189,13 @@
         out_ref[at, :] = (rest_ref[at, :].astype(F32) + earlier).astype(BF16)
 
 
-def norm_kernel(
-    half, rows, query_ref, intra_ref, own_ref, gain_ref, mine_ref, other_ref, out_ref
-):
+def norm_kernel(half, rows, scaled_ref, intra_ref, gain_ref, mine_ref, other_ref, out_ref):
     for i, (owner, state_ref) in enumerate(zip((side(), 1 - side()), (mine_ref, other_ref))):
-        own = pick(owner, own_ref[rows, :], 1)
         for j in range(half):
             at = half_at(owner * half + j, HEAD_DIM)
             state = state_ref[state_rows(j), :]
-            inter = jnp.dot(query_ref[rows, at], state, preferred_element_type=F32)
-            attended = intra_ref[rows, at] + own[:, j : j + 1] * inter
+            inter = jnp.dot(scaled_ref[rows, at], state, preferred_element_type=F32)
+            attended = intra_ref[rows, at].astype(F32) + inter
             mean_square = jnp.mean(attended * attended, axis=-1, keepdims=True)
             normed = (attended * lax.rsqrt(mean_square + 1e-06) * gain_ref[:, at]).astype(BF16)
             to = (i * half + j) * HEAD_DIM
@@ -349,9 +348,9 @@
     )(*received)
     earlier, other_earlier = earlier_groups(total, again, half, devices)
     inside = swap(sent, 1)
-    intra, own = call(
+    intra, scaled = call(
         functools.partial(local_kernel, heads),
-        (shape(wide, F32), shape((tokens, heads), F32)),
+        (shape(wide, BF16),) * 2,
         [VMEM] * 4,
         "local",
         cost=4 * tokens * tokens * heads * HEAD_DIM,
@@ -364,7 +363,7 @@
         [ANY] * 2 + [VMEM],
         "fetch_far",
         scratch=[pltpu.SemaphoreType.DMA((2,))],
-    )(*weights, own)
+    )(*weights, scaled)
     mine, rest, factor = call(
         functools.partial(start_kernel, half),
         (state, state, shape((half * 8, HEAD_DIM), F32)),
@@ -379,9 +378,9 @@
             part = call(
                 functools.partial(norm_kernel, half, rows),
                 shape((rows.stop - rows.start, heads * HEAD_DIM), BF16),
-                [VMEM] * 6,
+                [VMEM] * 5,
                 f"norm_{i}",
-            )(queries, intra, own, gain, mine, other)
+            )(scaled, intra, gain, mine, other)
             pairs.append((part, lax.ppermute(part, "tp", near_pairs)))
         for i, rows in enumerate(chunks):
             part = call(

time: 32.6 us -> 32.5 us (level)
  the two profiles are of different devices: /device:TPU:24 before, /device:TPU:0 now
where the time goes in v2:
time: 32.5 us; the launch traced here: 32.3 us
  starting transfers between devices  11.9 us (37%)
  Pallas kernels  11.7 us (36%)
  waiting for transfers between devices  8.48 us (26%)
    ppermute x4, starting transfers between devices, swap(): return lax.ppermute(piece, 'seq', [(i, i ^ step) for i in range(devices)])  5.68 us
    ppermute x4, waiting for transfers between devices, swap(): return lax.ppermute(piece, 'seq', [(i, i ^ step) for i in range(devices)])  4.25 us
    ppermute x2, waiting for transfers between devices, finish(): far.append(lax.ppermute(part, 'tp', far_pairs))  4.22 us
    ppermute x2, starting transfers between devices, swap(): return lax.ppermute(message, 'seq', [(i, i ^ step) for i in range(devices)])  2.93 us
    pallas_call x2, Pallas kernels, finish(): call(functools.partial(norm_kernel, half, rows), shape((rows.stop - rows....  2.56 us
    pallas_call x1, Pallas kernels, on_device(): call(fetch_kernel, (shape(block, BF16),) * 2, [ANY] * 2 + [VMEM], 'fetch_...  2.18 us
    ppermute x2, starting transfers between devices, finish(): far.append(lax.ppermute(part, 'tp', far_pairs))  2.16 us
    pallas_call x2, Pallas kernels, finish(): call(far_kernel, shape((rows.stop - rows.start, out_width), BF16), [VMEM]...  1.65 us
  transfers between devices with their start and end apart: 11, of which 5 were waited for; matrix products, arithmetic and copies ran while one was open for 0% of the time, Pallas kernels for 36%

profile of v2, /device:TPU:0, one launch (start us, length us, event | category | flops | bytes accessed | tf_op | source)
XLA Modules:
  0.0 32.3 jit_solution(3818592640174499876)
XLA Ops:
  0.0 0.5 %collective-permute-start.13 = (bf16[512,2048]{1,0:T(8,128)(2,1)}, bf16[512,2048]{1,0:T(8,128)(2,1)}, u32[]{:S(2)}, u32[]{:S(2)}) collective-permute-start(bf16[512,2048]{1,0:T(8,128)(2,1)} %weight_hbm.1), channel_id=1, source_target_pairs={{0,1},{1,0},{2,3},{3,2},{4,5},{5,4},{6,7},{7,6},{8,9},{9,8},{10,11... | collective-permute-start | bytes 6291464 | tf_op jit(solution)/shard_map/ppermute | solution.py:330
  0.5 1.4 %states.1 = (bf16[272,128]{1,0:T(8,128)(2,1)S(1)}, bf16[272,128]{1,0:T(8,128)(2,1)S(1)}, f32[4,256]{1,0:T(4,128)S(1)}, bf16[256,512]{1,0:T(8,128)(2,1)S(1)}, bf1...) custom-call(f32[4,256]{1,0:T(4,128)} %refs_0_.1, bf16[256,512]{1,0:T(8,128)(2,1)} %refs_1_.1, ...), custom_call_target="tpu_custom_call" | custom-call | tf_op jit(solution)/shard_map/states/pallas_call | solution.py:332
  1.8 2.6 %collective-permute-start.9 = (bf16[272,128]{1,0:T(8,128)(2,1)S(1)}, bf16[272,128]{1,0:T(8,128)(2,1)S(1)}, u32[]{:S(2)}, u32[]{:S(2)}) collective-permute-start(bf16[272,128]{1,0:T(8,128)(2,1)S(1)} %get-tuple-element.100), channel_id=1, source_target_pairs={{0,4},{4,0},{8,12},{12,8},{16,20},{20,16},{24,28},{28,24},{1,5},{5... | collective-permute-start | bytes 208904 | tf_op jit(solution)/shard_map/ppermute | solution.py:328
  4.4 1.5 %collective-permute-start.8 = (bf16[272,128]{1,0:T(8,128)(2,1)S(1)}, bf16[272,128]{1,0:T(8,128)(2,1)S(1)}, u32[]{:S(2)}, u32[]{:S(2)}) collective-permute-start(bf16[272,128]{1,0:T(8,128)(2,1)S(1)} %get-tuple-element.100), channel_id=1, source_target_pairs={{0,12},{4,8},{8,4},{12,0},{16,28},{20,24},{24,20},{28,16},{1,13},{... | collective-permute-start | bytes 208904 | tf_op jit(solution)/shard_map/ppermute | solution.py:328
  6.0 2.1 %collective-permute-done.9.refs_1_ = bf16[272,128]{1,0:T(8,128)(2,1)S(1)} collective-permute-done((bf16[272,128]{1,0:T(8,128)(2,1)S(1)}, bf16[272,128]{1,0:T(8,128)(2,1)S(1)}, u32[]{:S(2)}, u32[]{:S(2)}) %collective-permute-start.9) | collective-permute-done | bytes 69664 | tf_op jit(solution)/shard_map/ppermute | solution.py:328
  8.1 1.8 %collective-permute-done.8.refs_0_ = bf16[272,128]{1,0:T(8,128)(2,1)S(1)} collective-permute-done((bf16[272,128]{1,0:T(8,128)(2,1)S(1)}, bf16[272,128]{1,0:T(8,128)(2,1)S(1)}, u32[]{:S(2)}, u32[]{:S(2)}) %collective-permute-start.8) | collective-permute-done | bytes 69664 | tf_op jit(solution)/shard_map/ppermute | solution.py:328
  9.9 0.4 %collective-permute-done.10.refs_2_ = bf16[272,128]{1,0:T(8,128)(2,1)S(1)} collective-permute-done((bf16[272,128]{1,0:T(8,128)(2,1)S(1)}, bf16[272,128]{1,0:T(8,128)(2,1)S(1)}, u32[]{:S(2)}, u32[]{:S(2)}) %collective-permute-start.10) | collective-permute-done | bytes 69664 | tf_op jit(solution)/shard_map/ppermute | solution.py:328
  10.4 2.7 %collective-permute-start.12 = (bf16[272,128]{1,0:T(8,128)(2,1)S(1)}, bf16[272,128]{1,0:T(8,128)(2,1)S(1)}, u32[]{:S(2)}, u32[]{:S(2)}) collective-permute-start(bf16[272,128]{1,0:T(8,128)(2,1)S(1)} %get-tuple-element.105), channel_id=1, source_target_pairs={{0,16},{4,20},{8,24},{12,28},{16,0},{20,4},{24,8},{28,12},{1,17},{... | collective-permute-start | bytes 208904 | tf_op jit(solution)/shard_map/ppermute | solution.py:288
  13.0 1.5 %collective-permute-start.11 = (bf16[256,128]{1,0:T(8,128)(2,1)S(1)}, bf16[256,128]{1,0:T(8,128)(2,1)S(1)}, u32[]{:S(2)}, u32[]{:S(2)}) collective-permute-start(bf16[256,128]{1,0:T(8,128)(2,1)S(1)} %get-tuple-element.104), channel_id=1, source_target_pairs={{0,4},{4,0},{8,12},{12,8},{16,20},{20,16},{24,28},{28,24},{1,5},{5... | collective-permute-start | bytes 196616 | tf_op jit(solution)/shard_map/ppermute | solution.py:328
  14.6 0.3 collective-permute-start.14
  14.8 1.5 %local.1 = (bf16[256,512]{1,0:T(8,128)(2,1)}, bf16[256,512]{1,0:T(8,128)(2,1)S(1)}) custom-call(f32[4,256]{1,0:T(4,128)S(1)} %get-tuple-element.106.decay_ref, bf16[256,512]{1,0:T(8,128)(2,1)S(1)} %get-tuple-element.107.query_ref, bf16[256,512]{1,0:T(8,128)(2,1)S(1)} %get-tuple-element.108.key_ref, bf16[256,512]{1,0:T(8,128)(2,1)S(1)} %get-tuple-element.109.value_ref), custom_call_target="tpu_custom_call" | custom-call | flops 134217728 | bytes 2000000 | tf_op jit(solution)/shard_map/local/pallas_call | solution.py:351
  16.3 2.2 %fetch_far.1 = (bf16[512,512]{1,0:T(8,128)(2,1)S(1)}, bf16[512,512]{1,0:T(8,128)(2,1)}) custom-call(bf16[512,2048]{1,0:T(8,128)(2,1)} %weight_hbm.1, bf16[512,2048]{1,0:T(8,128)(2,1)} %collective-permute-done.13.other_weight_hbm, bf16[256,512]{1,0:T(8,128)(2,1)S(1)} %get-tuple-element.110._), custom_call_target="tpu_custom_call" | custom-call | tf_op jit(solution)/shard_map/fetch_far/pallas_call | solution.py:360
  18.6 13.6 %conditional.2 = (bf16[256,512]{1,0:T(8,128)(2,1)}) conditional(s32[]{:T(128)} %convert_element_type.4, () %tuple.17, (bf16[256,512]{1,0:T(8,128)(2,1)S(1)}, bf16[256,512]{1,0:T(8,128)(2,1)}, f32[1,512]{1,0:T(1,128)S(1)}, bf16[256,128]{1,0:T(8,128)(2,1)S(1)}, bf16[256,128]{1,0:T(8,128)(2,1)S(1)}, /*index=5*/bf16[256,512]{1,0:T(8,128)(2,1)}, ...), branch_computations={%region_0.0_spmd, %region_1.0_spmd} | conditional | bytes 5243104 | solution.py:430
  18.6 1.3 %norm_0.2.refs_0_.mine_ref = bf16[128,512]{1,0:T(8,128)(2,1)S(1)} custom-call(bf16[256,512]{1,0:T(8,128)(2,1)S(1)} %get-tuple-element.61.scaled_ref, bf16[256,512]{1,0:T(8,128)(2,1)} %get-tuple-element.62.intra_ref, f32[1,512]{1,0:T(1,128)S(1)} %get-tuple-element.63.gain_ref, bf16[256,128]{1,0:T(8,128)(2,1)S(1)} %get-tuple-element.64.mine_ref, ...), custom_call_target="tpu_custom_call" | custom-call | tf_op jit(solution)/shard_map/cond/branch_1_fun/norm_0/pallas_call | solution.py:378
  20.0 1.2 %norm_1.2.refs_2_.mine_ref = bf16[128,512]{1,0:T(8,128)(2,1)S(1)} custom-call(bf16[256,512]{1,0:T(8,128)(2,1)S(1)} %get-tuple-element.61.scaled_ref, bf16[256,512]{1,0:T(8,128)(2,1)} %get-tuple-element.62.intra_ref, f32[1,512]{1,0:T(1,128)S(1)} %get-tuple-element.63.gain_ref, bf16[256,128]{1,0:T(8,128)(2,1)S(1)} %get-tuple-element.64.mine_ref, ...), custom_call_target="tpu_custom_call" | custom-call | tf_op jit(solution)/shard_map/cond/branch_1_fun/norm_1/pallas_call | solution.py:378
  21.3 0.6 %collective-permute-start.1 = (bf16[128,512]{1,0:T(8,128)(2,1)S(1)}, bf16[128,512]{1,0:T(8,128)(2,1)S(1)}, u32[]{:S(2)}, u32[]{:S(2)}) collective-permute-start(bf16[128,512]{1,0:T(8,128)(2,1)S(1)} %norm_1.2.refs_2_.mine_ref), channel_id=1, source_target_pairs={{0,1},{1,0},{2,3},{3,2},{4,5},{5,4},{6,7},{7,6},{8,9},{9,8},{10,11... | collective-permute-start | bytes 393224 | tf_op jit(solution)/shard_map/cond/branch_1_fun/ppermute | solution.py:384
  21.8 1.3 %project_far_0.2 = bf16[128,512]{1,0:T(8,128)(2,1)S(1)} custom-call(bf16[128,512]{1,0:T(8,128)(2,1)S(1)} %norm_0.2.refs_0_.mine_ref, bf16[128,512]{1,0:T(8,128)(2,1)S(1)} %collective-permute-done.refs_1_.other_ref, bf16[512,512]{1,0:T(8,128)(2,1)S(1)} %get-tuple-element.66.weight_ref, bf16[512,512]{1,0:T(8,128)(2,1)} %get-tuple-element.67.other_weight_ref), custom_call_target="tpu_custom_call" | custom-call | tf_op jit(solution)/shard_map/cond/branch_1_fun/project_far_0/pallas_call | solution.py:386
  23.2 1.6 %collective-permute-start.2 = (bf16[128,512]{1,0:T(8,128)(2,1)S(1)}, bf16[128,512]{1,0:T(8,128)(2,1)S(1)}, u32[]{:S(2)}, u32[]{:S(2)}) collective-permute-start(bf16[128,512]{1,0:T(8,128)(2,1)S(1)} %project_far_0.2), channel_id=1, source_target_pairs={{0,2},{1,3},{2,0},{3,1},{4,6},{5,7},{6,4},{7,5},{8,10},{9,11},{10,... | collective-permute-start | bytes 393224 | tf_op jit(solution)/shard_map/cond/branch_1_fun/ppermute | solution.py:392
  24.7 0.3 project_far_1.2
  25.1 0.6 %collective-permute-start.3 = (bf16[128,512]{1,0:T(8,128)(2,1)S(1)}, bf16[128,512]{1,0:T(8,128)(2,1)S(1)}, u32[]{:S(2)}, u32[]{:S(2)}) collective-permute-start(bf16[128,512]{1,0:T(8,128)(2,1)S(1)} %project_far_1.2), channel_id=1, source_target_pairs={{0,2},{1,3},{2,0},{3,1},{4,6},{5,7},{6,4},{7,5},{8,10},{9,11},{10,... | collective-permute-start | bytes 393224 | tf_op jit(solution)/shard_map/cond/branch_1_fun/ppermute | solution.py:392
  25.7 1.6 %project_near.2.near_ref = f32[256,512]{1,0:T(8,128)S(1)} custom-call(bf16[256,512]{1,0:T(8,128)(2,1)S(1)} %copy-done.3, bf16[512,2048]{1,0:T(8,128)(2,1)S(1)} %get-tuple-element.59.weight_hbm, bf16[512,2048]{1,0:T(8,128)(2,1)} %get-tuple-element.60.other_weight_hbm, bf16[128,512]{1,0:T(8,128)(2,1)S(1)} %norm_0.2.refs_0_.mine_ref, ...), custom_call_target="tpu_custom_call" | custom-call | tf_op jit(solution)/shard_map/cond/branch_1_fun/project_near/pallas_call | solution.py:393
  27.3 2.3 %collective-permute-done.2.refs_0_ = bf16[128,512]{1,0:T(8,128)(2,1)S(1)} collective-permute-done((bf16[128,512]{1,0:T(8,128)(2,1)S(1)}, bf16[128,512]{1,0:T(8,128)(2,1)S(1)}, u32[]{:S(2)}, u32[]{:S(2)}) %collective-permute-start.2) | collective-permute-done | bytes 131104 | tf_op jit(solution)/shard_map/cond/branch_1_fun/ppermute | solution.py:392
  29.6 1.9 %collective-permute-done.3.refs_1_ = bf16[128,512]{1,0:T(8,128)(2,1)S(1)} collective-permute-done((bf16[128,512]{1,0:T(8,128)(2,1)S(1)}, bf16[128,512]{1,0:T(8,128)(2,1)S(1)}, u32[]{:S(2)}, u32[]{:S(2)}) %collective-permute-start.3) | collective-permute-done | bytes 131104 | tf_op jit(solution)/shard_map/cond/branch_1_fun/ppermute | solution.py:392
  31.5 0.7 %add.2 = bf16[256,512]{1,0:T(8,128)(2,1)} custom-call(f32[256,512]{1,0:T(8,128)S(1)} %project_near.2.near_ref, bf16[128,512]{1,0:T(8,128)(2,1)S(1)} %collective-permute-done.2.refs_0_, bf16[128,512]{1,0:T(8,128)(2,1)S(1)} %collective-permute-done.3.refs_1_), custom_call_target="tpu_custom_call" | custom-call | tf_op jit(solution)/shard_map/cond/branch_1_fun/add/pallas_call | solution.py:405
  (17 shorter events, 0.3 us)
Async XLA Ops:
  0.0 16.3 %collective-permute-start.13 = (bf16[512,2048]{1,0:T(8,128)(2,1)}, bf16[512,2048]{1,0:T(8,128)(2,1)}, u32[]{:S(2)}, u32[]{:S(2)}) collective-permute-start(bf16[512,2048]{1,0:T(8,128)(2,1)} %weight_hbm.1), channel_id=1, source_target_pairs={{0,1},{1,0},{2,3},{3,2},{4,5},{5,4},{6,7},{7,6},{8,9},{9,8},{10,11... | collective-permute-start | bytes 6291464 | tf_op jit(solution)/shard_map/ppermute | solution.py:330
  1.8 6.2 %collective-permute-start.9 = (bf16[272,128]{1,0:T(8,128)(2,1)S(1)}, bf16[272,128]{1,0:T(8,128)(2,1)S(1)}, u32[]{:S(2)}, u32[]{:S(2)}) collective-permute-start(bf16[272,128]{1,0:T(8,128)(2,1)S(1)} %get-tuple-element.100), channel_id=1, source_target_pairs={{0,4},{4,0},{8,12},{12,8},{16,20},{20,16},{24,28},{28,24},{1,5},{5... | collective-permute-start | bytes 208904 | tf_op jit(solution)/shard_map/ppermute | solution.py:328
  4.4 5.5 %collective-permute-start.8 = (bf16[272,128]{1,0:T(8,128)(2,1)S(1)}, bf16[272,128]{1,0:T(8,128)(2,1)S(1)}, u32[]{:S(2)}, u32[]{:S(2)}) collective-permute-start(bf16[272,128]{1,0:T(8,128)(2,1)S(1)} %get-tuple-element.100), channel_id=1, source_target_pairs={{0,12},{4,8},{8,4},{12,0},{16,28},{20,24},{24,20},{28,16},{1,13},{... | collective-permute-start | bytes 208904 | tf_op jit(solution)/shard_map/ppermute | solution.py:328
  5.9 4.3 %collective-permute-start.10 = (bf16[272,128]{1,0:T(8,128)(2,1)S(1)}, bf16[272,128]{1,0:T(8,128)(2,1)S(1)}, u32[]{:S(2)}, u32[]{:S(2)}) collective-permute-start(bf16[272,128]{1,0:T(8,128)(2,1)S(1)} %get-tuple-element.101.refs_3_), channel_id=1, source_target_pairs={{0,8},{4,12},{8,0},{12,4},{16,24},{20,28},{24,16},{28,20},{1,9},{5... | collective-permute-start | bytes 208904 | tf_op jit(solution)/shard_map/ppermute | solution.py:328
  10.4 8.1 %collective-permute-start.12 = (bf16[272,128]{1,0:T(8,128)(2,1)S(1)}, bf16[272,128]{1,0:T(8,128)(2,1)S(1)}, u32[]{:S(2)}, u32[]{:S(2)}) collective-permute-start(bf16[272,128]{1,0:T(8,128)(2,1)S(1)} %get-tuple-element.105), channel_id=1, source_target_pairs={{0,16},{4,20},{8,24},{12,28},{16,0},{20,4},{24,8},{28,12},{1,17},{... | collective-permute-start | bytes 208904 | tf_op jit(solution)/shard_map/ppermute | solution.py:288
  13.0 5.5 %collective-permute-start.11 = (bf16[256,128]{1,0:T(8,128)(2,1)S(1)}, bf16[256,128]{1,0:T(8,128)(2,1)S(1)}, u32[]{:S(2)}, u32[]{:S(2)}) collective-permute-start(bf16[256,128]{1,0:T(8,128)(2,1)S(1)} %get-tuple-element.104), channel_id=1, source_target_pairs={{0,4},{4,0},{8,12},{12,8},{16,20},{20,16},{24,28},{28,24},{1,5},{5... | collective-permute-start | bytes 196616 | tf_op jit(solution)/shard_map/ppermute | solution.py:328
  14.6 17.7 %collective-permute-start.14 = (bf16[256,128]{1,0:T(8,128)(2,1)S(1)}, bf16[256,128]{1,0:T(8,128)(2,1)S(1)}, u32[]{:S(2)}, u32[]{:S(2)}) collective-permute-start(bf16[256,128]{1,0:T(8,128)(2,1)S(1)} %get-tuple-element.114), channel_id=1, source_target_pairs={{0,20},{4,16},{8,28},{12,24},{16,4},{20,0},{24,12},{28,8},{1,21},{... | collective-permute-start | bytes 196616 | tf_op jit(solution)/shard_map/ppermute | solution.py:288
  16.3 2.2 %copy-start = (bf16[512,2048]{1,0:T(8,128)(2,1)S(1)}, bf16[512,2048]{1,0:T(8,128)(2,1)}, u32[]{:S(2)}) copy-start(bf16[512,2048]{1,0:T(8,128)(2,1)} %weight_hbm.1) | copy-start | bytes 6291460
  18.6 6.2 %copy-start.1 = (bf16[512,512]{1,0:T(8,128)(2,1)S(1)}, bf16[512,512]{1,0:T(8,128)(2,1)}, u32[]{:S(2)}) copy-start(bf16[512,512]{1,0:T(8,128)(2,1)} %get-tuple-element.67.other_weight_ref) | copy-start | bytes 1572868 | tf_op jit(solution)/shard_map/cond
  18.6 7.1 %copy-start.3 = (bf16[256,512]{1,0:T(8,128)(2,1)S(1)}, bf16[256,512]{1,0:T(8,128)(2,1)}, u32[]{:S(2)}) copy-start(bf16[256,512]{1,0:T(8,128)(2,1)} %get-tuple-element.58.residual_hbm) | copy-start | bytes 786436 | tf_op jit(solution)/shard_map/cond
  19.9 1.9 %collective-permute-start = (bf16[128,512]{1,0:T(8,128)(2,1)S(1)}, bf16[128,512]{1,0:T(8,128)(2,1)S(1)}, u32[]{:S(2)}, u32[]{:S(2)}) collective-permute-start(bf16[128,512]{1,0:T(8,128)(2,1)S(1)} %norm_0.2.refs_0_.mine_ref), channel_id=1, source_target_pairs={{0,1},{1,0},{2,3},{3,2},{4,5},{5,4},{6,7},{7,6},{8,9},{9,8},{10,11... | collective-permute-start | bytes 393224 | tf_op jit(solution)/shard_map/cond/branch_1_fun/ppermute | solution.py:384
  21.3 3.5 %collective-permute-start.1 = (bf16[128,512]{1,0:T(8,128)(2,1)S(1)}, bf16[128,512]{1,0:T(8,128)(2,1)S(1)}, u32[]{:S(2)}, u32[]{:S(2)}) collective-permute-start(bf16[128,512]{1,0:T(8,128)(2,1)S(1)} %norm_1.2.refs_2_.mine_ref), channel_id=1, source_target_pairs={{0,1},{1,0},{2,3},{3,2},{4,5},{5,4},{6,7},{7,6},{8,9},{9,8},{10,11... | collective-permute-start | bytes 393224 | tf_op jit(solution)/shard_map/cond/branch_1_fun/ppermute | solution.py:384
  23.2 6.4 %collective-permute-start.2 = (bf16[128,512]{1,0:T(8,128)(2,1)S(1)}, bf16[128,512]{1,0:T(8,128)(2,1)S(1)}, u32[]{:S(2)}, u32[]{:S(2)}) collective-permute-start(bf16[128,512]{1,0:T(8,128)(2,1)S(1)} %project_far_0.2), channel_id=1, source_target_pairs={{0,2},{1,3},{2,0},{3,1},{4,6},{5,7},{6,4},{7,5},{8,10},{9,11},{10,... | collective-permute-start | bytes 393224 | tf_op jit(solution)/shard_map/cond/branch_1_fun/ppermute | solution.py:392
  25.1 6.4 %collective-permute-start.3 = (bf16[128,512]{1,0:T(8,128)(2,1)S(1)}, bf16[128,512]{1,0:T(8,128)(2,1)S(1)}, u32[]{:S(2)}, u32[]{:S(2)}) collective-permute-start(bf16[128,512]{1,0:T(8,128)(2,1)S(1)} %project_far_1.2), channel_id=1, source_target_pairs={{0,2},{1,3},{2,0},{3,1},{4,6},{5,7},{6,4},{7,5},{8,10},{9,11},{10,... | collective-permute-start | bytes 393224 | tf_op jit(solution)/shard_map/cond/branch_1_fun/ppermute | solution.py:392

commit v3 on v0

--- a/solution.py
+++ b/solution.py
@@ -14,7 +14,6 @@
 BF16 = jnp.bfloat16
 VMEM = pl.BlockSpec(memory_space=pltpu.VMEM)
 HBM = pl.BlockSpec(memory_space=pltpu.HBM)
-ANY = pl.BlockSpec(memory_space=pl.ANY)
 DECAY_ROWS = 16
 MEMBERS = 4
 PARAMS = pltpu.CompilerParams(vmem_limit_bytes=24 * 1024 * 1024)
@@ -134,7 +133,7 @@
 
 
 def gather_kernel(half, steps, *refs):
-    received, (before_ref, sent_ref, through_ref, total_ref, again_ref, held_ref) = (
+    received, (before_ref, sent_ref, through_ref, total_ref, held_ref) = (
         refs[: len(steps)],
         refs[len(steps) :],
     )
@@ -163,13 +162,12 @@
         before_ref[at, :] = jnp.where(upper, last, first)
         sent_ref[at, :] = jnp.where(upper, first, last).astype(BF16)
         total_ref[at, :] = held[MEMBERS].astype(BF16)
-        again_ref[at, :] = held[MEMBERS].astype(BF16)
         totals.append(through[MEMBERS])
     total_ref[half * HEAD_DIM :, :] = decays_to_rows(totals)
 
 
 def start_kernel(half, before_ref, through_ref, inside_ref, earlier_ref, _, *outs):
-    mine_ref, rest_ref, factor_ref = outs
+    mine_ref, rest_ref, factor_ref, sent_ref = outs
     started = lax.axis_index("seq") >= MEMBERS
     for j in range(half):
         at = state_rows(j)
@@ -178,6 +176,7 @@
         mine_ref[at, :] = held.astype(BF16)
     rest_ref[...] = inside_ref[...]
     factor_ref[...] = through_ref[8 * half :, :]
+    sent_ref[...] = earlier_ref[...]
 
 
 def start_other_kernel(half, rest_ref, factor_ref, earlier_ref, _, out_ref):
@@ -260,12 +259,8 @@
         out_ref[rows, :] = near
 
 
-def nothing_kernel(out_hbm):
-    pass
-
-
 def add_kernel(chunks, near_ref, *refs):
-    far, (out_hbm, out_ref, sems) = refs[: len(chunks)], refs[-3:]
+    far, (out_hbm, out_ref, sems) = refs[: len(chunks)], refs[len(chunks) :]
     copies = []
     for i, rows in enumerate(chunks):
         out_ref[rows, :] = (near_ref[rows, :] + far[i][...].astype(F32)).astype(BF16)
@@ -277,7 +272,7 @@
         copy.wait()
 
 
-def call(kernel, out_shape, in_specs, name, out_specs=None, scratch=(), cost=0, aliases={}):
+def call(kernel, out_shape, in_specs, name, out_specs=None, scratch=(), cost=0):
     single = isinstance(out_shape, jax.ShapeDtypeStruct)
     if out_specs is None:
         out_specs = VMEM if single else (VMEM,) * len(out_shape)
@@ -290,21 +285,16 @@
         in_specs=in_specs,
         out_specs=out_specs,
         scratch_shapes=scratch,
-        input_output_aliases=aliases,
         compiler_params=PARAMS,
         cost_estimate=cost,
         name=name,
     )
 
 
-def earlier_groups(total, again, half, devices):
+def earlier_groups(total, half, devices):
     groups = devices // MEMBERS
-
-    def swap(message, step):
-        return lax.ppermute(message, "seq", [(i, i ^ step) for i in range(devices)])
-
     if groups == 2:
-        return swap(total, MEMBERS), swap(again, MEMBERS + 1)
+        return lax.ppermute(total, "seq", [(i, i ^ MEMBERS) for i in range(devices)])
 
     def shift(message, by):
         moves = [(i, i + by * MEMBERS) for i in range(devices - by * MEMBERS)]
@@ -321,7 +311,7 @@
         through = [a * b for a, b in zip(decays, rows_to_decays(before[rows:], half))]
         held = jnp.concatenate([state.astype(BF16), decays_to_rows(through)], axis=0)
         by *= 2
-    return held, swap(held, 1)
+    return held
 
 
 def on_device(
@@ -344,6 +334,7 @@
         return lax.ppermute(piece, "seq", [(i, i ^ step) for i in range(devices)])
 
     other_weight = lax.ppermute(out_weight, "tp", near_pairs)
+    weight = pltpu.with_memory_space_constraint(out_weight, pltpu.HBM)
     arguments = (log_decay, key_vectors, value_vectors, query_vectors, norm_gain.reshape(1, -1))
     theirs, mine, decays, keys, values, queries, gain = call(
         functools.partial(state_kernel, half),
@@ -355,14 +346,14 @@
     steps = (3, 1, 2, 0)
     received = [swap(theirs, 3), swap(theirs, 1), swap(mine, 2), mine]
     state = shape(states, BF16)
-    before, sent, through, total, again = call(
+    before, sent, through, total = call(
         functools.partial(gather_kernel, half, steps),
-        (shape(states, F32), state, shape((heads * 8, HEAD_DIM), F32), message, state),
+        (shape(states, F32), state, shape((heads * 8, HEAD_DIM), F32), message),
         [VMEM] * len(steps),
         "gather_states",
         scratch=[pltpu.VMEM((MEMBERS,) + message.shape, BF16)],
     )(*received)
-    earlier, other_earlier = earlier_groups(total, again, half, devices)
+    earlier = earlier_groups(total, half, devices)
     inside = swap(sent, 1)
     intra, own = call(
         functools.partial(local_kernel, heads),
@@ -371,22 +362,17 @@
         "local",
         cost=4 * tokens * tokens * heads * HEAD_DIM,
     )(decays, queries, keys, values)
-    block = (out_weight.shape[0], out_width)
-    weights = (out_weight, other_weight)
-    far_weights = call(
-        fetch_kernel,
-        (shape(block, BF16),) * 2,
-        [ANY] * 2 + [VMEM],
-        "fetch_far",
-        scratch=[pltpu.SemaphoreType.DMA((2,))],
-    )(*weights, own)
-    mine, rest, factor = call(
+    mine, rest, factor, sent = call(
         functools.partial(start_kernel, half),
-        (state, state, shape((half * 8, HEAD_DIM), F32)),
+        (state, state, shape((half * 8, HEAD_DIM), F32), message),
         [VMEM] * 5,
         "start_states",
-    )(before, through, inside, earlier, far_weights[0])
+    )(before, through, inside, earlier, own)
+
     chunks = [slice(0, tokens // 2), slice(tokens // 2, tokens)]
+    block = (out_weight.shape[0], out_width)
+    weights = (weight, other_weight)
+    weight_specs = [HBM, pl.BlockSpec(memory_space=pl.ANY)]
 
     def normed(name, halves, rows, *states):
         part = call(
@@ -397,20 +383,29 @@
         )(queries, intra, own, gain, *states)
         return part, lax.ppermute(part, "tp", near_pairs)
 
-    def send_far(name, kernel, rows, *operands):
+    def far_columns(after):
+        return call(
+            fetch_kernel,
+            (shape(block, BF16),) * 2,
+            weight_specs + [VMEM],
+            "fetch_far",
+            scratch=[pltpu.SemaphoreType.DMA((2,))],
+        )(*weights, after)
+
+    def send_far(i, kernel, *operands):
         part = call(
             kernel,
-            shape((rows.stop - rows.start, out_width), BF16),
-            [VMEM] * (len(operands) + 2),
-            name,
-        )(*operands, *far_weights)
+            shape((chunks[i].stop - chunks[i].start, out_width), BF16),
+            [VMEM] * len(operands),
+            f"project_far_{i}",
+        )(*operands)
         return lax.ppermute(part, "tp", far_pairs)
 
-    def add(passes, pairs, far, out=()):
+    def finish(passes, pairs, far):
         near = call(
             functools.partial(near_kernel, chunks, passes),
             shape((tokens, out_width), F32),
-            [ANY] * 3 + [VMEM] * (2 * len(pairs)),
+            [HBM] + weight_specs + [VMEM] * (2 * len(pairs)),
             "project_near",
             scratch=[
                 pltpu.VMEM(residual.shape, BF16),
@@ -418,36 +413,34 @@
                 pltpu.VMEM(block, BF16),
                 pltpu.SemaphoreType.DMA((3,)),
             ],
-        )(residual, *weights, *(a for pair in pairs for a in pair))
+        )(
+            pltpu.with_memory_space_constraint(residual, pltpu.HBM),
+            *weights,
+            *(a for pair in pairs for a in pair),
+        )
         return call(
             functools.partial(add_kernel, chunks),
             pltpu.HBM((tokens, out_width), BF16),
-            [VMEM] * (1 + len(chunks)) + [HBM] * len(out),
+            [VMEM] * (1 + len(chunks)),
             "add",
             out_specs=HBM,
             scratch=[
                 pltpu.VMEM((tokens, out_width), BF16),
                 pltpu.SemaphoreType.DMA((len(chunks),)),
             ],
-            aliases={1 + len(chunks): 0} if out else {},
-        )(near, *far, *out)
+        )(near, *far)
 
     def first_group():
         both = (True, False)
         pairs = [normed(f"norm_{i}", both, rows, mine, rest) for i, rows in enumerate(chunks)]
-        far = [
-            send_far(f"project_far_{i}", far_all_kernel, rows, *pairs[i])
-            for i, rows in enumerate(chunks)
-        ]
-        return add((both,), pairs, far)
-
-    def not_yet():
-        return call(
-            nothing_kernel, pltpu.HBM((tokens, out_width), BF16), [], "nothing", out_specs=HBM
-        )()
-
-    def later_group(out):
+        far_weights = far_columns(pairs[-1][0])
+        far = [send_far(i, far_all_kernel, *pairs[i], *far_weights) for i in range(len(chunks))]
+        return finish((both,), pairs, far)
+
+    def later_group():
+        swapped = swap(sent, 1)
         begun = [normed(f"norm_mine_{i}", (True,), rows, mine) for i, rows in enumerate(chunks)]
+        far_weights = far_columns(begun[-1][0])
         far_begun = call(
             functools.partial(far_mine_kernel, chunks),
             shape((tokens, out_width), F32),
@@ -455,21 +448,17 @@
             "project_far_mine",
         )(*far_weights, *(a for pair in begun for a in pair))
         other = call(functools.partial(start_other_kernel, half), state, [VMEM] * 4, "start_other")(
-            rest, factor, other_earlier, far_begun
+            rest, factor, swapped, far_begun
         )
         parts = [normed(f"norm_{i}", (False,), rows, other) for i, rows in enumerate(chunks)]
         far = [
-            send_far(
-                f"project_far_{i}", functools.partial(far_kernel, rows), rows, far_begun, *parts[i]
-            )
+            send_far(i, functools.partial(far_kernel, rows), far_begun, *parts[i], *far_weights)
             for i, rows in enumerate(chunks)
         ]
         pairs = [pair for i in range(len(chunks)) for pair in (begun[i], parts[i])]
-        return add(((True,), (False,)), pairs, far, (out,))
-
-    first = lax.axis_index("seq") < MEMBERS
-    out = lax.cond(first, first_group, not_yet)
-    return lax.cond(first, lambda out: out, later_group, out)
+        return finish(((True,), (False,)), pairs, far)
+
+    return lax.cond(lax.axis_index("seq") < MEMBERS, first_group, later_group)
 
 
 def solution(mesh):

time: 31.9 us -> 30.4 us (0.953)
  starting transfers between devices: 11.4 us -> 9.21 us
  waiting for transfers between devices: 12.3 us -> 13.2 us
    ppermute x4 -> x5, waiting for transfers between devices: 3.6 us -> 7.03 us  [swap(): return lax.ppermute(piece, 'seq', [(i, i ^ step) for i in range(devices)])]
    ppermute x2 -> x1, starting transfers between devices: 3.8 us -> 0.4 us  [earlier_groups(): lax.ppermute(total, 'seq', [(i, i ^ MEMBERS) for i in range(devices)])]
    ppermute x2 -> x1, waiting for transfers between devices: 2.82 us -> 1.35 us  [earlier_groups(): lax.ppermute(total, 'seq', [(i, i ^ MEMBERS) for i in range(devices)])]
    ppermute x4 -> x5, starting transfers between devices: 4.21 us -> 5.4 us  [swap(): return lax.ppermute(piece, 'seq', [(i, i ^ step) for i in range(devices)])]
    ppermute x4, waiting for transfers between devices: 1.28 us -> 0.4 us  [normed(): return (part, lax.ppermute(part, 'tp', near_pairs))]
    pallas_call x6 -> x5, Pallas kernels: 4.06 us -> 3.85 us  [the longest x1 1.6 us: finish(): call(functools.partial(near_kernel, chunks, passes), shape((tokens, out_w...]
  transfers between devices with their start and end apart: 13 -> 13, of which waited for: 10 -> 9; matrix products, arithmetic and copies ran while one was open for 0% -> 0% of each run, Pallas kernels for 19% -> 22%
where the time goes in v3:
time: 30.4 us; the launch traced here: 30.2 us
  waiting for transfers between devices  13.2 us (43%)
  starting transfers between devices  9.21 us (30%)
  Pallas kernels  7.58 us (25%)
    ppermute x5, waiting for transfers between devices, swap(): return lax.ppermute(piece, 'seq', [(i, i ^ step) for i in range(devices)])  7.03 us
    ppermute x5, starting transfers between devices, swap(): return lax.ppermute(piece, 'seq', [(i, i ^ step) for i in range(devices)])  5.4 us
    ppermute x2, waiting for transfers between devices, send_far(): return lax.ppermute(part, 'tp', far_pairs)  4.43 us
    ppermute x2, starting transfers between devices, send_far(): return lax.ppermute(part, 'tp', far_pairs)  2.16 us
    pallas_call x1, Pallas kernels, finish(): call(functools.partial(near_kernel, chunks, passes), shape((tokens, out_w...  1.6 us
    pallas_call x1, Pallas kernels, on_device(): call(functools.partial(state_kernel, half), (message, message) + tuple((s...  1.37 us
    ppermute x1, waiting for transfers between devices, earlier_groups(): lax.ppermute(total, 'seq', [(i, i ^ MEMBERS) for i in range(devices)])  1.35 us
    ppermute x4, starting transfers between devices, normed(): return (part, lax.ppermute(part, 'tp', near_pairs))  1.26 us
  transfers between devices with their start and end apart: 13, of which 9 were waited for; matrix products, arithmetic and copies ran while one was open for 0% of the time, Pallas kernels for 22%

profile of v3, /device:TPU:24, one launch (start us, length us, event | category | flops | bytes accessed | tf_op | source)
XLA Modules:
  0.0 30.2 jit_solution(17564863261574436379)
XLA Ops:
  0.0 1.4 %states.1 = (bf16[272,128]{1,0:T(8,128)(2,1)S(1)}, bf16[272,128]{1,0:T(8,128)(2,1)S(1)}, f32[4,256]{1,0:T(4,128)S(1)}, bf16[256,512]{1,0:T(8,128)(2,1)S(1)}, bf1...) custom-call(f32[4,256]{1,0:T(4,128)} %refs_0_.1, bf16[256,512]{1,0:T(8,128)(2,1)} %refs_1_.1, ...), custom_call_target="tpu_custom_call" | custom-call | tf_op jit(solution)/shard_map/states/pallas_call | solution.py:339
  1.4 1.5 %collective-permute-start.11 = (bf16[272,128]{1,0:T(8,128)(2,1)S(1)}, bf16[272,128]{1,0:T(8,128)(2,1)S(1)}, u32[]{:S(2)}, u32[]{:S(2)}) collective-permute-start(bf16[272,128]{1,0:T(8,128)(2,1)S(1)} %get-tuple-element.96), channel_id=1, source_target_pairs={{0,12},{4,8},{8,4},{12,0},{16,28},{20,24},{24,20},{28,16},{1,13},{... | collective-permute-start | bytes 208904 | tf_op jit(solution)/shard_map/ppermute | solution.py:334
  2.9 0.5 %collective-permute-start.12 = (bf16[272,128]{1,0:T(8,128)(2,1)S(1)}, bf16[272,128]{1,0:T(8,128)(2,1)S(1)}, u32[]{:S(2)}, u32[]{:S(2)}) collective-permute-start(bf16[272,128]{1,0:T(8,128)(2,1)S(1)} %get-tuple-element.96), channel_id=1, source_target_pairs={{0,4},{4,0},{8,12},{12,8},{16,20},{20,16},{24,28},{28,24},{1,5},{5... | collective-permute-start | bytes 208904 | tf_op jit(solution)/shard_map/ppermute | solution.py:334
  3.4 1.6 %collective-permute-start.13 = (bf16[272,128]{1,0:T(8,128)(2,1)S(1)}, bf16[272,128]{1,0:T(8,128)(2,1)S(1)}, u32[]{:S(2)}, u32[]{:S(2)}) collective-permute-start(bf16[272,128]{1,0:T(8,128)(2,1)S(1)} %get-tuple-element.97.refs_3_), channel_id=1, source_target_pairs={{0,8},{4,12},{8,0},{12,4},{16,24},{20,28},{24,16},{28,20},{1,9},{5... | collective-permute-start | bytes 208904 | tf_op jit(solution)/shard_map/ppermute | solution.py:334
  4.9 2.1 %collective-permute-done.11.refs_0_ = bf16[272,128]{1,0:T(8,128)(2,1)S(1)} collective-permute-done((bf16[272,128]{1,0:T(8,128)(2,1)S(1)}, bf16[272,128]{1,0:T(8,128)(2,1)S(1)}, u32[]{:S(2)}, u32[]{:S(2)}) %collective-permute-start.11) | collective-permute-done | bytes 69664 | tf_op jit(solution)/shard_map/ppermute | solution.py:334
  7.0 1.4 %collective-permute-done.12.refs_1_ = bf16[272,128]{1,0:T(8,128)(2,1)S(1)} collective-permute-done((bf16[272,128]{1,0:T(8,128)(2,1)S(1)}, bf16[272,128]{1,0:T(8,128)(2,1)S(1)}, u32[]{:S(2)}, u32[]{:S(2)}) %collective-permute-start.12) | collective-permute-done | bytes 69664 | tf_op jit(solution)/shard_map/ppermute | solution.py:334
  8.7 0.4 %collective-permute-start.15 = (bf16[272,128]{1,0:T(8,128)(2,1)S(1)}, bf16[272,128]{1,0:T(8,128)(2,1)S(1)}, u32[]{:S(2)}, u32[]{:S(2)}) collective-permute-start(bf16[272,128]{1,0:T(8,128)(2,1)S(1)} %get-tuple-element.101), channel_id=1, source_target_pairs={{0,16},{4,20},{8,24},{12,28},{16,0},{20,4},{24,8},{28,12},{1,17},{... | collective-permute-start | bytes 208904 | tf_op jit(solution)/shard_map/ppermute | solution.py:297
  9.1 0.7 %collective-permute-start.14 = (bf16[256,128]{1,0:T(8,128)(2,1)S(1)}, bf16[256,128]{1,0:T(8,128)(2,1)S(1)}, u32[]{:S(2)}, u32[]{:S(2)}) collective-permute-start(bf16[256,128]{1,0:T(8,128)(2,1)S(1)} %get-tuple-element.100), channel_id=1, source_target_pairs={{0,4},{4,0},{8,12},{12,8},{16,20},{20,16},{24,28},{28,24},{1,5},{5... | collective-permute-start | bytes 196616 | tf_op jit(solution)/shard_map/ppermute | solution.py:334
  9.7 0.7 %local.1 = (f32[256,512]{1,0:T(8,128)S(1)}, f32[256,4]{1,0:T(8,128)S(1)}) custom-call(f32[4,256]{1,0:T(4,128)S(1)} %get-tuple-element.90.decay_ref, bf16[256,512]{1,0:T(8,128)(2,1)S(1)} %get-tuple-element.89.query_ref, bf16[256,512]{1,0:T(8,128)(2,1)S(1)} %get-tuple-element.91.key_ref, bf16[256,512]{1,0:T(8,128)(2,1)S(1)} %get-tuple-element.92.value_ref), custom_call_target="tpu_custom_call" | custom-call | flops 134217728 | bytes 2000000 | tf_op jit(solution)/shard_map/local/pallas_call | solution.py:358
  10.5 2.9 %collective-permute-done.14.inside_ref = bf16[256,128]{1,0:T(8,128)(2,1)S(1)} collective-permute-done((bf16[256,128]{1,0:T(8,128)(2,1)S(1)}, bf16[256,128]{1,0:T(8,128)(2,1)S(1)}, u32[]{:S(2)}, u32[]{:S(2)}) %collective-permute-start.14) | collective-permute-done | bytes 65568 | tf_op jit(solution)/shard_map/ppermute | solution.py:334
  13.3 1.4 %collective-permute-done.15.earlier_ref = bf16[272,128]{1,0:T(8,128)(2,1)S(1)} collective-permute-done((bf16[272,128]{1,0:T(8,128)(2,1)S(1)}, bf16[272,128]{1,0:T(8,128)(2,1)S(1)}, u32[]{:S(2)}, u32[]{:S(2)}) %collective-permute-start.15) | collective-permute-done | bytes 69664 | tf_op jit(solution)/shard_map/ppermute | solution.py:297
  14.7 15.4 %conditional.1 = (bf16[256,512]{1,0:T(8,128)(2,1)}) conditional(s32[]{:T(128)} %convert_element_type.3, (bf16[256,512]{1,0:T(8,128)(2,1)S(1)}, f32[256,512]{1,0:T(8,128)S(1)}, f32[256,4]{1,0:T(8,128)S(1)}, f32[1,512]{1,0:T(1,128)S(1)}, bf16[256,128]{1,0:T(8,128)(2,1)S(1)}, /*index=5*/bf16[272,128]{1,0:T(8,128)(2,1)S(1)}, bf16[512,2048]{1,0:T(8,128)(2,1)}, ...), branch_computations={%region_0.0_spmd, %region_1.0_spmd} | conditional | bytes 2375968 | solution.py:461
  14.7 1.2 %collective-permute-start.1 = (bf16[272,128]{1,0:T(8,128)(2,1)S(1)}, bf16[272,128]{1,0:T(8,128)(2,1)S(1)}, u32[]{:S(2)}, u32[]{:S(2)}) collective-permute-start(bf16[272,128]{1,0:T(8,128)(2,1)S(1)} %get-tuple-element.58), channel_id=1, source_target_pairs={{0,4},{4,0},{8,12},{12,8},{16,20},{20,16},{24,28},{28,24},{1,5},{5... | collective-permute-start | bytes 208904 | tf_op jit(solution)/shard_map/cond/branch_0_fun/ppermute | solution.py:334
  16.6 0.6 %collective-permute-start = (bf16[128,256]{1,0:T(8,128)(2,1)S(1)}, bf16[128,256]{1,0:T(8,128)(2,1)S(1)}, u32[]{:S(2)}, u32[]{:S(2)}) collective-permute-start(bf16[128,256]{1,0:T(8,128)(2,1)S(1)} %norm_mine_0.1.refs_0_), channel_id=1, source_target_pairs={{0,1},{1,0},{2,3},{3,2},{4,5},{5,4},{6,7},{7,6},{8,9},{9,8},{10,11... | collective-permute-start | bytes 196616 | tf_op jit(solution)/shard_map/cond/branch_0_fun/ppermute | solution.py:384
  17.1 1.1 %fetch_far.2 = (bf16[512,512]{1,0:T(8,128)(2,1)S(1)}, bf16[512,512]{1,0:T(8,128)(2,1)S(1)}) custom-call(bf16[512,2048]{1,0:T(8,128)(2,1)} %get-tuple-element.49.weight_hbm, bf16[512,2048]{1,0:T(8,128)(2,1)S(1)} %get-tuple-element.50.other_weight_hbm, bf16[128,256]{1,0:T(8,128)(2,1)S(1)} %norm_mine_1.1._.refs_2_.refs_4_), custom_call_target="tpu_custom_call" | custom-call | tf_op jit(solution)/shard_map/cond/branch_0_fun/fetch_far/pallas_call | solution.py:387
  18.6 0.6 %collective-permute-done.1.earlier_ref = bf16[272,128]{1,0:T(8,128)(2,1)S(1)} collective-permute-done((bf16[272,128]{1,0:T(8,128)(2,1)S(1)}, bf16[272,128]{1,0:T(8,128)(2,1)S(1)}, u32[]{:S(2)}, u32[]{:S(2)}) %collective-permute-start.1) | collective-permute-done | bytes 69664 | tf_op jit(solution)/shard_map/cond/branch_0_fun/ppermute | solution.py:334
  19.8 0.6 %collective-permute-start.3 = (bf16[128,256]{1,0:T(8,128)(2,1)S(1)}, bf16[128,256]{1,0:T(8,128)(2,1)S(1)}, u32[]{:S(2)}, u32[]{:S(2)}) collective-permute-start(bf16[128,256]{1,0:T(8,128)(2,1)S(1)} %norm_0.2.refs_2_.mine_ref), channel_id=1, source_target_pairs={{0,1},{1,0},{2,3},{3,2},{4,5},{5,4},{6,7},{7,6},{8,9},{9,8},{10,11... | collective-permute-start | bytes 196616 | tf_op jit(solution)/shard_map/cond/branch_0_fun/ppermute | solution.py:384
  20.4 0.4 %collective-permute-done.4.refs_7_.other_ref = bf16[128,256]{1,0:T(8,128)(2,1)S(1)} collective-permute-done((bf16[128,256]{1,0:T(8,128)(2,1)S(1)}, bf16[128,256]{1,0:T(8,128)(2,1)S(1)}, u32[]{:S(2)}, u32[]{:S(2)}) %collective-permute-start.4) | collective-permute-done | bytes 65568 | tf_op jit(solution)/shard_map/cond/branch_0_fun/ppermute | solution.py:384
  21.0 1.6 %collective-permute-start.6 = (bf16[128,512]{1,0:T(8,128)(2,1)S(1)}, bf16[128,512]{1,0:T(8,128)(2,1)S(1)}, u32[]{:S(2)}, u32[]{:S(2)}) collective-permute-start(bf16[128,512]{1,0:T(8,128)(2,1)S(1)} %project_far_1.2), channel_id=1, source_target_pairs={{0,2},{1,3},{2,0},{3,1},{4,6},{5,7},{6,4},{7,5},{8,10},{9,11},{10,... | collective-permute-start | bytes 393224 | tf_op jit(solution)/shard_map/cond/branch_0_fun/ppermute | solution.py:402
  22.8 0.6 %collective-permute-start.5 = (bf16[128,512]{1,0:T(8,128)(2,1)S(1)}, bf16[128,512]{1,0:T(8,128)(2,1)S(1)}, u32[]{:S(2)}, u32[]{:S(2)}) collective-permute-start(bf16[128,512]{1,0:T(8,128)(2,1)S(1)} %project_far_0.2), channel_id=1, source_target_pairs={{0,2},{1,3},{2,0},{3,1},{4,6},{5,7},{6,4},{7,5},{8,10},{9,11},{10,... | collective-permute-start | bytes 393224 | tf_op jit(solution)/shard_map/cond/branch_0_fun/ppermute | solution.py:402
  23.4 1.6 %project_near.2.near_ref = f32[256,512]{1,0:T(8,128)S(1)} custom-call(bf16[256,512]{1,0:T(8,128)(2,1)} %get-tuple-element.48.residual_hbm, bf16[512,2048]{1,0:T(8,128)(2,1)} %get-tuple-element.49.weight_hbm, bf16[512,2048]{1,0:T(8,128)(2,1)S(1)} %get-tuple-element.50.other_weight_hbm, bf16[128,256]{1,0:T(8,128)(2,1)S(1)} %norm_mine_0.1.refs_0_, ...), custom_call_target="tpu_custom_call" | custom-call | tf_op jit(solution)/shard_map/cond/branch_0_fun/project_near/pallas_call | solution.py:405
  25.0 2.4 %collective-permute-done.6.refs_1_ = bf16[128,512]{1,0:T(8,128)(2,1)S(1)} collective-permute-done((bf16[128,512]{1,0:T(8,128)(2,1)S(1)}, bf16[128,512]{1,0:T(8,128)(2,1)S(1)}, u32[]{:S(2)}, u32[]{:S(2)}) %collective-permute-start.6) | collective-permute-done | bytes 131104 | tf_op jit(solution)/shard_map/cond/branch_0_fun/ppermute | solution.py:402
  27.4 2.0 %collective-permute-done.5.refs_0_ = bf16[128,512]{1,0:T(8,128)(2,1)S(1)} collective-permute-done((bf16[128,512]{1,0:T(8,128)(2,1)S(1)}, bf16[128,512]{1,0:T(8,128)(2,1)S(1)}, u32[]{:S(2)}, u32[]{:S(2)}) %collective-permute-start.5) | collective-permute-done | bytes 131104 | tf_op jit(solution)/shard_map/cond/branch_0_fun/ppermute | solution.py:402
  29.4 0.7 %add.2 = bf16[256,512]{1,0:T(8,128)(2,1)} custom-call(f32[256,512]{1,0:T(8,128)S(1)} %project_near.2.near_ref, bf16[128,512]{1,0:T(8,128)(2,1)S(1)} %collective-permute-done.5.refs_0_, bf16[128,512]{1,0:T(8,128)(2,1)S(1)} %collective-permute-done.6.refs_1_), custom_call_target="tpu_custom_call" | custom-call | tf_op jit(solution)/shard_map/cond/branch_0_fun/add/pallas_call | solution.py:421
  (18 shorter events, 2.3 us)
Async XLA Ops:
  0.0 14.7 %collective-permute-start.16 = (bf16[512,2048]{1,0:T(8,128)(2,1)}, bf16[512,2048]{1,0:T(8,128)(2,1)S(1)}, u32[]{:S(2)}, u32[]{:S(2)}) collective-permute-start(bf16[512,2048]{1,0:T(8,128)(2,1)} %param.15), channel_id=1, source_target_pairs={{0,1},{1,0},{2,3},{3,2},{4,5},{5,4},{6,7},{7,6},{8,9},{9,8},{10,11... | collective-permute-start | bytes 6291464 | tf_op jit(solution)/shard_map/ppermute | solution.py:336
  1.4 5.7 %collective-permute-start.11 = (bf16[272,128]{1,0:T(8,128)(2,1)S(1)}, bf16[272,128]{1,0:T(8,128)(2,1)S(1)}, u32[]{:S(2)}, u32[]{:S(2)}) collective-permute-start(bf16[272,128]{1,0:T(8,128)(2,1)S(1)} %get-tuple-element.96), channel_id=1, source_target_pairs={{0,12},{4,8},{8,4},{12,0},{16,28},{20,24},{24,20},{28,16},{1,13},{... | collective-permute-start | bytes 208904 | tf_op jit(solution)/shard_map/ppermute | solution.py:334
  2.9 5.6 %collective-permute-start.12 = (bf16[272,128]{1,0:T(8,128)(2,1)S(1)}, bf16[272,128]{1,0:T(8,128)(2,1)S(1)}, u32[]{:S(2)}, u32[]{:S(2)}) collective-permute-start(bf16[272,128]{1,0:T(8,128)(2,1)S(1)} %get-tuple-element.96), channel_id=1, source_target_pairs={{0,4},{4,0},{8,12},{12,8},{16,20},{20,16},{24,28},{28,24},{1,5},{5... | collective-permute-start | bytes 208904 | tf_op jit(solution)/shard_map/ppermute | solution.py:334
  3.4 5.2 %collective-permute-start.13 = (bf16[272,128]{1,0:T(8,128)(2,1)S(1)}, bf16[272,128]{1,0:T(8,128)(2,1)S(1)}, u32[]{:S(2)}, u32[]{:S(2)}) collective-permute-start(bf16[272,128]{1,0:T(8,128)(2,1)S(1)} %get-tuple-element.97.refs_3_), channel_id=1, source_target_pairs={{0,8},{4,12},{8,0},{12,4},{16,24},{20,28},{24,16},{28,20},{1,9},{5... | collective-permute-start | bytes 208904 | tf_op jit(solution)/shard_map/ppermute | solution.py:334
  8.7 6.0 %collective-permute-start.15 = (bf16[272,128]{1,0:T(8,128)(2,1)S(1)}, bf16[272,128]{1,0:T(8,128)(2,1)S(1)}, u32[]{:S(2)}, u32[]{:S(2)}) collective-permute-start(bf16[272,128]{1,0:T(8,128)(2,1)S(1)} %get-tuple-element.101), channel_id=1, source_target_pairs={{0,16},{4,20},{8,24},{12,28},{16,0},{20,4},{24,8},{28,12},{1,17},{... | collective-permute-start | bytes 208904 | tf_op jit(solution)/shard_map/ppermute | solution.py:297
  9.1 4.3 %collective-permute-start.14 = (bf16[256,128]{1,0:T(8,128)(2,1)S(1)}, bf16[256,128]{1,0:T(8,128)(2,1)S(1)}, u32[]{:S(2)}, u32[]{:S(2)}) collective-permute-start(bf16[256,128]{1,0:T(8,128)(2,1)S(1)} %get-tuple-element.100), channel_id=1, source_target_pairs={{0,4},{4,0},{8,12},{12,8},{16,20},{20,16},{24,28},{28,24},{1,5},{5... | collective-permute-start | bytes 196616 | tf_op jit(solution)/shard_map/ppermute | solution.py:334
  14.7 4.4 %collective-permute-start.1 = (bf16[272,128]{1,0:T(8,128)(2,1)S(1)}, bf16[272,128]{1,0:T(8,128)(2,1)S(1)}, u32[]{:S(2)}, u32[]{:S(2)}) collective-permute-start(bf16[272,128]{1,0:T(8,128)(2,1)S(1)} %get-tuple-element.58), channel_id=1, source_target_pairs={{0,4},{4,0},{8,12},{12,8},{16,20},{20,16},{24,28},{28,24},{1,5},{5... | collective-permute-start | bytes 208904 | tf_op jit(solution)/shard_map/cond/branch_0_fun/ppermute | solution.py:334
  16.2 2.0 %collective-permute-start.2 = (bf16[128,256]{1,0:T(8,128)(2,1)S(1)}, bf16[128,256]{1,0:T(8,128)(2,1)S(1)}, u32[]{:S(2)}, u32[]{:S(2)}) collective-permute-start(bf16[128,256]{1,0:T(8,128)(2,1)S(1)} %norm_mine_1.1._.refs_2_.refs_4_), channel_id=1, source_target_pairs={{0,1},{1,0},{2,3},{3,2},{4,5},{5,4},{6,7},{7,6},{8,9},{9,8},{10,11... | collective-permute-start | bytes 196616 | tf_op jit(solution)/shard_map/cond/branch_0_fun/ppermute | solution.py:384
  16.6 1.6 %collective-permute-start = (bf16[128,256]{1,0:T(8,128)(2,1)S(1)}, bf16[128,256]{1,0:T(8,128)(2,1)S(1)}, u32[]{:S(2)}, u32[]{:S(2)}) collective-permute-start(bf16[128,256]{1,0:T(8,128)(2,1)S(1)} %norm_mine_0.1.refs_0_), channel_id=1, source_target_pairs={{0,1},{1,0},{2,3},{3,2},{4,5},{5,4},{6,7},{7,6},{8,9},{9,8},{10,11... | collective-permute-start | bytes 196616 | tf_op jit(solution)/shard_map/cond/branch_0_fun/ppermute | solution.py:384
  19.4 1.3 %collective-permute-start.4 = (bf16[128,256]{1,0:T(8,128)(2,1)S(1)}, bf16[128,256]{1,0:T(8,128)(2,1)S(1)}, u32[]{:S(2)}, u32[]{:S(2)}) collective-permute-start(bf16[128,256]{1,0:T(8,128)(2,1)S(1)} %norm_1.2.refs_6_.mine_ref), channel_id=1, source_target_pairs={{0,1},{1,0},{2,3},{3,2},{4,5},{5,4},{6,7},{7,6},{8,9},{9,8},{10,11... | collective-permute-start | bytes 196616 | tf_op jit(solution)/shard_map/cond/branch_0_fun/ppermute | solution.py:384
  19.8 2.7 %collective-permute-start.3 = (bf16[128,256]{1,0:T(8,128)(2,1)S(1)}, bf16[128,256]{1,0:T(8,128)(2,1)S(1)}, u32[]{:S(2)}, u32[]{:S(2)}) collective-permute-start(bf16[128,256]{1,0:T(8,128)(2,1)S(1)} %norm_0.2.refs_2_.mine_ref), channel_id=1, source_target_pairs={{0,1},{1,0},{2,3},{3,2},{4,5},{5,4},{6,7},{7,6},{8,9},{9,8},{10,11... | collective-permute-start | bytes 196616 | tf_op jit(solution)/shard_map/cond/branch_0_fun/ppermute | solution.py:384
  21.0 6.4 %collective-permute-start.6 = (bf16[128,512]{1,0:T(8,128)(2,1)S(1)}, bf16[128,512]{1,0:T(8,128)(2,1)S(1)}, u32[]{:S(2)}, u32[]{:S(2)}) collective-permute-start(bf16[128,512]{1,0:T(8,128)(2,1)S(1)} %project_far_1.2), channel_id=1, source_target_pairs={{0,2},{1,3},{2,0},{3,1},{4,6},{5,7},{6,4},{7,5},{8,10},{9,11},{10,... | collective-permute-start | bytes 393224 | tf_op jit(solution)/shard_map/cond/branch_0_fun/ppermute | solution.py:402
  22.8 6.6 %collective-permute-start.5 = (bf16[128,512]{1,0:T(8,128)(2,1)S(1)}, bf16[128,512]{1,0:T(8,128)(2,1)S(1)}, u32[]{:S(2)}, u32[]{:S(2)}) collective-permute-start(bf16[128,512]{1,0:T(8,128)(2,1)S(1)} %project_far_0.2), channel_id=1, source_target_pairs={{0,2},{1,3},{2,0},{3,1},{4,6},{5,7},{6,4},{7,5},{8,10},{9,11},{10,... | collective-permute-start | bytes 393224 | tf_op jit(solution)/shard_map/cond/branch_0_fun/ppermute | solution.py:402

commit v4 on v3

--- a/solution.py
+++ b/solution.py
@@ -343,8 +343,8 @@
         "states",
         scratch=[pltpu.SemaphoreType.DMA((5,))],
     )(*(pltpu.with_memory_space_constraint(a, pltpu.HBM) for a in arguments))
-    steps = (3, 1, 2, 0)
-    received = [swap(theirs, 3), swap(theirs, 1), swap(mine, 2), mine]
+    steps = (3, 2, 1, 0)
+    received = [swap(theirs, 3), swap(mine, 2), swap(theirs, 1), mine]
     state = shape(states, BF16)
     before, sent, through, total = call(
         functools.partial(gather_kernel, half, steps),

time: 30.4 us -> 30.7 us (level)
  starting transfers between devices: 9.21 us -> 10.4 us
  waiting for transfers between devices: 13.2 us -> 12.2 us
    ppermute x5, starting transfers between devices: 5.4 us -> 6.55 us  [swap(): return lax.ppermute(piece, 'seq', [(i, i ^ step) for i in range(devices)])]
    ppermute x5, waiting for transfers between devices: 7.03 us -> 6.12 us  [swap(): return lax.ppermute(piece, 'seq', [(i, i ^ step) for i in range(devices)])]
  transfers between devices with their start and end apart: 13 -> 13, of which waited for: 9 -> 8; matrix products, arithmetic and copies ran while one was open for 0% -> 0% of each run, Pallas kernels for 22% -> 22%
where the time goes in v4:
time: 30.7 us; the launch traced here: 30.3 us
  waiting for transfers between devices  12.2 us (40%)
  starting transfers between devices  10.4 us (34%)
  Pallas kernels  7.58 us (25%)
    ppermute x5, starting transfers between devices, swap(): return lax.ppermute(piece, 'seq', [(i, i ^ step) for i in range(devices)])  6.55 us
    ppermute x5, waiting for transfers between devices, swap(): return lax.ppermute(piece, 'seq', [(i, i ^ step) for i in range(devices)])  6.12 us
    ppermute x2, waiting for transfers between devices, send_far(): return lax.ppermute(part, 'tp', far_pairs)  4.43 us
    ppermute x2, starting transfers between devices, send_far(): return lax.ppermute(part, 'tp', far_pairs)  2.16 us
    pallas_call x1, Pallas kernels, finish(): call(functools.partial(near_kernel, chunks, passes), shape((tokens, out_w...  1.6 us
    pallas_call x1, Pallas kernels, on_device(): call(functools.partial(state_kernel, half), (message, message) + tuple((s...  1.37 us
    ppermute x4, starting transfers between devices, normed(): return (part, lax.ppermute(part, 'tp', near_pairs))  1.27 us
    ppermute x1, waiting for transfers between devices, earlier_groups(): lax.ppermute(total, 'seq', [(i, i ^ MEMBERS) for i in range(devices)])  1.24 us
  transfers between devices with their start and end apart: 13, of which 8 were waited for; matrix products, arithmetic and copies ran while one was open for 0% of the time, Pallas kernels for 22%

profile of v4, /device:TPU:24, one launch (start us, length us, event | category | flops | bytes accessed | tf_op | source)
XLA Modules:
  0.0 30.3 jit_solution(16480658618540894519)
XLA Ops:
  0.0 1.4 %states.1 = (bf16[272,128]{1,0:T(8,128)(2,1)S(1)}, bf16[272,128]{1,0:T(8,128)(2,1)S(1)}, f32[4,256]{1,0:T(4,128)S(1)}, bf16[256,512]{1,0:T(8,128)(2,1)S(1)}, bf1...) custom-call(f32[4,256]{1,0:T(4,128)} %refs_0_.1, bf16[256,512]{1,0:T(8,128)(2,1)} %refs_1_.1, ...), custom_call_target="tpu_custom_call" | custom-call | tf_op jit(solution)/shard_map/states/pallas_call | solution.py:339
  1.4 1.5 %collective-permute-start.11 = (bf16[272,128]{1,0:T(8,128)(2,1)S(1)}, bf16[272,128]{1,0:T(8,128)(2,1)S(1)}, u32[]{:S(2)}, u32[]{:S(2)}) collective-permute-start(bf16[272,128]{1,0:T(8,128)(2,1)S(1)} %get-tuple-element.96), channel_id=1, source_target_pairs={{0,12},{4,8},{8,4},{12,0},{16,28},{20,24},{24,20},{28,16},{1,13},{... | collective-permute-start | bytes 208904 | tf_op jit(solution)/shard_map/ppermute | solution.py:334
  2.9 1.6 %collective-permute-start.12 = (bf16[272,128]{1,0:T(8,128)(2,1)S(1)}, bf16[272,128]{1,0:T(8,128)(2,1)S(1)}, u32[]{:S(2)}, u32[]{:S(2)}) collective-permute-start(bf16[272,128]{1,0:T(8,128)(2,1)S(1)} %get-tuple-element.97.refs_3_), channel_id=1, source_target_pairs={{0,8},{4,12},{8,0},{12,4},{16,24},{20,28},{24,16},{28,20},{1,9},{5... | collective-permute-start | bytes 208904 | tf_op jit(solution)/shard_map/ppermute | solution.py:334
  4.4 0.5 %collective-permute-start.13 = (bf16[272,128]{1,0:T(8,128)(2,1)S(1)}, bf16[272,128]{1,0:T(8,128)(2,1)S(1)}, u32[]{:S(2)}, u32[]{:S(2)}) collective-permute-start(bf16[272,128]{1,0:T(8,128)(2,1)S(1)} %get-tuple-element.96), channel_id=1, source_target_pairs={{0,4},{4,0},{8,12},{12,8},{16,20},{20,16},{24,28},{28,24},{1,5},{5... | collective-permute-start | bytes 208904 | tf_op jit(solution)/shard_map/ppermute | solution.py:334
  4.9 2.4 %collective-permute-done.11.refs_0_ = bf16[272,128]{1,0:T(8,128)(2,1)S(1)} collective-permute-done((bf16[272,128]{1,0:T(8,128)(2,1)S(1)}, bf16[272,128]{1,0:T(8,128)(2,1)S(1)}, u32[]{:S(2)}, u32[]{:S(2)}) %collective-permute-start.11) | collective-permute-done | bytes 69664 | tf_op jit(solution)/shard_map/ppermute | solution.py:334
  7.3 1.2 %collective-permute-done.12.refs_1_ = bf16[272,128]{1,0:T(8,128)(2,1)S(1)} collective-permute-done((bf16[272,128]{1,0:T(8,128)(2,1)S(1)}, bf16[272,128]{1,0:T(8,128)(2,1)S(1)}, u32[]{:S(2)}, u32[]{:S(2)}) %collective-permute-start.12) | collective-permute-done | bytes 69664 | tf_op jit(solution)/shard_map/ppermute | solution.py:334
  8.9 0.4 %collective-permute-start.15 = (bf16[272,128]{1,0:T(8,128)(2,1)S(1)}, bf16[272,128]{1,0:T(8,128)(2,1)S(1)}, u32[]{:S(2)}, u32[]{:S(2)}) collective-permute-start(bf16[272,128]{1,0:T(8,128)(2,1)S(1)} %get-tuple-element.101), channel_id=1, source_target_pairs={{0,16},{4,20},{8,24},{12,28},{16,0},{20,4},{24,8},{28,12},{1,17},{... | collective-permute-start | bytes 208904 | tf_op jit(solution)/shard_map/ppermute | solution.py:297
  9.3 1.2 %collective-permute-start.14 = (bf16[256,128]{1,0:T(8,128)(2,1)S(1)}, bf16[256,128]{1,0:T(8,128)(2,1)S(1)}, u32[]{:S(2)}, u32[]{:S(2)}) collective-permute-start(bf16[256,128]{1,0:T(8,128)(2,1)S(1)} %get-tuple-element.100), channel_id=1, source_target_pairs={{0,4},{4,0},{8,12},{12,8},{16,20},{20,16},{24,28},{28,24},{1,5},{5... | collective-permute-start | bytes 196616 | tf_op jit(solution)/shard_map/ppermute | solution.py:334
  10.5 0.7 %local.1 = (f32[256,512]{1,0:T(8,128)S(1)}, f32[256,4]{1,0:T(8,128)S(1)}) custom-call(f32[4,256]{1,0:T(4,128)S(1)} %get-tuple-element.90.decay_ref, bf16[256,512]{1,0:T(8,128)(2,1)S(1)} %get-tuple-element.89.query_ref, bf16[256,512]{1,0:T(8,128)(2,1)S(1)} %get-tuple-element.91.key_ref, bf16[256,512]{1,0:T(8,128)(2,1)S(1)} %get-tuple-element.92.value_ref), custom_call_target="tpu_custom_call" | custom-call | flops 134217728 | bytes 2000000 | tf_op jit(solution)/shard_map/local/pallas_call | solution.py:358
  11.2 2.3 %collective-permute-done.14.inside_ref = bf16[256,128]{1,0:T(8,128)(2,1)S(1)} collective-permute-done((bf16[256,128]{1,0:T(8,128)(2,1)S(1)}, bf16[256,128]{1,0:T(8,128)(2,1)S(1)}, u32[]{:S(2)}, u32[]{:S(2)}) %collective-permute-start.14) | collective-permute-done | bytes 65568 | tf_op jit(solution)/shard_map/ppermute | solution.py:334
  13.5 1.2 %collective-permute-done.15.earlier_ref = bf16[272,128]{1,0:T(8,128)(2,1)S(1)} collective-permute-done((bf16[272,128]{1,0:T(8,128)(2,1)S(1)}, bf16[272,128]{1,0:T(8,128)(2,1)S(1)}, u32[]{:S(2)}, u32[]{:S(2)}) %collective-permute-start.15) | collective-permute-done | bytes 69664 | tf_op jit(solution)/shard_map/ppermute | solution.py:297
  14.8 15.5 %conditional.1 = (bf16[256,512]{1,0:T(8,128)(2,1)}) conditional(s32[]{:T(128)} %convert_element_type.3, (bf16[256,512]{1,0:T(8,128)(2,1)S(1)}, f32[256,512]{1,0:T(8,128)S(1)}, f32[256,4]{1,0:T(8,128)S(1)}, f32[1,512]{1,0:T(1,128)S(1)}, bf16[256,128]{1,0:T(8,128)(2,1)S(1)}, /*index=5*/bf16[272,128]{1,0:T(8,128)(2,1)S(1)}, bf16[512,2048]{1,0:T(8,128)(2,1)}, ...), branch_computations={%region_0.0_spmd, %region_1.0_spmd} | conditional | bytes 2375968 | solution.py:461
  14.8 1.8 %collective-permute-start.1 = (bf16[272,128]{1,0:T(8,128)(2,1)S(1)}, bf16[272,128]{1,0:T(8,128)(2,1)S(1)}, u32[]{:S(2)}, u32[]{:S(2)}) collective-permute-start(bf16[272,128]{1,0:T(8,128)(2,1)S(1)} %get-tuple-element.58), channel_id=1, source_target_pairs={{0,4},{4,0},{8,12},{12,8},{16,20},{20,16},{24,28},{28,24},{1,5},{5... | collective-permute-start | bytes 208904 | tf_op jit(solution)/shard_map/cond/branch_0_fun/ppermute | solution.py:334
  17.3 0.6 %collective-permute-start = (bf16[128,256]{1,0:T(8,128)(2,1)S(1)}, bf16[128,256]{1,0:T(8,128)(2,1)S(1)}, u32[]{:S(2)}, u32[]{:S(2)}) collective-permute-start(bf16[128,256]{1,0:T(8,128)(2,1)S(1)} %norm_mine_0.1.refs_0_), channel_id=1, source_target_pairs={{0,1},{1,0},{2,3},{3,2},{4,5},{5,4},{6,7},{7,6},{8,9},{9,8},{10,11... | collective-permute-start | bytes 196616 | tf_op jit(solution)/shard_map/cond/branch_0_fun/ppermute | solution.py:384
  17.8 1.1 %fetch_far.2 = (bf16[512,512]{1,0:T(8,128)(2,1)S(1)}, bf16[512,512]{1,0:T(8,128)(2,1)S(1)}) custom-call(bf16[512,2048]{1,0:T(8,128)(2,1)} %get-tuple-element.49.weight_hbm, bf16[512,2048]{1,0:T(8,128)(2,1)S(1)} %get-tuple-element.50.other_weight_hbm, bf16[128,256]{1,0:T(8,128)(2,1)S(1)} %norm_mine_1.1._.refs_2_.refs_4_), custom_call_target="tpu_custom_call" | custom-call | tf_op jit(solution)/shard_map/cond/branch_0_fun/fetch_far/pallas_call | solution.py:387
  18.9 0.3 %project_far_mine.1._.begun_ref = f32[256,512]{1,0:T(8,128)S(1)} custom-call(bf16[512,512]{1,0:T(8,128)(2,1)S(1)} %get-tuple-element.59.weight_ref, bf16[512,512]{1,0:T(8,128)(2,1)S(1)} %get-tuple-element.60.other_weight_ref, bf16[128,256]{1,0:T(8,128)(2,1)S(1)} %norm_mine_0.1.refs_0_, bf16[128,256]{1,0:T(8,128)(2,1)S(1)} %collective-permute-done.refs_1_, ...), custom_call_target="tpu_custom_call" | custom-call | tf_op jit(solution)/shard_map/cond/branch_0_fun/project_far_mine/pallas_call | solution.py:444
  20.1 0.4 %collective-permute-start.3 = (bf16[128,256]{1,0:T(8,128)(2,1)S(1)}, bf16[128,256]{1,0:T(8,128)(2,1)S(1)}, u32[]{:S(2)}, u32[]{:S(2)}) collective-permute-start(bf16[128,256]{1,0:T(8,128)(2,1)S(1)} %norm_0.2.refs_2_.mine_ref), channel_id=1, source_target_pairs={{0,1},{1,0},{2,3},{3,2},{4,5},{5,4},{6,7},{7,6},{8,9},{9,8},{10,11... | collective-permute-start | bytes 196616 | tf_op jit(solution)/shard_map/cond/branch_0_fun/ppermute | solution.py:384
  20.5 0.4 %collective-permute-done.4.refs_7_.other_ref = bf16[128,256]{1,0:T(8,128)(2,1)S(1)} collective-permute-done((bf16[128,256]{1,0:T(8,128)(2,1)S(1)}, bf16[128,256]{1,0:T(8,128)(2,1)S(1)}, u32[]{:S(2)}, u32[]{:S(2)}) %collective-permute-start.4) | collective-permute-done | bytes 65568 | tf_op jit(solution)/shard_map/cond/branch_0_fun/ppermute | solution.py:384
  21.1 1.6 %collective-permute-start.6 = (bf16[128,512]{1,0:T(8,128)(2,1)S(1)}, bf16[128,512]{1,0:T(8,128)(2,1)S(1)}, u32[]{:S(2)}, u32[]{:S(2)}) collective-permute-start(bf16[128,512]{1,0:T(8,128)(2,1)S(1)} %project_far_1.2), channel_id=1, source_target_pairs={{0,2},{1,3},{2,0},{3,1},{4,6},{5,7},{6,4},{7,5},{8,10},{9,11},{10,... | collective-permute-start | bytes 393224 | tf_op jit(solution)/shard_map/cond/branch_0_fun/ppermute | solution.py:402
  22.9 0.6 %collective-permute-start.5 = (bf16[128,512]{1,0:T(8,128)(2,1)S(1)}, bf16[128,512]{1,0:T(8,128)(2,1)S(1)}, u32[]{:S(2)}, u32[]{:S(2)}) collective-permute-start(bf16[128,512]{1,0:T(8,128)(2,1)S(1)} %project_far_0.2), channel_id=1, source_target_pairs={{0,2},{1,3},{2,0},{3,1},{4,6},{5,7},{6,4},{7,5},{8,10},{9,11},{10,... | collective-permute-start | bytes 393224 | tf_op jit(solution)/shard_map/cond/branch_0_fun/ppermute | solution.py:402
  23.5 1.6 %project_near.2.near_ref = f32[256,512]{1,0:T(8,128)S(1)} custom-call(bf16[256,512]{1,0:T(8,128)(2,1)} %get-tuple-element.48.residual_hbm, bf16[512,2048]{1,0:T(8,128)(2,1)} %get-tuple-element.49.weight_hbm, bf16[512,2048]{1,0:T(8,128)(2,1)S(1)} %get-tuple-element.50.other_weight_hbm, bf16[128,256]{1,0:T(8,128)(2,1)S(1)} %norm_mine_0.1.refs_0_, ...), custom_call_target="tpu_custom_call" | custom-call | tf_op jit(solution)/shard_map/cond/branch_0_fun/project_near/pallas_call | solution.py:405
  25.1 2.4 %collective-permute-done.6.refs_1_ = bf16[128,512]{1,0:T(8,128)(2,1)S(1)} collective-permute-done((bf16[128,512]{1,0:T(8,128)(2,1)S(1)}, bf16[128,512]{1,0:T(8,128)(2,1)S(1)}, u32[]{:S(2)}, u32[]{:S(2)}) %collective-permute-start.6) | collective-permute-done | bytes 131104 | tf_op jit(solution)/shard_map/cond/branch_0_fun/ppermute | solution.py:402
  27.5 2.0 %collective-permute-done.5.refs_0_ = bf16[128,512]{1,0:T(8,128)(2,1)S(1)} collective-permute-done((bf16[128,512]{1,0:T(8,128)(2,1)S(1)}, bf16[128,512]{1,0:T(8,128)(2,1)S(1)}, u32[]{:S(2)}, u32[]{:S(2)}) %collective-permute-start.5) | collective-permute-done | bytes 131104 | tf_op jit(solution)/shard_map/cond/branch_0_fun/ppermute | solution.py:402
  29.6 0.7 %add.2 = bf16[256,512]{1,0:T(8,128)(2,1)} custom-call(f32[256,512]{1,0:T(8,128)S(1)} %project_near.2.near_ref, bf16[128,512]{1,0:T(8,128)(2,1)S(1)} %collective-permute-done.5.refs_0_, bf16[128,512]{1,0:T(8,128)(2,1)S(1)} %collective-permute-done.6.refs_1_), custom_call_target="tpu_custom_call" | custom-call | tf_op jit(solution)/shard_map/cond/branch_0_fun/add/pallas_call | solution.py:421
  (18 shorter events, 2.3 us)
Async XLA Ops:
  0.0 14.8 %collective-permute-start.16 = (bf16[512,2048]{1,0:T(8,128)(2,1)}, bf16[512,2048]{1,0:T(8,128)(2,1)S(1)}, u32[]{:S(2)}, u32[]{:S(2)}) collective-permute-start(bf16[512,2048]{1,0:T(8,128)(2,1)} %param.15), channel_id=1, source_target_pairs={{0,1},{1,0},{2,3},{3,2},{4,5},{5,4},{6,7},{7,6},{8,9},{9,8},{10,11... | collective-permute-start | bytes 6291464 | tf_op jit(solution)/shard_map/ppermute | solution.py:336
  1.4 5.9 %collective-permute-start.11 = (bf16[272,128]{1,0:T(8,128)(2,1)S(1)}, bf16[272,128]{1,0:T(8,128)(2,1)S(1)}, u32[]{:S(2)}, u32[]{:S(2)}) collective-permute-start(bf16[272,128]{1,0:T(8,128)(2,1)S(1)} %get-tuple-element.96), channel_id=1, source_target_pairs={{0,12},{4,8},{8,4},{12,0},{16,28},{20,24},{24,20},{28,16},{1,13},{... | collective-permute-start | bytes 208904 | tf_op jit(solution)/shard_map/ppermute | solution.py:334
  2.9 5.6 %collective-permute-start.12 = (bf16[272,128]{1,0:T(8,128)(2,1)S(1)}, bf16[272,128]{1,0:T(8,128)(2,1)S(1)}, u32[]{:S(2)}, u32[]{:S(2)}) collective-permute-start(bf16[272,128]{1,0:T(8,128)(2,1)S(1)} %get-tuple-element.97.refs_3_), channel_id=1, source_target_pairs={{0,8},{4,12},{8,0},{12,4},{16,24},{20,28},{24,16},{28,20},{1,9},{5... | collective-permute-start | bytes 208904 | tf_op jit(solution)/shard_map/ppermute | solution.py:334
  4.4 4.3 %collective-permute-start.13 = (bf16[272,128]{1,0:T(8,128)(2,1)S(1)}, bf16[272,128]{1,0:T(8,128)(2,1)S(1)}, u32[]{:S(2)}, u32[]{:S(2)}) collective-permute-start(bf16[272,128]{1,0:T(8,128)(2,1)S(1)} %get-tuple-element.96), channel_id=1, source_target_pairs={{0,4},{4,0},{8,12},{12,8},{16,20},{20,16},{24,28},{28,24},{1,5},{5... | collective-permute-start | bytes 208904 | tf_op jit(solution)/shard_map/ppermute | solution.py:334
  8.9 5.9 %collective-permute-start.15 = (bf16[272,128]{1,0:T(8,128)(2,1)S(1)}, bf16[272,128]{1,0:T(8,128)(2,1)S(1)}, u32[]{:S(2)}, u32[]{:S(2)}) collective-permute-start(bf16[272,128]{1,0:T(8,128)(2,1)S(1)} %get-tuple-element.101), channel_id=1, source_target_pairs={{0,16},{4,20},{8,24},{12,28},{16,0},{20,4},{24,8},{28,12},{1,17},{... | collective-permute-start | bytes 208904 | tf_op jit(solution)/shard_map/ppermute | solution.py:297
  9.3 4.3 %collective-permute-start.14 = (bf16[256,128]{1,0:T(8,128)(2,1)S(1)}, bf16[256,128]{1,0:T(8,128)(2,1)S(1)}, u32[]{:S(2)}, u32[]{:S(2)}) collective-permute-start(bf16[256,128]{1,0:T(8,128)(2,1)S(1)} %get-tuple-element.100), channel_id=1, source_target_pairs={{0,4},{4,0},{8,12},{12,8},{16,20},{20,16},{24,28},{28,24},{1,5},{5... | collective-permute-start | bytes 196616 | tf_op jit(solution)/shard_map/ppermute | solution.py:334
  14.8 4.4 %collective-permute-start.1 = (bf16[272,128]{1,0:T(8,128)(2,1)S(1)}, bf16[272,128]{1,0:T(8,128)(2,1)S(1)}, u32[]{:S(2)}, u32[]{:S(2)}) collective-permute-start(bf16[272,128]{1,0:T(8,128)(2,1)S(1)} %get-tuple-element.58), channel_id=1, source_target_pairs={{0,4},{4,0},{8,12},{12,8},{16,20},{20,16},{24,28},{28,24},{1,5},{5... | collective-permute-start | bytes 208904 | tf_op jit(solution)/shard_map/cond/branch_0_fun/ppermute | solution.py:334
  16.9 2.0 %collective-permute-start.2 = (bf16[128,256]{1,0:T(8,128)(2,1)S(1)}, bf16[128,256]{1,0:T(8,128)(2,1)S(1)}, u32[]{:S(2)}, u32[]{:S(2)}) collective-permute-start(bf16[128,256]{1,0:T(8,128)(2,1)S(1)} %norm_mine_1.1._.refs_2_.refs_4_), channel_id=1, source_target_pairs={{0,1},{1,0},{2,3},{3,2},{4,5},{5,4},{6,7},{7,6},{8,9},{9,8},{10,11... | collective-permute-start | bytes 196616 | tf_op jit(solution)/shard_map/cond/branch_0_fun/ppermute | solution.py:384
  17.3 1.6 %collective-permute-start = (bf16[128,256]{1,0:T(8,128)(2,1)S(1)}, bf16[128,256]{1,0:T(8,128)(2,1)S(1)}, u32[]{:S(2)}, u32[]{:S(2)}) collective-permute-start(bf16[128,256]{1,0:T(8,128)(2,1)S(1)} %norm_mine_0.1.refs_0_), channel_id=1, source_target_pairs={{0,1},{1,0},{2,3},{3,2},{4,5},{5,4},{6,7},{7,6},{8,9},{9,8},{10,11... | collective-permute-start | bytes 196616 | tf_op jit(solution)/shard_map/cond/branch_0_fun/ppermute | solution.py:384
  19.6 1.3 %collective-permute-start.4 = (bf16[128,256]{1,0:T(8,128)(2,1)S(1)}, bf16[128,256]{1,0:T(8,128)(2,1)S(1)}, u32[]{:S(2)}, u32[]{:S(2)}) collective-permute-start(bf16[128,256]{1,0:T(8,128)(2,1)S(1)} %norm_1.2.refs_6_.mine_ref), channel_id=1, source_target_pairs={{0,1},{1,0},{2,3},{3,2},{4,5},{5,4},{6,7},{7,6},{8,9},{9,8},{10,11... | collective-permute-start | bytes 196616 | tf_op jit(solution)/shard_map/cond/branch_0_fun/ppermute | solution.py:384
  20.1 2.6 %collective-permute-start.3 = (bf16[128,256]{1,0:T(8,128)(2,1)S(1)}, bf16[128,256]{1,0:T(8,128)(2,1)S(1)}, u32[]{:S(2)}, u32[]{:S(2)}) collective-permute-start(bf16[128,256]{1,0:T(8,128)(2,1)S(1)} %norm_0.2.refs_2_.mine_ref), channel_id=1, source_target_pairs={{0,1},{1,0},{2,3},{3,2},{4,5},{5,4},{6,7},{7,6},{8,9},{9,8},{10,11... | collective-permute-start | bytes 196616 | tf_op jit(solution)/shard_map/cond/branch_0_fun/ppermute | solution.py:384
  21.1 6.4 %collective-permute-start.6 = (bf16[128,512]{1,0:T(8,128)(2,1)S(1)}, bf16[128,512]{1,0:T(8,128)(2,1)S(1)}, u32[]{:S(2)}, u32[]{:S(2)}) collective-permute-start(bf16[128,512]{1,0:T(8,128)(2,1)S(1)} %project_far_1.2), channel_id=1, source_target_pairs={{0,2},{1,3},{2,0},{3,1},{4,6},{5,7},{6,4},{7,5},{8,10},{9,11},{10,... | collective-permute-start | bytes 393224 | tf_op jit(solution)/shard_map/cond/branch_0_fun/ppermute | solution.py:402
  22.9 6.6 %collective-permute-start.5 = (bf16[128,512]{1,0:T(8,128)(2,1)S(1)}, bf16[128,512]{1,0:T(8,128)(2,1)S(1)}, u32[]{:S(2)}, u32[]{:S(2)}) collective-permute-start(bf16[128,512]{1,0:T(8,128)(2,1)S(1)} %project_far_0.2), channel_id=1, source_target_pairs={{0,2},{1,3},{2,0},{3,1},{4,6},{5,7},{6,4},{7,5},{8,10},{9,11},{10,... | collective-permute-start | bytes 393224 | tf_op jit(solution)/shard_map/cond/branch_0_fun/ppermute | solution.py:402

commit v5 on v3

--- a/solution.py
+++ b/solution.py
@@ -86,9 +86,15 @@
 
 def state_kernel(half, *refs):
     sources, outs, held, sems = refs[:5], refs[5:7], refs[7:12], refs[12]
+    moves = [(sources[0], held[0])]
+    for i in (1, 2):
+        middle = sources[i].shape[0] // 2
+        for rows in (slice(0, middle), slice(middle, 2 * middle)):
+            moves.append((sources[i].at[rows, :], held[i].at[rows, :]))
+    moves += list(zip(sources[3:], held[3:]))
     copies = [
         pltpu.make_async_copy(source, target, sems.at[i])
-        for i, (source, target) in enumerate(zip(sources, held))
+        for i, (source, target) in enumerate(moves)
     ]
     for copy in copies:
         copy.start()
@@ -100,8 +106,8 @@
     decays = decay_ref[...]
     tail = jnp.exp(sums_across(later, decays))
     whole = jnp.exp(jnp.sum(decays, axis=1, keepdims=True))
-    copies[1].wait()
-    copies[2].wait()
+    for copy in copies[1:5]:
+        copy.wait()
     decay_rows = decays_to_rows([whole[h : h + 1] for h in range(2 * half)])
     for owner, out_ref in zip((1 - me, me), outs):
         factors = pick(owner, tail, 0)
@@ -111,7 +117,7 @@
             update = jnp.dot(weighted, value_ref[:, at], preferred_element_type=F32)
             out_ref[state_rows(j), :] = update.astype(BF16)
         out_ref[half * HEAD_DIM :, :] = decay_rows
-    for copy in copies[3:]:
+    for copy in copies[5:]:
         copy.wait()
 
 
@@ -218,8 +224,11 @@
     copies = []
     for i, (weight, ref) in enumerate(zip(whole, held)):
         at = half_at(lax.axis_index("tp") ^ step, ref.shape[1])
-        copies.append(pltpu.make_async_copy(weight.at[:, at], ref, sems.at[i]))
-        copies[i].start()
+        middle = ref.shape[0] // 2
+        for j, rows in enumerate((slice(0, middle), slice(middle, 2 * middle))):
+            source = weight.at[rows, at]
+            copies.append(pltpu.make_async_copy(source, ref.at[rows, :], sems.at[2 * i + j]))
+            copies[-1].start()
     return copies
 
 
@@ -247,8 +256,8 @@
 def near_kernel(chunks, passes, residual_hbm, weight_hbm, other_weight_hbm, *refs):
     out_ref, residual_ref, *weights, sems = refs[-5:]
     copies = fetch(0, (weight_hbm, other_weight_hbm), weights, sems)
-    copies.append(pltpu.make_async_copy(residual_hbm, residual_ref, sems.at[2]))
-    copies[2].start()
+    copies.append(pltpu.make_async_copy(residual_hbm, residual_ref, sems.at[4]))
+    copies[4].start()
     for copy in copies:
         copy.wait()
     pairs = iter(zip(refs[0:-5:2], refs[1:-5:2]))
@@ -341,7 +350,7 @@
         (message, message) + tuple(shape(a.shape, a.dtype) for a in arguments),
         [HBM] * 5,
         "states",
-        scratch=[pltpu.SemaphoreType.DMA((5,))],
+        scratch=[pltpu.SemaphoreType.DMA((7,))],
     )(*(pltpu.with_memory_space_constraint(a, pltpu.HBM) for a in arguments))
     steps = (3, 1, 2, 0)
     received = [swap(theirs, 3), swap(theirs, 1), swap(mine, 2), mine]
@@ -389,7 +398,7 @@
             (shape(block, BF16),) * 2,
             weight_specs + [VMEM],
             "fetch_far",
-            scratch=[pltpu.SemaphoreType.DMA((2,))],
+            scratch=[pltpu.SemaphoreType.DMA((4,))],
         )(*weights, after)
 
     def send_far(i, kernel, *operands):
@@ -411,7 +420,7 @@
                 pltpu.VMEM(residual.shape, BF16),
                 pltpu.VMEM(block, BF16),
                 pltpu.VMEM(block, BF16),
-                pltpu.SemaphoreType.DMA((3,)),
+                pltpu.SemaphoreType.DMA((5,)),
             ],
         )(
             pltpu.with_memory_space_constraint(residual, pltpu.HBM),

time: 30.4 us -> 30.4 us (level)
  no operation moved by 1% of the time
where the time goes in v5:
time: 30.4 us; the launch traced here: 30.3 us
  waiting for transfers between devices  13.2 us (43%)
  starting transfers between devices  9.22 us (30%)
  Pallas kernels  7.69 us (25%)
    ppermute x5, waiting for transfers between devices, swap(): return lax.ppermute(piece, 'seq', [(i, i ^ step) for i in range(devices)])  7.01 us
    ppermute x5, starting transfers between devices, swap(): return lax.ppermute(piece, 'seq', [(i, i ^ step) for i in range(devices)])  5.4 us
    ppermute x2, waiting for transfers between devices, send_far(): return lax.ppermute(part, 'tp', far_pairs)  4.42 us
    ppermute x2, starting transfers between devices, send_far(): return lax.ppermute(part, 'tp', far_pairs)  2.16 us
    pallas_call x1, Pallas kernels, finish(): call(functools.partial(near_kernel, chunks, passes), shape((tokens, out_w...  1.61 us
    pallas_call x1, Pallas kernels, on_device(): call(functools.partial(state_kernel, half), (message, message) + tuple((s...  1.46 us
    ppermute x1, waiting for transfers between devices, earlier_groups(): lax.ppermute(total, 'seq', [(i, i ^ MEMBERS) for i in range(devices)])  1.35 us
    ppermute x4, starting transfers between devices, normed(): return (part, lax.ppermute(part, 'tp', near_pairs))  1.26 us
  transfers between devices with their start and end apart: 13, of which 9 were waited for; matrix products, arithmetic and copies ran while one was open for 0% of the time, Pallas kernels for 22%

profile of v5, /device:TPU:24, one launch (start us, length us, event | category | flops | bytes accessed | tf_op | source)
XLA Modules:
  0.0 30.3 jit_solution(6012764462576998096)
XLA Ops:
  0.0 1.5 %states.1 = (bf16[272,128]{1,0:T(8,128)(2,1)S(1)}, bf16[272,128]{1,0:T(8,128)(2,1)S(1)}, f32[4,256]{1,0:T(4,128)S(1)}, bf16[256,512]{1,0:T(8,128)(2,1)S(1)}, bf1...) custom-call(f32[4,256]{1,0:T(4,128)} %refs_0_.1, bf16[256,512]{1,0:T(8,128)(2,1)} %refs_1_.1, ...), custom_call_target="tpu_custom_call" | custom-call | tf_op jit(solution)/shard_map/states/pallas_call | solution.py:348
  1.5 1.5 %collective-permute-start.11 = (bf16[272,128]{1,0:T(8,128)(2,1)S(1)}, bf16[272,128]{1,0:T(8,128)(2,1)S(1)}, u32[]{:S(2)}, u32[]{:S(2)}) collective-permute-start(bf16[272,128]{1,0:T(8,128)(2,1)S(1)} %get-tuple-element.96), channel_id=1, source_target_pairs={{0,12},{4,8},{8,4},{12,0},{16,28},{20,24},{24,20},{28,16},{1,13},{... | collective-permute-start | bytes 208904 | tf_op jit(solution)/shard_map/ppermute | solution.py:343
  2.9 0.5 %collective-permute-start.12 = (bf16[272,128]{1,0:T(8,128)(2,1)S(1)}, bf16[272,128]{1,0:T(8,128)(2,1)S(1)}, u32[]{:S(2)}, u32[]{:S(2)}) collective-permute-start(bf16[272,128]{1,0:T(8,128)(2,1)S(1)} %get-tuple-element.96), channel_id=1, source_target_pairs={{0,4},{4,0},{8,12},{12,8},{16,20},{20,16},{24,28},{28,24},{1,5},{5... | collective-permute-start | bytes 208904 | tf_op jit(solution)/shard_map/ppermute | solution.py:343
  3.4 1.6 %collective-permute-start.13 = (bf16[272,128]{1,0:T(8,128)(2,1)S(1)}, bf16[272,128]{1,0:T(8,128)(2,1)S(1)}, u32[]{:S(2)}, u32[]{:S(2)}) collective-permute-start(bf16[272,128]{1,0:T(8,128)(2,1)S(1)} %get-tuple-element.97.refs_3_), channel_id=1, source_target_pairs={{0,8},{4,12},{8,0},{12,4},{16,24},{20,28},{24,16},{28,20},{1,9},{5... | collective-permute-start | bytes 208904 | tf_op jit(solution)/shard_map/ppermute | solution.py:343
  5.0 2.1 %collective-permute-done.11.refs_0_ = bf16[272,128]{1,0:T(8,128)(2,1)S(1)} collective-permute-done((bf16[272,128]{1,0:T(8,128)(2,1)S(1)}, bf16[272,128]{1,0:T(8,128)(2,1)S(1)}, u32[]{:S(2)}, u32[]{:S(2)}) %collective-permute-start.11) | collective-permute-done | bytes 69664 | tf_op jit(solution)/shard_map/ppermute | solution.py:343
  7.1 1.4 %collective-permute-done.12.refs_1_ = bf16[272,128]{1,0:T(8,128)(2,1)S(1)} collective-permute-done((bf16[272,128]{1,0:T(8,128)(2,1)S(1)}, bf16[272,128]{1,0:T(8,128)(2,1)S(1)}, u32[]{:S(2)}, u32[]{:S(2)}) %collective-permute-start.12) | collective-permute-done | bytes 69664 | tf_op jit(solution)/shard_map/ppermute | solution.py:343
  8.7 0.4 %collective-permute-start.15 = (bf16[272,128]{1,0:T(8,128)(2,1)S(1)}, bf16[272,128]{1,0:T(8,128)(2,1)S(1)}, u32[]{:S(2)}, u32[]{:S(2)}) collective-permute-start(bf16[272,128]{1,0:T(8,128)(2,1)S(1)} %get-tuple-element.101), channel_id=1, source_target_pairs={{0,16},{4,20},{8,24},{12,28},{16,0},{20,4},{24,8},{28,12},{1,17},{... | collective-permute-start | bytes 208904 | tf_op jit(solution)/shard_map/ppermute | solution.py:306
  9.1 0.7 %collective-permute-start.14 = (bf16[256,128]{1,0:T(8,128)(2,1)S(1)}, bf16[256,128]{1,0:T(8,128)(2,1)S(1)}, u32[]{:S(2)}, u32[]{:S(2)}) collective-permute-start(bf16[256,128]{1,0:T(8,128)(2,1)S(1)} %get-tuple-element.100), channel_id=1, source_target_pairs={{0,4},{4,0},{8,12},{12,8},{16,20},{20,16},{24,28},{28,24},{1,5},{5... | collective-permute-start | bytes 196616 | tf_op jit(solution)/shard_map/ppermute | solution.py:343
  9.8 0.7 %local.1 = (f32[256,512]{1,0:T(8,128)S(1)}, f32[256,4]{1,0:T(8,128)S(1)}) custom-call(f32[4,256]{1,0:T(4,128)S(1)} %get-tuple-element.90.decay_ref, bf16[256,512]{1,0:T(8,128)(2,1)S(1)} %get-tuple-element.89.query_ref, bf16[256,512]{1,0:T(8,128)(2,1)S(1)} %get-tuple-element.91.key_ref, bf16[256,512]{1,0:T(8,128)(2,1)S(1)} %get-tuple-element.92.value_ref), custom_call_target="tpu_custom_call" | custom-call | flops 134217728 | bytes 2000000 | tf_op jit(solution)/shard_map/local/pallas_call | solution.py:367
  10.5 2.9 %collective-permute-done.14.inside_ref = bf16[256,128]{1,0:T(8,128)(2,1)S(1)} collective-permute-done((bf16[256,128]{1,0:T(8,128)(2,1)S(1)}, bf16[256,128]{1,0:T(8,128)(2,1)S(1)}, u32[]{:S(2)}, u32[]{:S(2)}) %collective-permute-start.14) | collective-permute-done | bytes 65568 | tf_op jit(solution)/shard_map/ppermute | solution.py:343
  13.4 1.4 %collective-permute-done.15.earlier_ref = bf16[272,128]{1,0:T(8,128)(2,1)S(1)} collective-permute-done((bf16[272,128]{1,0:T(8,128)(2,1)S(1)}, bf16[272,128]{1,0:T(8,128)(2,1)S(1)}, u32[]{:S(2)}, u32[]{:S(2)}) %collective-permute-start.15) | collective-permute-done | bytes 69664 | tf_op jit(solution)/shard_map/ppermute | solution.py:306
  14.8 15.4 %conditional.1 = (bf16[256,512]{1,0:T(8,128)(2,1)}) conditional(s32[]{:T(128)} %convert_element_type.3, (bf16[256,512]{1,0:T(8,128)(2,1)S(1)}, f32[256,512]{1,0:T(8,128)S(1)}, f32[256,4]{1,0:T(8,128)S(1)}, f32[1,512]{1,0:T(1,128)S(1)}, bf16[256,128]{1,0:T(8,128)(2,1)S(1)}, /*index=5*/bf16[272,128]{1,0:T(8,128)(2,1)S(1)}, bf16[512,2048]{1,0:T(8,128)(2,1)}, ...), branch_computations={%region_0.0_spmd, %region_1.0_spmd} | conditional | bytes 2375968 | solution.py:470
  14.8 1.2 %collective-permute-start.1 = (bf16[272,128]{1,0:T(8,128)(2,1)S(1)}, bf16[272,128]{1,0:T(8,128)(2,1)S(1)}, u32[]{:S(2)}, u32[]{:S(2)}) collective-permute-start(bf16[272,128]{1,0:T(8,128)(2,1)S(1)} %get-tuple-element.58), channel_id=1, source_target_pairs={{0,4},{4,0},{8,12},{12,8},{16,20},{20,16},{24,28},{28,24},{1,5},{5... | collective-permute-start | bytes 208904 | tf_op jit(solution)/shard_map/cond/branch_0_fun/ppermute | solution.py:343
  16.7 0.6 %collective-permute-start = (bf16[128,256]{1,0:T(8,128)(2,1)S(1)}, bf16[128,256]{1,0:T(8,128)(2,1)S(1)}, u32[]{:S(2)}, u32[]{:S(2)}) collective-permute-start(bf16[128,256]{1,0:T(8,128)(2,1)S(1)} %norm_mine_0.1.refs_0_), channel_id=1, source_target_pairs={{0,1},{1,0},{2,3},{3,2},{4,5},{5,4},{6,7},{7,6},{8,9},{9,8},{10,11... | collective-permute-start | bytes 196616 | tf_op jit(solution)/shard_map/cond/branch_0_fun/ppermute | solution.py:393
  17.2 1.1 %fetch_far.2 = (bf16[512,512]{1,0:T(8,128)(2,1)S(1)}, bf16[512,512]{1,0:T(8,128)(2,1)S(1)}) custom-call(bf16[512,2048]{1,0:T(8,128)(2,1)} %get-tuple-element.49.weight_hbm, bf16[512,2048]{1,0:T(8,128)(2,1)S(1)} %get-tuple-element.50.other_weight_hbm, bf16[128,256]{1,0:T(8,128)(2,1)S(1)} %norm_mine_1.1._.refs_2_.refs_4_), custom_call_target="tpu_custom_call" | custom-call | tf_op jit(solution)/shard_map/cond/branch_0_fun/fetch_far/pallas_call | solution.py:396
  18.7 0.5 %collective-permute-done.1.earlier_ref = bf16[272,128]{1,0:T(8,128)(2,1)S(1)} collective-permute-done((bf16[272,128]{1,0:T(8,128)(2,1)S(1)}, bf16[272,128]{1,0:T(8,128)(2,1)S(1)}, u32[]{:S(2)}, u32[]{:S(2)}) %collective-permute-start.1) | collective-permute-done | bytes 69664 | tf_op jit(solution)/shard_map/cond/branch_0_fun/ppermute | solution.py:343
  19.9 0.6 %collective-permute-start.3 = (bf16[128,256]{1,0:T(8,128)(2,1)S(1)}, bf16[128,256]{1,0:T(8,128)(2,1)S(1)}, u32[]{:S(2)}, u32[]{:S(2)}) collective-permute-start(bf16[128,256]{1,0:T(8,128)(2,1)S(1)} %norm_0.2.refs_2_.mine_ref), channel_id=1, source_target_pairs={{0,1},{1,0},{2,3},{3,2},{4,5},{5,4},{6,7},{7,6},{8,9},{9,8},{10,11... | collective-permute-start | bytes 196616 | tf_op jit(solution)/shard_map/cond/branch_0_fun/ppermute | solution.py:393
  20.5 0.4 %collective-permute-done.4.refs_7_.other_ref = bf16[128,256]{1,0:T(8,128)(2,1)S(1)} collective-permute-done((bf16[128,256]{1,0:T(8,128)(2,1)S(1)}, bf16[128,256]{1,0:T(8,128)(2,1)S(1)}, u32[]{:S(2)}, u32[]{:S(2)}) %collective-permute-start.4) | collective-permute-done | bytes 65568 | tf_op jit(solution)/shard_map/cond/branch_0_fun/ppermute | solution.py:393
  21.1 1.6 %collective-permute-start.6 = (bf16[128,512]{1,0:T(8,128)(2,1)S(1)}, bf16[128,512]{1,0:T(8,128)(2,1)S(1)}, u32[]{:S(2)}, u32[]{:S(2)}) collective-permute-start(bf16[128,512]{1,0:T(8,128)(2,1)S(1)} %project_far_1.2), channel_id=1, source_target_pairs={{0,2},{1,3},{2,0},{3,1},{4,6},{5,7},{6,4},{7,5},{8,10},{9,11},{10,... | collective-permute-start | bytes 393224 | tf_op jit(solution)/shard_map/cond/branch_0_fun/ppermute | solution.py:411
  22.9 0.6 %collective-permute-start.5 = (bf16[128,512]{1,0:T(8,128)(2,1)S(1)}, bf16[128,512]{1,0:T(8,128)(2,1)S(1)}, u32[]{:S(2)}, u32[]{:S(2)}) collective-permute-start(bf16[128,512]{1,0:T(8,128)(2,1)S(1)} %project_far_0.2), channel_id=1, source_target_pairs={{0,2},{1,3},{2,0},{3,1},{4,6},{5,7},{6,4},{7,5},{8,10},{9,11},{10,... | collective-permute-start | bytes 393224 | tf_op jit(solution)/shard_map/cond/branch_0_fun/ppermute | solution.py:411
  23.5 1.6 %project_near.2.near_ref = f32[256,512]{1,0:T(8,128)S(1)} custom-call(bf16[256,512]{1,0:T(8,128)(2,1)} %get-tuple-element.48.residual_hbm, bf16[512,2048]{1,0:T(8,128)(2,1)} %get-tuple-element.49.weight_hbm, bf16[512,2048]{1,0:T(8,128)(2,1)S(1)} %get-tuple-element.50.other_weight_hbm, bf16[128,256]{1,0:T(8,128)(2,1)S(1)} %norm_mine_0.1.refs_0_, ...), custom_call_target="tpu_custom_call" | custom-call | tf_op jit(solution)/shard_map/cond/branch_0_fun/project_near/pallas_call | solution.py:414
  25.1 2.4 %collective-permute-done.6.refs_1_ = bf16[128,512]{1,0:T(8,128)(2,1)S(1)} collective-permute-done((bf16[128,512]{1,0:T(8,128)(2,1)S(1)}, bf16[128,512]{1,0:T(8,128)(2,1)S(1)}, u32[]{:S(2)}, u32[]{:S(2)}) %collective-permute-start.6) | collective-permute-done | bytes 131104 | tf_op jit(solution)/shard_map/cond/branch_0_fun/ppermute | solution.py:411
  27.5 2.0 %collective-permute-done.5.refs_0_ = bf16[128,512]{1,0:T(8,128)(2,1)S(1)} collective-permute-done((bf16[128,512]{1,0:T(8,128)(2,1)S(1)}, bf16[128,512]{1,0:T(8,128)(2,1)S(1)}, u32[]{:S(2)}, u32[]{:S(2)}) %collective-permute-start.5) | collective-permute-done | bytes 131104 | tf_op jit(solution)/shard_map/cond/branch_0_fun/ppermute | solution.py:411
  29.5 0.7 %add.2 = bf16[256,512]{1,0:T(8,128)(2,1)} custom-call(f32[256,512]{1,0:T(8,128)S(1)} %project_near.2.near_ref, bf16[128,512]{1,0:T(8,128)(2,1)S(1)} %collective-permute-done.5.refs_0_, bf16[128,512]{1,0:T(8,128)(2,1)S(1)} %collective-permute-done.6.refs_1_), custom_call_target="tpu_custom_call" | custom-call | tf_op jit(solution)/shard_map/cond/branch_0_fun/add/pallas_call | solution.py:430
  (18 shorter events, 2.4 us)
Async XLA Ops:
  0.0 14.8 %collective-permute-start.16 = (bf16[512,2048]{1,0:T(8,128)(2,1)}, bf16[512,2048]{1,0:T(8,128)(2,1)S(1)}, u32[]{:S(2)}, u32[]{:S(2)}) collective-permute-start(bf16[512,2048]{1,0:T(8,128)(2,1)} %param.15), channel_id=1, source_target_pairs={{0,1},{1,0},{2,3},{3,2},{4,5},{5,4},{6,7},{7,6},{8,9},{9,8},{10,11... | collective-permute-start | bytes 6291464 | tf_op jit(solution)/shard_map/ppermute | solution.py:345
  1.5 5.7 %collective-permute-start.11 = (bf16[272,128]{1,0:T(8,128)(2,1)S(1)}, bf16[272,128]{1,0:T(8,128)(2,1)S(1)}, u32[]{:S(2)}, u32[]{:S(2)}) collective-permute-start(bf16[272,128]{1,0:T(8,128)(2,1)S(1)} %get-tuple-element.96), channel_id=1, source_target_pairs={{0,12},{4,8},{8,4},{12,0},{16,28},{20,24},{24,20},{28,16},{1,13},{... | collective-permute-start | bytes 208904 | tf_op jit(solution)/shard_map/ppermute | solution.py:343
  2.9 5.6 %collective-permute-start.12 = (bf16[272,128]{1,0:T(8,128)(2,1)S(1)}, bf16[272,128]{1,0:T(8,128)(2,1)S(1)}, u32[]{:S(2)}, u32[]{:S(2)}) collective-permute-start(bf16[272,128]{1,0:T(8,128)(2,1)S(1)} %get-tuple-element.96), channel_id=1, source_target_pairs={{0,4},{4,0},{8,12},{12,8},{16,20},{20,16},{24,28},{28,24},{1,5},{5... | collective-permute-start | bytes 208904 | tf_op jit(solution)/shard_map/ppermute | solution.py:343
  3.4 5.2 %collective-permute-start.13 = (bf16[272,128]{1,0:T(8,128)(2,1)S(1)}, bf16[272,128]{1,0:T(8,128)(2,1)S(1)}, u32[]{:S(2)}, u32[]{:S(2)}) collective-permute-start(bf16[272,128]{1,0:T(8,128)(2,1)S(1)} %get-tuple-element.97.refs_3_), channel_id=1, source_target_pairs={{0,8},{4,12},{8,0},{12,4},{16,24},{20,28},{24,16},{28,20},{1,9},{5... | collective-permute-start | bytes 208904 | tf_op jit(solution)/shard_map/ppermute | solution.py:343
  8.7 6.0 %collective-permute-start.15 = (bf16[272,128]{1,0:T(8,128)(2,1)S(1)}, bf16[272,128]{1,0:T(8,128)(2,1)S(1)}, u32[]{:S(2)}, u32[]{:S(2)}) collective-permute-start(bf16[272,128]{1,0:T(8,128)(2,1)S(1)} %get-tuple-element.101), channel_id=1, source_target_pairs={{0,16},{4,20},{8,24},{12,28},{16,0},{20,4},{24,8},{28,12},{1,17},{... | collective-permute-start | bytes 208904 | tf_op jit(solution)/shard_map/ppermute | solution.py:306
  9.1 4.3 %collective-permute-start.14 = (bf16[256,128]{1,0:T(8,128)(2,1)S(1)}, bf16[256,128]{1,0:T(8,128)(2,1)S(1)}, u32[]{:S(2)}, u32[]{:S(2)}) collective-permute-start(bf16[256,128]{1,0:T(8,128)(2,1)S(1)} %get-tuple-element.100), channel_id=1, source_target_pairs={{0,4},{4,0},{8,12},{12,8},{16,20},{20,16},{24,28},{28,24},{1,5},{5... | collective-permute-start | bytes 196616 | tf_op jit(solution)/shard_map/ppermute | solution.py:343
  14.8 4.4 %collective-permute-start.1 = (bf16[272,128]{1,0:T(8,128)(2,1)S(1)}, bf16[272,128]{1,0:T(8,128)(2,1)S(1)}, u32[]{:S(2)}, u32[]{:S(2)}) collective-permute-start(bf16[272,128]{1,0:T(8,128)(2,1)S(1)} %get-tuple-element.58), channel_id=1, source_target_pairs={{0,4},{4,0},{8,12},{12,8},{16,20},{20,16},{24,28},{28,24},{1,5},{5... | collective-permute-start | bytes 208904 | tf_op jit(solution)/shard_map/cond/branch_0_fun/ppermute | solution.py:343
  16.3 2.0 %collective-permute-start.2 = (bf16[128,256]{1,0:T(8,128)(2,1)S(1)}, bf16[128,256]{1,0:T(8,128)(2,1)S(1)}, u32[]{:S(2)}, u32[]{:S(2)}) collective-permute-start(bf16[128,256]{1,0:T(8,128)(2,1)S(1)} %norm_mine_1.1._.refs_2_.refs_4_), channel_id=1, source_target_pairs={{0,1},{1,0},{2,3},{3,2},{4,5},{5,4},{6,7},{7,6},{8,9},{9,8},{10,11... | collective-permute-start | bytes 196616 | tf_op jit(solution)/shard_map/cond/branch_0_fun/ppermute | solution.py:393
  16.7 1.6 %collective-permute-start = (bf16[128,256]{1,0:T(8,128)(2,1)S(1)}, bf16[128,256]{1,0:T(8,128)(2,1)S(1)}, u32[]{:S(2)}, u32[]{:S(2)}) collective-permute-start(bf16[128,256]{1,0:T(8,128)(2,1)S(1)} %norm_mine_0.1.refs_0_), channel_id=1, source_target_pairs={{0,1},{1,0},{2,3},{3,2},{4,5},{5,4},{6,7},{7,6},{8,9},{9,8},{10,11... | collective-permute-start | bytes 196616 | tf_op jit(solution)/shard_map/cond/branch_0_fun/ppermute | solution.py:393
  19.5 1.3 %collective-permute-start.4 = (bf16[128,256]{1,0:T(8,128)(2,1)S(1)}, bf16[128,256]{1,0:T(8,128)(2,1)S(1)}, u32[]{:S(2)}, u32[]{:S(2)}) collective-permute-start(bf16[128,256]{1,0:T(8,128)(2,1)S(1)} %norm_1.2.refs_6_.mine_ref), channel_id=1, source_target_pairs={{0,1},{1,0},{2,3},{3,2},{4,5},{5,4},{6,7},{7,6},{8,9},{9,8},{10,11... | collective-permute-start | bytes 196616 | tf_op jit(solution)/shard_map/cond/branch_0_fun/ppermute | solution.py:393
  19.9 2.7 %collective-permute-start.3 = (bf16[128,256]{1,0:T(8,128)(2,1)S(1)}, bf16[128,256]{1,0:T(8,128)(2,1)S(1)}, u32[]{:S(2)}, u32[]{:S(2)}) collective-permute-start(bf16[128,256]{1,0:T(8,128)(2,1)S(1)} %norm_0.2.refs_2_.mine_ref), channel_id=1, source_target_pairs={{0,1},{1,0},{2,3},{3,2},{4,5},{5,4},{6,7},{7,6},{8,9},{9,8},{10,11... | collective-permute-start | bytes 196616 | tf_op jit(solution)/shard_map/cond/branch_0_fun/ppermute | solution.py:393
  21.1 6.4 %collective-permute-start.6 = (bf16[128,512]{1,0:T(8,128)(2,1)S(1)}, bf16[128,512]{1,0:T(8,128)(2,1)S(1)}, u32[]{:S(2)}, u32[]{:S(2)}) collective-permute-start(bf16[128,512]{1,0:T(8,128)(2,1)S(1)} %project_far_1.2), channel_id=1, source_target_pairs={{0,2},{1,3},{2,0},{3,1},{4,6},{5,7},{6,4},{7,5},{8,10},{9,11},{10,... | collective-permute-start | bytes 393224 | tf_op jit(solution)/shard_map/cond/branch_0_fun/ppermute | solution.py:411
  22.9 6.6 %collective-permute-start.5 = (bf16[128,512]{1,0:T(8,128)(2,1)S(1)}, bf16[128,512]{1,0:T(8,128)(2,1)S(1)}, u32[]{:S(2)}, u32[]{:S(2)}) collective-permute-start(bf16[128,512]{1,0:T(8,128)(2,1)S(1)} %project_far_0.2), channel_id=1, source_target_pairs={{0,2},{1,3},{2,0},{3,1},{4,6},{5,7},{6,4},{7,5},{8,10},{9,11},{10,... | collective-permute-start | bytes 393224 | tf_op jit(solution)/shard_map/cond/branch_0_fun/ppermute | solution.py:411

commit v6 on v3

--- a/solution.py
+++ b/solution.py
@@ -224,7 +224,7 @@
 
 
 def fetch_kernel(weight_hbm, other_weight_hbm, _, weight_ref, other_weight_ref, sems):
-    for copy in fetch(2, (weight_hbm, other_weight_hbm), (weight_ref, other_weight_ref), sems):
+    for copy in fetch(3, (weight_hbm, other_weight_hbm), (weight_ref, other_weight_ref), sems):
         copy.wait()
 
 
@@ -326,7 +326,7 @@
     out_width = out_weight.shape[1] // tp
     states = (half * HEAD_DIM, HEAD_DIM)
     near_pairs = [(i, i ^ 1) for i in range(tp)]
-    far_pairs = [(i, i ^ 2) for i in range(tp)]
+    far_pairs = [(i, i ^ 3) for i in range(tp)]
     shape = jax.ShapeDtypeStruct
     message = shape((half * HEAD_DIM + DECAY_ROWS, HEAD_DIM), BF16)
 

time: 30.4 us -> 30.6 us (level)
  no operation moved by 1% of the time
where the time goes in v6:
time: 30.6 us; the launch traced here: 30.1 us
  waiting for transfers between devices  13.4 us (44%)
  starting transfers between devices  8.94 us (29%)
  Pallas kernels  7.59 us (25%)
    ppermute x5, waiting for transfers between devices, swap(): return lax.ppermute(piece, 'seq', [(i, i ^ step) for i in range(devices)])  7.03 us
    ppermute x5, starting transfers between devices, swap(): return lax.ppermute(piece, 'seq', [(i, i ^ step) for i in range(devices)])  5.4 us
    ppermute x2, waiting for transfers between devices, send_far(): return lax.ppermute(part, 'tp', far_pairs)  4.61 us
    ppermute x2, starting transfers between devices, send_far(): return lax.ppermute(part, 'tp', far_pairs)  1.88 us
    pallas_call x1, Pallas kernels, finish(): call(functools.partial(near_kernel, chunks, passes), shape((tokens, out_w...  1.6 us
    pallas_call x1, Pallas kernels, on_device(): call(functools.partial(state_kernel, half), (message, message) + tuple((s...  1.37 us
    ppermute x1, waiting for transfers between devices, earlier_groups(): lax.ppermute(total, 'seq', [(i, i ^ MEMBERS) for i in range(devices)])  1.35 us
    ppermute x4, starting transfers between devices, normed(): return (part, lax.ppermute(part, 'tp', near_pairs))  1.26 us
  transfers between devices with their start and end apart: 13, of which 9 were waited for; matrix products, arithmetic and copies ran while one was open for 0% of the time, Pallas kernels for 22%

profile of v6, /device:TPU:24, one launch (start us, length us, event | category | flops | bytes accessed | tf_op | source)
XLA Modules:
  0.0 30.1 jit_solution(1454752323171989743)
XLA Ops:
  0.0 1.4 %states.1 = (bf16[272,128]{1,0:T(8,128)(2,1)S(1)}, bf16[272,128]{1,0:T(8,128)(2,1)S(1)}, f32[4,256]{1,0:T(4,128)S(1)}, bf16[256,512]{1,0:T(8,128)(2,1)S(1)}, bf1...) custom-call(f32[4,256]{1,0:T(4,128)} %refs_0_.1, bf16[256,512]{1,0:T(8,128)(2,1)} %refs_1_.1, ...), custom_call_target="tpu_custom_call" | custom-call | tf_op jit(solution)/shard_map/states/pallas_call | solution.py:339
  1.4 1.5 %collective-permute-start.11 = (bf16[272,128]{1,0:T(8,128)(2,1)S(1)}, bf16[272,128]{1,0:T(8,128)(2,1)S(1)}, u32[]{:S(2)}, u32[]{:S(2)}) collective-permute-start(bf16[272,128]{1,0:T(8,128)(2,1)S(1)} %get-tuple-element.96), channel_id=1, source_target_pairs={{0,12},{4,8},{8,4},{12,0},{16,28},{20,24},{24,20},{28,16},{1,13},{... | collective-permute-start | bytes 208904 | tf_op jit(solution)/shard_map/ppermute | solution.py:334
  2.9 0.5 %collective-permute-start.12 = (bf16[272,128]{1,0:T(8,128)(2,1)S(1)}, bf16[272,128]{1,0:T(8,128)(2,1)S(1)}, u32[]{:S(2)}, u32[]{:S(2)}) collective-permute-start(bf16[272,128]{1,0:T(8,128)(2,1)S(1)} %get-tuple-element.96), channel_id=1, source_target_pairs={{0,4},{4,0},{8,12},{12,8},{16,20},{20,16},{24,28},{28,24},{1,5},{5... | collective-permute-start | bytes 208904 | tf_op jit(solution)/shard_map/ppermute | solution.py:334
  3.4 1.6 %collective-permute-start.13 = (bf16[272,128]{1,0:T(8,128)(2,1)S(1)}, bf16[272,128]{1,0:T(8,128)(2,1)S(1)}, u32[]{:S(2)}, u32[]{:S(2)}) collective-permute-start(bf16[272,128]{1,0:T(8,128)(2,1)S(1)} %get-tuple-element.97.refs_3_), channel_id=1, source_target_pairs={{0,8},{4,12},{8,0},{12,4},{16,24},{20,28},{24,16},{28,20},{1,9},{5... | collective-permute-start | bytes 208904 | tf_op jit(solution)/shard_map/ppermute | solution.py:334
  4.9 2.1 %collective-permute-done.11.refs_0_ = bf16[272,128]{1,0:T(8,128)(2,1)S(1)} collective-permute-done((bf16[272,128]{1,0:T(8,128)(2,1)S(1)}, bf16[272,128]{1,0:T(8,128)(2,1)S(1)}, u32[]{:S(2)}, u32[]{:S(2)}) %collective-permute-start.11) | collective-permute-done | bytes 69664 | tf_op jit(solution)/shard_map/ppermute | solution.py:334
  7.0 1.4 %collective-permute-done.12.refs_1_ = bf16[272,128]{1,0:T(8,128)(2,1)S(1)} collective-permute-done((bf16[272,128]{1,0:T(8,128)(2,1)S(1)}, bf16[272,128]{1,0:T(8,128)(2,1)S(1)}, u32[]{:S(2)}, u32[]{:S(2)}) %collective-permute-start.12) | collective-permute-done | bytes 69664 | tf_op jit(solution)/shard_map/ppermute | solution.py:334
  8.7 0.4 %collective-permute-start.15 = (bf16[272,128]{1,0:T(8,128)(2,1)S(1)}, bf16[272,128]{1,0:T(8,128)(2,1)S(1)}, u32[]{:S(2)}, u32[]{:S(2)}) collective-permute-start(bf16[272,128]{1,0:T(8,128)(2,1)S(1)} %get-tuple-element.101), channel_id=1, source_target_pairs={{0,16},{4,20},{8,24},{12,28},{16,0},{20,4},{24,8},{28,12},{1,17},{... | collective-permute-start | bytes 208904 | tf_op jit(solution)/shard_map/ppermute | solution.py:297
  9.1 0.7 %collective-permute-start.14 = (bf16[256,128]{1,0:T(8,128)(2,1)S(1)}, bf16[256,128]{1,0:T(8,128)(2,1)S(1)}, u32[]{:S(2)}, u32[]{:S(2)}) collective-permute-start(bf16[256,128]{1,0:T(8,128)(2,1)S(1)} %get-tuple-element.100), channel_id=1, source_target_pairs={{0,4},{4,0},{8,12},{12,8},{16,20},{20,16},{24,28},{28,24},{1,5},{5... | collective-permute-start | bytes 196616 | tf_op jit(solution)/shard_map/ppermute | solution.py:334
  9.7 0.7 %local.1 = (f32[256,512]{1,0:T(8,128)S(1)}, f32[256,4]{1,0:T(8,128)S(1)}) custom-call(f32[4,256]{1,0:T(4,128)S(1)} %get-tuple-element.90.decay_ref, bf16[256,512]{1,0:T(8,128)(2,1)S(1)} %get-tuple-element.89.query_ref, bf16[256,512]{1,0:T(8,128)(2,1)S(1)} %get-tuple-element.91.key_ref, bf16[256,512]{1,0:T(8,128)(2,1)S(1)} %get-tuple-element.92.value_ref), custom_call_target="tpu_custom_call" | custom-call | flops 134217728 | bytes 2000000 | tf_op jit(solution)/shard_map/local/pallas_call | solution.py:358
  10.5 2.9 %collective-permute-done.14.inside_ref = bf16[256,128]{1,0:T(8,128)(2,1)S(1)} collective-permute-done((bf16[256,128]{1,0:T(8,128)(2,1)S(1)}, bf16[256,128]{1,0:T(8,128)(2,1)S(1)}, u32[]{:S(2)}, u32[]{:S(2)}) %collective-permute-start.14) | collective-permute-done | bytes 65568 | tf_op jit(solution)/shard_map/ppermute | solution.py:334
  13.3 1.4 %collective-permute-done.15.earlier_ref = bf16[272,128]{1,0:T(8,128)(2,1)S(1)} collective-permute-done((bf16[272,128]{1,0:T(8,128)(2,1)S(1)}, bf16[272,128]{1,0:T(8,128)(2,1)S(1)}, u32[]{:S(2)}, u32[]{:S(2)}) %collective-permute-start.15) | collective-permute-done | bytes 69664 | tf_op jit(solution)/shard_map/ppermute | solution.py:297
  14.7 15.3 %conditional.1 = (bf16[256,512]{1,0:T(8,128)(2,1)}) conditional(s32[]{:T(128)} %convert_element_type.3, (bf16[256,512]{1,0:T(8,128)(2,1)S(1)}, f32[256,512]{1,0:T(8,128)S(1)}, f32[256,4]{1,0:T(8,128)S(1)}, f32[1,512]{1,0:T(1,128)S(1)}, bf16[256,128]{1,0:T(8,128)(2,1)S(1)}, /*index=5*/bf16[272,128]{1,0:T(8,128)(2,1)S(1)}, bf16[512,2048]{1,0:T(8,128)(2,1)}, ...), branch_computations={%region_0.0_spmd, %region_1.0_spmd} | conditional | bytes 2375968 | solution.py:461
  14.7 1.2 %collective-permute-start.1 = (bf16[272,128]{1,0:T(8,128)(2,1)S(1)}, bf16[272,128]{1,0:T(8,128)(2,1)S(1)}, u32[]{:S(2)}, u32[]{:S(2)}) collective-permute-start(bf16[272,128]{1,0:T(8,128)(2,1)S(1)} %get-tuple-element.58), channel_id=1, source_target_pairs={{0,4},{4,0},{8,12},{12,8},{16,20},{20,16},{24,28},{28,24},{1,5},{5... | collective-permute-start | bytes 208904 | tf_op jit(solution)/shard_map/cond/branch_0_fun/ppermute | solution.py:334
  16.6 0.6 %collective-permute-start = (bf16[128,256]{1,0:T(8,128)(2,1)S(1)}, bf16[128,256]{1,0:T(8,128)(2,1)S(1)}, u32[]{:S(2)}, u32[]{:S(2)}) collective-permute-start(bf16[128,256]{1,0:T(8,128)(2,1)S(1)} %norm_mine_0.1.refs_0_), channel_id=1, source_target_pairs={{0,1},{1,0},{2,3},{3,2},{4,5},{5,4},{6,7},{7,6},{8,9},{9,8},{10,11... | collective-permute-start | bytes 196616 | tf_op jit(solution)/shard_map/cond/branch_0_fun/ppermute | solution.py:384
  17.1 1.1 %fetch_far.2 = (bf16[512,512]{1,0:T(8,128)(2,1)S(1)}, bf16[512,512]{1,0:T(8,128)(2,1)S(1)}) custom-call(bf16[512,2048]{1,0:T(8,128)(2,1)} %get-tuple-element.49.weight_hbm, bf16[512,2048]{1,0:T(8,128)(2,1)S(1)} %get-tuple-element.50.other_weight_hbm, bf16[128,256]{1,0:T(8,128)(2,1)S(1)} %norm_mine_1.1._.refs_2_.refs_4_), custom_call_target="tpu_custom_call" | custom-call | tf_op jit(solution)/shard_map/cond/branch_0_fun/fetch_far/pallas_call | solution.py:387
  18.6 0.6 %collective-permute-done.1.earlier_ref = bf16[272,128]{1,0:T(8,128)(2,1)S(1)} collective-permute-done((bf16[272,128]{1,0:T(8,128)(2,1)S(1)}, bf16[272,128]{1,0:T(8,128)(2,1)S(1)}, u32[]{:S(2)}, u32[]{:S(2)}) %collective-permute-start.1) | collective-permute-done | bytes 69664 | tf_op jit(solution)/shard_map/cond/branch_0_fun/ppermute | solution.py:334
  19.8 0.6 %collective-permute-start.3 = (bf16[128,256]{1,0:T(8,128)(2,1)S(1)}, bf16[128,256]{1,0:T(8,128)(2,1)S(1)}, u32[]{:S(2)}, u32[]{:S(2)}) collective-permute-start(bf16[128,256]{1,0:T(8,128)(2,1)S(1)} %norm_0.2.refs_2_.mine_ref), channel_id=1, source_target_pairs={{0,1},{1,0},{2,3},{3,2},{4,5},{5,4},{6,7},{7,6},{8,9},{9,8},{10,11... | collective-permute-start | bytes 196616 | tf_op jit(solution)/shard_map/cond/branch_0_fun/ppermute | solution.py:384
  20.4 0.4 %collective-permute-done.4.refs_7_.other_ref = bf16[128,256]{1,0:T(8,128)(2,1)S(1)} collective-permute-done((bf16[128,256]{1,0:T(8,128)(2,1)S(1)}, bf16[128,256]{1,0:T(8,128)(2,1)S(1)}, u32[]{:S(2)}, u32[]{:S(2)}) %collective-permute-start.4) | collective-permute-done | bytes 65568 | tf_op jit(solution)/shard_map/cond/branch_0_fun/ppermute | solution.py:384
  21.0 1.3 %collective-permute-start.6 = (bf16[128,512]{1,0:T(8,128)(2,1)S(1)}, bf16[128,512]{1,0:T(8,128)(2,1)S(1)}, u32[]{:S(2)}, u32[]{:S(2)}) collective-permute-start(bf16[128,512]{1,0:T(8,128)(2,1)S(1)} %project_far_1.2), channel_id=1, source_target_pairs={{0,3},{1,2},{2,1},{3,0},{4,7},{5,6},{6,5},{7,4},{8,11},{9,10},{10,... | collective-permute-start | bytes 393224 | tf_op jit(solution)/shard_map/cond/branch_0_fun/ppermute | solution.py:402
  22.5 0.6 %collective-permute-start.5 = (bf16[128,512]{1,0:T(8,128)(2,1)S(1)}, bf16[128,512]{1,0:T(8,128)(2,1)S(1)}, u32[]{:S(2)}, u32[]{:S(2)}) collective-permute-start(bf16[128,512]{1,0:T(8,128)(2,1)S(1)} %project_far_0.2), channel_id=1, source_target_pairs={{0,3},{1,2},{2,1},{3,0},{4,7},{5,6},{6,5},{7,4},{8,11},{9,10},{10,... | collective-permute-start | bytes 393224 | tf_op jit(solution)/shard_map/cond/branch_0_fun/ppermute | solution.py:402
  23.1 1.6 %project_near.2.near_ref = f32[256,512]{1,0:T(8,128)S(1)} custom-call(bf16[256,512]{1,0:T(8,128)(2,1)} %get-tuple-element.48.residual_hbm, bf16[512,2048]{1,0:T(8,128)(2,1)} %get-tuple-element.49.weight_hbm, bf16[512,2048]{1,0:T(8,128)(2,1)S(1)} %get-tuple-element.50.other_weight_hbm, bf16[128,256]{1,0:T(8,128)(2,1)S(1)} %norm_mine_0.1.refs_0_, ...), custom_call_target="tpu_custom_call" | custom-call | tf_op jit(solution)/shard_map/cond/branch_0_fun/project_near/pallas_call | solution.py:405
  24.7 1.8 %collective-permute-done.6.refs_1_ = bf16[128,512]{1,0:T(8,128)(2,1)S(1)} collective-permute-done((bf16[128,512]{1,0:T(8,128)(2,1)S(1)}, bf16[128,512]{1,0:T(8,128)(2,1)S(1)}, u32[]{:S(2)}, u32[]{:S(2)}) %collective-permute-start.6) | collective-permute-done | bytes 131104 | tf_op jit(solution)/shard_map/cond/branch_0_fun/ppermute | solution.py:402
  26.5 2.8 %collective-permute-done.5.refs_0_ = bf16[128,512]{1,0:T(8,128)(2,1)S(1)} collective-permute-done((bf16[128,512]{1,0:T(8,128)(2,1)S(1)}, bf16[128,512]{1,0:T(8,128)(2,1)S(1)}, u32[]{:S(2)}, u32[]{:S(2)}) %collective-permute-start.5) | collective-permute-done | bytes 131104 | tf_op jit(solution)/shard_map/cond/branch_0_fun/ppermute | solution.py:402
  29.3 0.7 %add.2 = bf16[256,512]{1,0:T(8,128)(2,1)} custom-call(f32[256,512]{1,0:T(8,128)S(1)} %project_near.2.near_ref, bf16[128,512]{1,0:T(8,128)(2,1)S(1)} %collective-permute-done.5.refs_0_, bf16[128,512]{1,0:T(8,128)(2,1)S(1)} %collective-permute-done.6.refs_1_), custom_call_target="tpu_custom_call" | custom-call | tf_op jit(solution)/shard_map/cond/branch_0_fun/add/pallas_call | solution.py:421
  (18 shorter events, 2.3 us)
Async XLA Ops:
  0.0 14.7 %collective-permute-start.16 = (bf16[512,2048]{1,0:T(8,128)(2,1)}, bf16[512,2048]{1,0:T(8,128)(2,1)S(1)}, u32[]{:S(2)}, u32[]{:S(2)}) collective-permute-start(bf16[512,2048]{1,0:T(8,128)(2,1)} %param.15), channel_id=1, source_target_pairs={{0,1},{1,0},{2,3},{3,2},{4,5},{5,4},{6,7},{7,6},{8,9},{9,8},{10,11... | collective-permute-start | bytes 6291464 | tf_op jit(solution)/shard_map/ppermute | solution.py:336
  1.4 5.7 %collective-permute-start.11 = (bf16[272,128]{1,0:T(8,128)(2,1)S(1)}, bf16[272,128]{1,0:T(8,128)(2,1)S(1)}, u32[]{:S(2)}, u32[]{:S(2)}) collective-permute-start(bf16[272,128]{1,0:T(8,128)(2,1)S(1)} %get-tuple-element.96), channel_id=1, source_target_pairs={{0,12},{4,8},{8,4},{12,0},{16,28},{20,24},{24,20},{28,16},{1,13},{... | collective-permute-start | bytes 208904 | tf_op jit(solution)/shard_map/ppermute | solution.py:334
  2.9 5.6 %collective-permute-start.12 = (bf16[272,128]{1,0:T(8,128)(2,1)S(1)}, bf16[272,128]{1,0:T(8,128)(2,1)S(1)}, u32[]{:S(2)}, u32[]{:S(2)}) collective-permute-start(bf16[272,128]{1,0:T(8,128)(2,1)S(1)} %get-tuple-element.96), channel_id=1, source_target_pairs={{0,4},{4,0},{8,12},{12,8},{16,20},{20,16},{24,28},{28,24},{1,5},{5... | collective-permute-start | bytes 208904 | tf_op jit(solution)/shard_map/ppermute | solution.py:334
  3.4 5.2 %collective-permute-start.13 = (bf16[272,128]{1,0:T(8,128)(2,1)S(1)}, bf16[272,128]{1,0:T(8,128)(2,1)S(1)}, u32[]{:S(2)}, u32[]{:S(2)}) collective-permute-start(bf16[272,128]{1,0:T(8,128)(2,1)S(1)} %get-tuple-element.97.refs_3_), channel_id=1, source_target_pairs={{0,8},{4,12},{8,0},{12,4},{16,24},{20,28},{24,16},{28,20},{1,9},{5... | collective-permute-start | bytes 208904 | tf_op jit(solution)/shard_map/ppermute | solution.py:334
  8.7 6.0 %collective-permute-start.15 = (bf16[272,128]{1,0:T(8,128)(2,1)S(1)}, bf16[272,128]{1,0:T(8,128)(2,1)S(1)}, u32[]{:S(2)}, u32[]{:S(2)}) collective-permute-start(bf16[272,128]{1,0:T(8,128)(2,1)S(1)} %get-tuple-element.101), channel_id=1, source_target_pairs={{0,16},{4,20},{8,24},{12,28},{16,0},{20,4},{24,8},{28,12},{1,17},{... | collective-permute-start | bytes 208904 | tf_op jit(solution)/shard_map/ppermute | solution.py:297
  9.1 4.3 %collective-permute-start.14 = (bf16[256,128]{1,0:T(8,128)(2,1)S(1)}, bf16[256,128]{1,0:T(8,128)(2,1)S(1)}, u32[]{:S(2)}, u32[]{:S(2)}) collective-permute-start(bf16[256,128]{1,0:T(8,128)(2,1)S(1)} %get-tuple-element.100), channel_id=1, source_target_pairs={{0,4},{4,0},{8,12},{12,8},{16,20},{20,16},{24,28},{28,24},{1,5},{5... | collective-permute-start | bytes 196616 | tf_op jit(solution)/shard_map/ppermute | solution.py:334
  14.7 4.4 %collective-permute-start.1 = (bf16[272,128]{1,0:T(8,128)(2,1)S(1)}, bf16[272,128]{1,0:T(8,128)(2,1)S(1)}, u32[]{:S(2)}, u32[]{:S(2)}) collective-permute-start(bf16[272,128]{1,0:T(8,128)(2,1)S(1)} %get-tuple-element.58), channel_id=1, source_target_pairs={{0,4},{4,0},{8,12},{12,8},{16,20},{20,16},{24,28},{28,24},{1,5},{5... | collective-permute-start | bytes 208904 | tf_op jit(solution)/shard_map/cond/branch_0_fun/ppermute | solution.py:334
  16.2 2.0 %collective-permute-start.2 = (bf16[128,256]{1,0:T(8,128)(2,1)S(1)}, bf16[128,256]{1,0:T(8,128)(2,1)S(1)}, u32[]{:S(2)}, u32[]{:S(2)}) collective-permute-start(bf16[128,256]{1,0:T(8,128)(2,1)S(1)} %norm_mine_1.1._.refs_2_.refs_4_), channel_id=1, source_target_pairs={{0,1},{1,0},{2,3},{3,2},{4,5},{5,4},{6,7},{7,6},{8,9},{9,8},{10,11... | collective-permute-start | bytes 196616 | tf_op jit(solution)/shard_map/cond/branch_0_fun/ppermute | solution.py:384
  16.6 1.6 %collective-permute-start = (bf16[128,256]{1,0:T(8,128)(2,1)S(1)}, bf16[128,256]{1,0:T(8,128)(2,1)S(1)}, u32[]{:S(2)}, u32[]{:S(2)}) collective-permute-start(bf16[128,256]{1,0:T(8,128)(2,1)S(1)} %norm_mine_0.1.refs_0_), channel_id=1, source_target_pairs={{0,1},{1,0},{2,3},{3,2},{4,5},{5,4},{6,7},{7,6},{8,9},{9,8},{10,11... | collective-permute-start | bytes 196616 | tf_op jit(solution)/shard_map/cond/branch_0_fun/ppermute | solution.py:384
  19.4 1.3 %collective-permute-start.4 = (bf16[128,256]{1,0:T(8,128)(2,1)S(1)}, bf16[128,256]{1,0:T(8,128)(2,1)S(1)}, u32[]{:S(2)}, u32[]{:S(2)}) collective-permute-start(bf16[128,256]{1,0:T(8,128)(2,1)S(1)} %norm_1.2.refs_6_.mine_ref), channel_id=1, source_target_pairs={{0,1},{1,0},{2,3},{3,2},{4,5},{5,4},{6,7},{7,6},{8,9},{9,8},{10,11... | collective-permute-start | bytes 196616 | tf_op jit(solution)/shard_map/cond/branch_0_fun/ppermute | solution.py:384
  19.8 2.5 %collective-permute-start.3 = (bf16[128,256]{1,0:T(8,128)(2,1)S(1)}, bf16[128,256]{1,0:T(8,128)(2,1)S(1)}, u32[]{:S(2)}, u32[]{:S(2)}) collective-permute-start(bf16[128,256]{1,0:T(8,128)(2,1)S(1)} %norm_0.2.refs_2_.mine_ref), channel_id=1, source_target_pairs={{0,1},{1,0},{2,3},{3,2},{4,5},{5,4},{6,7},{7,6},{8,9},{9,8},{10,11... | collective-permute-start | bytes 196616 | tf_op jit(solution)/shard_map/cond/branch_0_fun/ppermute | solution.py:384
  21.0 5.5 %collective-permute-start.6 = (bf16[128,512]{1,0:T(8,128)(2,1)S(1)}, bf16[128,512]{1,0:T(8,128)(2,1)S(1)}, u32[]{:S(2)}, u32[]{:S(2)}) collective-permute-start(bf16[128,512]{1,0:T(8,128)(2,1)S(1)} %project_far_1.2), channel_id=1, source_target_pairs={{0,3},{1,2},{2,1},{3,0},{4,7},{5,6},{6,5},{7,4},{8,11},{9,10},{10,... | collective-permute-start | bytes 393224 | tf_op jit(solution)/shard_map/cond/branch_0_fun/ppermute | solution.py:402
  22.5 6.8 %collective-permute-start.5 = (bf16[128,512]{1,0:T(8,128)(2,1)S(1)}, bf16[128,512]{1,0:T(8,128)(2,1)S(1)}, u32[]{:S(2)}, u32[]{:S(2)}) collective-permute-start(bf16[128,512]{1,0:T(8,128)(2,1)S(1)} %project_far_0.2), channel_id=1, source_target_pairs={{0,3},{1,2},{2,1},{3,0},{4,7},{5,6},{6,5},{7,4},{8,11},{9,10},{10,... | collective-permute-start | bytes 393224 | tf_op jit(solution)/shard_map/cond/branch_0_fun/ppermute | solution.py:402

commit v7 on v3

--- a/solution.py
+++ b/solution.py
@@ -186,6 +186,10 @@
         out_ref[at, :] = (rest_ref[at, :].astype(F32) + earlier).astype(BF16)
 
 
+def nothing_kernel(out_ref):
+    pass
+
+
 def norm_kernel(half, halves, rows, query_ref, intra_ref, own_ref, gain_ref, *refs):
     states, out_ref = refs[: len(halves)], refs[-1]
     for i, (mine, state_ref) in enumerate(zip(halves, states)):
@@ -291,10 +295,17 @@
     )
 
 
-def earlier_groups(total, half, devices):
+def earlier_groups(total, half, devices, first_alone):
     groups = devices // MEMBERS
     if groups == 2:
-        return lax.ppermute(total, "seq", [(i, i ^ MEMBERS) for i in range(devices)])
+        tp = lax.axis_size("tp")
+        swapped = first_alone(
+            lambda: lax.ppermute(total, "tp", [(i, i ^ 1) for i in range(tp)]), total
+        )
+        pairs = [
+            (i * tp + j, (i ^ MEMBERS) * tp + (j ^ 1)) for i in range(devices) for j in range(tp)
+        ]
+        return lax.ppermute(swapped, ("seq", "tp"), pairs)
 
     def shift(message, by):
         moves = [(i, i + by * MEMBERS) for i in range(devices - by * MEMBERS)]
@@ -353,7 +364,15 @@
         "gather_states",
         scratch=[pltpu.VMEM((MEMBERS,) + message.shape, BF16)],
     )(*received)
-    earlier = earlier_groups(total, half, devices)
+    first = lax.axis_index("seq") < MEMBERS
+
+    def first_alone(work, like):
+        def nothing():
+            return call(nothing_kernel, shape(like.shape, like.dtype), [], "nothing")()
+
+        return lax.cond(first, work, nothing)
+
+    earlier = earlier_groups(total, half, devices, first_alone)
     inside = swap(sent, 1)
     intra, own = call(
         functools.partial(local_kernel, heads),
@@ -458,7 +477,7 @@
         pairs = [pair for i in range(len(chunks)) for pair in (begun[i], parts[i])]
         return finish(((True,), (False,)), pairs, far)
 
-    return lax.cond(lax.axis_index("seq") < MEMBERS, first_group, later_group)
+    return lax.cond(first, first_group, later_group)
 
 
 def solution(mesh):

time: 30.4 us -> 31.6 us (1.039)
  waiting for transfers between devices: 13.2 us -> 14.3 us
  Pallas kernels: 7.58 us -> 8.19 us
  starting transfers between devices: 9.21 us -> 8.65 us
    ppermute x5, waiting for transfers between devices: 7.03 us -> 8.22 us  [swap(): return lax.ppermute(piece, 'seq', [(i, i ^ step) for i in range(devices)])]
    ppermute x5, starting transfers between devices: 5.4 us -> 4.28 us  [swap(): return lax.ppermute(piece, 'seq', [(i, i ^ step) for i in range(devices)])]
    pallas_call x0 -> x1, Pallas kernels: none -> 0.62 us  [nothing(): return call(nothing_kernel, shape(like.shape, like.dtype), [], 'nothing')()]
    ppermute x1, starting transfers between devices: 0.4 us -> 0.94 us  [earlier_groups(): return lax.ppermute(swapped, ('seq', 'tp'), pairs)]
  transfers between devices with their start and end apart: 13 -> 13, of which waited for: 9 -> 9; matrix products, arithmetic and copies ran while one was open for 0% -> 0% of each run, Pallas kernels for 22% -> 23%
where the time goes in v7:
time: 31.6 us; the launch traced here: 31.4 us
  waiting for transfers between devices  14.3 us (45%)
  starting transfers between devices  8.65 us (27%)
  Pallas kernels  8.19 us (26%)
    ppermute x5, waiting for transfers between devices, swap(): return lax.ppermute(piece, 'seq', [(i, i ^ step) for i in range(devices)])  8.22 us
    ppermute x2, waiting for transfers between devices, send_far(): return lax.ppermute(part, 'tp', far_pairs)  4.43 us
    ppermute x5, starting transfers between devices, swap(): return lax.ppermute(piece, 'seq', [(i, i ^ step) for i in range(devices)])  4.28 us
    ppermute x2, starting transfers between devices, send_far(): return lax.ppermute(part, 'tp', far_pairs)  2.16 us
    pallas_call x1, Pallas kernels, finish(): call(functools.partial(near_kernel, chunks, passes), shape((tokens, out_w...  1.6 us
    pallas_call x1, Pallas kernels, on_device(): call(functools.partial(state_kernel, half), (message, message) + tuple((s...  1.37 us
    ppermute x1, waiting for transfers between devices, earlier_groups(): return lax.ppermute(swapped, ('seq', 'tp'), pairs)  1.29 us
    ppermute x4, starting transfers between devices, normed(): return (part, lax.ppermute(part, 'tp', near_pairs))  1.28 us
  transfers between devices with their start and end apart: 13, of which 9 were waited for; matrix products, arithmetic and copies ran while one was open for 0% of the time, Pallas kernels for 23%

profile of v7, /device:TPU:24, one launch (start us, length us, event | category | flops | bytes accessed | tf_op | source)
XLA Modules:
  0.0 31.4 jit_solution(1887409425084425979)
XLA Ops:
  0.0 1.4 %states.1 = (bf16[272,128]{1,0:T(8,128)(2,1)S(1)}, bf16[272,128]{1,0:T(8,128)(2,1)S(1)}, f32[4,256]{1,0:T(4,128)S(1)}, bf16[256,512]{1,0:T(8,128)(2,1)S(1)}, bf1...) custom-call(f32[4,256]{1,0:T(4,128)} %refs_0_.1, bf16[256,512]{1,0:T(8,128)(2,1)} %refs_1_.1, ...), custom_call_target="tpu_custom_call" | custom-call | tf_op jit(solution)/shard_map/states/pallas_call | solution.py:350
  1.4 1.5 %collective-permute-start.12 = (bf16[272,128]{1,0:T(8,128)(2,1)S(1)}, bf16[272,128]{1,0:T(8,128)(2,1)S(1)}, u32[]{:S(2)}, u32[]{:S(2)}) collective-permute-start(bf16[272,128]{1,0:T(8,128)(2,1)S(1)} %get-tuple-element.100), channel_id=1, source_target_pairs={{0,12},{4,8},{8,4},{12,0},{16,28},{20,24},{24,20},{28,16},{1,13},{... | collective-permute-start | bytes 208904 | tf_op jit(solution)/shard_map/ppermute | solution.py:345
  2.9 0.5 %collective-permute-start.13 = (bf16[272,128]{1,0:T(8,128)(2,1)S(1)}, bf16[272,128]{1,0:T(8,128)(2,1)S(1)}, u32[]{:S(2)}, u32[]{:S(2)}) collective-permute-start(bf16[272,128]{1,0:T(8,128)(2,1)S(1)} %get-tuple-element.100), channel_id=1, source_target_pairs={{0,4},{4,0},{8,12},{12,8},{16,20},{20,16},{24,28},{28,24},{1,5},{5... | collective-permute-start | bytes 208904 | tf_op jit(solution)/shard_map/ppermute | solution.py:345
  3.4 1.6 %collective-permute-start.14 = (bf16[272,128]{1,0:T(8,128)(2,1)S(1)}, bf16[272,128]{1,0:T(8,128)(2,1)S(1)}, u32[]{:S(2)}, u32[]{:S(2)}) collective-permute-start(bf16[272,128]{1,0:T(8,128)(2,1)S(1)} %get-tuple-element.101.refs_3_), channel_id=1, source_target_pairs={{0,8},{4,12},{8,0},{12,4},{16,24},{20,28},{24,16},{28,20},{1,9},{5... | collective-permute-start | bytes 208904 | tf_op jit(solution)/shard_map/ppermute | solution.py:345
  4.9 2.1 %collective-permute-done.12.refs_0_ = bf16[272,128]{1,0:T(8,128)(2,1)S(1)} collective-permute-done((bf16[272,128]{1,0:T(8,128)(2,1)S(1)}, bf16[272,128]{1,0:T(8,128)(2,1)S(1)}, u32[]{:S(2)}, u32[]{:S(2)}) %collective-permute-start.12) | collective-permute-done | bytes 69664 | tf_op jit(solution)/shard_map/ppermute | solution.py:345
  7.0 1.4 %collective-permute-done.13.refs_1_ = bf16[272,128]{1,0:T(8,128)(2,1)S(1)} collective-permute-done((bf16[272,128]{1,0:T(8,128)(2,1)S(1)}, bf16[272,128]{1,0:T(8,128)(2,1)S(1)}, u32[]{:S(2)}, u32[]{:S(2)}) %collective-permute-start.13) | collective-permute-done | bytes 69664 | tf_op jit(solution)/shard_map/ppermute | solution.py:345
  8.7 0.6 %conditional.2 = (bf16[272,128]{1,0:T(8,128)(2,1)}) conditional(s32[]{:T(128)} %convert_element_type.4, () %tuple.17, bf16[272,128]{1,0:T(8,128)(2,1)S(1)} %get-tuple-element.105), branch_computations={%region_0.0_spmd, %region_1.0_spmd} | conditional | bytes 278576 | solution.py:373
  8.7 0.6 %nothing.1 = bf16[272,128]{1,0:T(8,128)(2,1)} custom-call(), custom_call_target="tpu_custom_call" | custom-call | tf_op jit(solution)/shard_map/cond/branch_0_fun/nothing/pallas_call | solution.py:371
  9.3 0.9 %collective-permute-start.16 = (bf16[272,128]{1,0:T(8,128)(2,1)}, bf16[272,128]{1,0:T(8,128)(2,1)S(1)}, u32[]{:S(2)}, u32[]{:S(2)}) collective-permute-start(bf16[272,128]{1,0:T(8,128)(2,1)} %get-tuple-element.113), channel_id=1, source_target_pairs={{0,17},{1,16},{2,19},{3,18},{4,21},{5,20},{6,23},{7,22},{8,25},{9,... | collective-permute-start | bytes 208904 | tf_op jit(solution)/shard_map/ppermute | solution.py:308
  10.2 0.7 %collective-permute-start.15 = (bf16[256,128]{1,0:T(8,128)(2,1)S(1)}, bf16[256,128]{1,0:T(8,128)(2,1)S(1)}, u32[]{:S(2)}, u32[]{:S(2)}) collective-permute-start(bf16[256,128]{1,0:T(8,128)(2,1)S(1)} %get-tuple-element.104), channel_id=1, source_target_pairs={{0,4},{4,0},{8,12},{12,8},{16,20},{20,16},{24,28},{28,24},{1,5},{5... | collective-permute-start | bytes 196616 | tf_op jit(solution)/shard_map/ppermute | solution.py:345
  10.9 0.7 %local.1 = (f32[256,512]{1,0:T(8,128)S(1)}, f32[256,4]{1,0:T(8,128)S(1)}) custom-call(f32[4,256]{1,0:T(4,128)S(1)} %get-tuple-element.94.decay_ref, bf16[256,512]{1,0:T(8,128)(2,1)S(1)} %get-tuple-element.93.query_ref, bf16[256,512]{1,0:T(8,128)(2,1)S(1)} %get-tuple-element.95.key_ref, bf16[256,512]{1,0:T(8,128)(2,1)S(1)} %get-tuple-element.96.value_ref), custom_call_target="tpu_custom_call" | custom-call | flops 134217728 | bytes 2000000 | tf_op jit(solution)/shard_map/local/pallas_call | solution.py:377
  11.6 3.0 %collective-permute-done.15.inside_ref = bf16[256,128]{1,0:T(8,128)(2,1)S(1)} collective-permute-done((bf16[256,128]{1,0:T(8,128)(2,1)S(1)}, bf16[256,128]{1,0:T(8,128)(2,1)S(1)}, u32[]{:S(2)}, u32[]{:S(2)}) %collective-permute-start.15) | collective-permute-done | bytes 65568 | tf_op jit(solution)/shard_map/ppermute | solution.py:345
  14.6 1.3 %collective-permute-done.16.earlier_ref = bf16[272,128]{1,0:T(8,128)(2,1)S(1)} collective-permute-done((bf16[272,128]{1,0:T(8,128)(2,1)}, bf16[272,128]{1,0:T(8,128)(2,1)S(1)}, u32[]{:S(2)}, u32[]{:S(2)}) %collective-permute-start.16) | collective-permute-done | bytes 69664 | tf_op jit(solution)/shard_map/ppermute | solution.py:308
  15.9 15.4 %conditional.3 = (bf16[256,512]{1,0:T(8,128)(2,1)}) conditional(s32[]{:T(128)} %convert_element_type.4, (bf16[256,512]{1,0:T(8,128)(2,1)S(1)}, f32[256,512]{1,0:T(8,128)S(1)}, f32[256,4]{1,0:T(8,128)S(1)}, f32[1,512]{1,0:T(1,128)S(1)}, bf16[256,128]{1,0:T(8,128)(2,1)S(1)}, /*index=5*/bf16[272,128]{1,0:T(8,128)(2,1)S(1)}, bf16[512,2048]{1,0:T(8,128)(2,1)}, ...), branch_computations={%region_2.0_spmd, %region_3.0_spmd} | conditional | bytes 2375968 | solution.py:480
  16.8 0.5 %collective-permute-start.1 = (bf16[128,256]{1,0:T(8,128)(2,1)S(1)}, bf16[128,256]{1,0:T(8,128)(2,1)S(1)}, u32[]{:S(2)}, u32[]{:S(2)}) collective-permute-start(bf16[128,256]{1,0:T(8,128)(2,1)S(1)} %norm_mine_0.1.refs_0_), channel_id=1, source_target_pairs={{0,1},{1,0},{2,3},{3,2},{4,5},{5,4},{6,7},{7,6},{8,9},{9,8},{10,11... | collective-permute-start | bytes 196616 | tf_op jit(solution)/shard_map/cond/branch_0_fun/ppermute | solution.py:403
  17.2 1.1 %fetch_far.2 = (bf16[512,512]{1,0:T(8,128)(2,1)S(1)}, bf16[512,512]{1,0:T(8,128)(2,1)S(1)}) custom-call(bf16[512,2048]{1,0:T(8,128)(2,1)} %get-tuple-element.53.weight_hbm, bf16[512,2048]{1,0:T(8,128)(2,1)S(1)} %get-tuple-element.54.other_weight_hbm, bf16[128,256]{1,0:T(8,128)(2,1)S(1)} %norm_mine_1.1._.refs_2_.refs_4_), custom_call_target="tpu_custom_call" | custom-call | tf_op jit(solution)/shard_map/cond/branch_0_fun/fetch_far/pallas_call | solution.py:406
  18.6 1.7 %collective-permute-done.2.earlier_ref = bf16[272,128]{1,0:T(8,128)(2,1)S(1)} collective-permute-done((bf16[272,128]{1,0:T(8,128)(2,1)S(1)}, bf16[272,128]{1,0:T(8,128)(2,1)S(1)}, u32[]{:S(2)}, u32[]{:S(2)}) %collective-permute-start.2) | collective-permute-done | bytes 69664 | tf_op jit(solution)/shard_map/cond/branch_0_fun/ppermute | solution.py:345
  21.0 0.6 %collective-permute-start.4 = (bf16[128,256]{1,0:T(8,128)(2,1)S(1)}, bf16[128,256]{1,0:T(8,128)(2,1)S(1)}, u32[]{:S(2)}, u32[]{:S(2)}) collective-permute-start(bf16[128,256]{1,0:T(8,128)(2,1)S(1)} %norm_0.2.refs_2_.mine_ref), channel_id=1, source_target_pairs={{0,1},{1,0},{2,3},{3,2},{4,5},{5,4},{6,7},{7,6},{8,9},{9,8},{10,11... | collective-permute-start | bytes 196616 | tf_op jit(solution)/shard_map/cond/branch_0_fun/ppermute | solution.py:403
  22.2 1.6 %collective-permute-start.7 = (bf16[128,512]{1,0:T(8,128)(2,1)S(1)}, bf16[128,512]{1,0:T(8,128)(2,1)S(1)}, u32[]{:S(2)}, u32[]{:S(2)}) collective-permute-start(bf16[128,512]{1,0:T(8,128)(2,1)S(1)} %project_far_1.2), channel_id=1, source_target_pairs={{0,2},{1,3},{2,0},{3,1},{4,6},{5,7},{6,4},{7,5},{8,10},{9,11},{10,... | collective-permute-start | bytes 393224 | tf_op jit(solution)/shard_map/cond/branch_0_fun/ppermute | solution.py:421
  24.0 0.6 %collective-permute-start.6 = (bf16[128,512]{1,0:T(8,128)(2,1)S(1)}, bf16[128,512]{1,0:T(8,128)(2,1)S(1)}, u32[]{:S(2)}, u32[]{:S(2)}) collective-permute-start(bf16[128,512]{1,0:T(8,128)(2,1)S(1)} %project_far_0.2), channel_id=1, source_target_pairs={{0,2},{1,3},{2,0},{3,1},{4,6},{5,7},{6,4},{7,5},{8,10},{9,11},{10,... | collective-permute-start | bytes 393224 | tf_op jit(solution)/shard_map/cond/branch_0_fun/ppermute | solution.py:421
  24.6 1.6 %project_near.2.near_ref = f32[256,512]{1,0:T(8,128)S(1)} custom-call(bf16[256,512]{1,0:T(8,128)(2,1)} %get-tuple-element.52.residual_hbm, bf16[512,2048]{1,0:T(8,128)(2,1)} %get-tuple-element.53.weight_hbm, bf16[512,2048]{1,0:T(8,128)(2,1)S(1)} %get-tuple-element.54.other_weight_hbm, bf16[128,256]{1,0:T(8,128)(2,1)S(1)} %norm_mine_0.1.refs_0_, ...), custom_call_target="tpu_custom_call" | custom-call | tf_op jit(solution)/shard_map/cond/branch_0_fun/project_near/pallas_call | solution.py:424
  26.2 2.4 %collective-permute-done.7.refs_1_ = bf16[128,512]{1,0:T(8,128)(2,1)S(1)} collective-permute-done((bf16[128,512]{1,0:T(8,128)(2,1)S(1)}, bf16[128,512]{1,0:T(8,128)(2,1)S(1)}, u32[]{:S(2)}, u32[]{:S(2)}) %collective-permute-start.7) | collective-permute-done | bytes 131104 | tf_op jit(solution)/shard_map/cond/branch_0_fun/ppermute | solution.py:421
  28.6 2.0 %collective-permute-done.6.refs_0_ = bf16[128,512]{1,0:T(8,128)(2,1)S(1)} collective-permute-done((bf16[128,512]{1,0:T(8,128)(2,1)S(1)}, bf16[128,512]{1,0:T(8,128)(2,1)S(1)}, u32[]{:S(2)}, u32[]{:S(2)}) %collective-permute-start.6) | collective-permute-done | bytes 131104 | tf_op jit(solution)/shard_map/cond/branch_0_fun/ppermute | solution.py:421
  30.6 0.7 %add.2 = bf16[256,512]{1,0:T(8,128)(2,1)} custom-call(f32[256,512]{1,0:T(8,128)S(1)} %project_near.2.near_ref, bf16[128,512]{1,0:T(8,128)(2,1)S(1)} %collective-permute-done.6.refs_0_, bf16[128,512]{1,0:T(8,128)(2,1)S(1)} %collective-permute-done.7.refs_1_), custom_call_target="tpu_custom_call" | custom-call | tf_op jit(solution)/shard_map/cond/branch_0_fun/add/pallas_call | solution.py:440
  (20 shorter events, 2.9 us)
Async XLA Ops:
  0.0 15.9 %collective-permute-start.17 = (bf16[512,2048]{1,0:T(8,128)(2,1)}, bf16[512,2048]{1,0:T(8,128)(2,1)S(1)}, u32[]{:S(2)}, u32[]{:S(2)}) collective-permute-start(bf16[512,2048]{1,0:T(8,128)(2,1)} %param.17), channel_id=1, source_target_pairs={{0,1},{1,0},{2,3},{3,2},{4,5},{5,4},{6,7},{7,6},{8,9},{9,8},{10,11... | collective-permute-start | bytes 6291464 | tf_op jit(solution)/shard_map/ppermute | solution.py:347
  1.4 5.7 %collective-permute-start.12 = (bf16[272,128]{1,0:T(8,128)(2,1)S(1)}, bf16[272,128]{1,0:T(8,128)(2,1)S(1)}, u32[]{:S(2)}, u32[]{:S(2)}) collective-permute-start(bf16[272,128]{1,0:T(8,128)(2,1)S(1)} %get-tuple-element.100), channel_id=1, source_target_pairs={{0,12},{4,8},{8,4},{12,0},{16,28},{20,24},{24,20},{28,16},{1,13},{... | collective-permute-start | bytes 208904 | tf_op jit(solution)/shard_map/ppermute | solution.py:345
  2.9 5.6 %collective-permute-start.13 = (bf16[272,128]{1,0:T(8,128)(2,1)S(1)}, bf16[272,128]{1,0:T(8,128)(2,1)S(1)}, u32[]{:S(2)}, u32[]{:S(2)}) collective-permute-start(bf16[272,128]{1,0:T(8,128)(2,1)S(1)} %get-tuple-element.100), channel_id=1, source_target_pairs={{0,4},{4,0},{8,12},{12,8},{16,20},{20,16},{24,28},{28,24},{1,5},{5... | collective-permute-start | bytes 208904 | tf_op jit(solution)/shard_map/ppermute | solution.py:345
  3.4 5.2 %collective-permute-start.14 = (bf16[272,128]{1,0:T(8,128)(2,1)S(1)}, bf16[272,128]{1,0:T(8,128)(2,1)S(1)}, u32[]{:S(2)}, u32[]{:S(2)}) collective-permute-start(bf16[272,128]{1,0:T(8,128)(2,1)S(1)} %get-tuple-element.101.refs_3_), channel_id=1, source_target_pairs={{0,8},{4,12},{8,0},{12,4},{16,24},{20,28},{24,16},{28,20},{1,9},{5... | collective-permute-start | bytes 208904 | tf_op jit(solution)/shard_map/ppermute | solution.py:345
  9.3 6.6 %collective-permute-start.16 = (bf16[272,128]{1,0:T(8,128)(2,1)}, bf16[272,128]{1,0:T(8,128)(2,1)S(1)}, u32[]{:S(2)}, u32[]{:S(2)}) collective-permute-start(bf16[272,128]{1,0:T(8,128)(2,1)} %get-tuple-element.113), channel_id=1, source_target_pairs={{0,17},{1,16},{2,19},{3,18},{4,21},{5,20},{6,23},{7,22},{8,25},{9,... | collective-permute-start | bytes 208904 | tf_op jit(solution)/shard_map/ppermute | solution.py:308
  10.2 4.4 %collective-permute-start.15 = (bf16[256,128]{1,0:T(8,128)(2,1)S(1)}, bf16[256,128]{1,0:T(8,128)(2,1)S(1)}, u32[]{:S(2)}, u32[]{:S(2)}) collective-permute-start(bf16[256,128]{1,0:T(8,128)(2,1)S(1)} %get-tuple-element.104), channel_id=1, source_target_pairs={{0,4},{4,0},{8,12},{12,8},{16,20},{20,16},{24,28},{28,24},{1,5},{5... | collective-permute-start | bytes 196616 | tf_op jit(solution)/shard_map/ppermute | solution.py:345
  15.9 4.4 %collective-permute-start.2 = (bf16[272,128]{1,0:T(8,128)(2,1)S(1)}, bf16[272,128]{1,0:T(8,128)(2,1)S(1)}, u32[]{:S(2)}, u32[]{:S(2)}) collective-permute-start(bf16[272,128]{1,0:T(8,128)(2,1)S(1)} %get-tuple-element.62), channel_id=1, source_target_pairs={{0,4},{4,0},{8,12},{12,8},{16,20},{20,16},{24,28},{28,24},{1,5},{5... | collective-permute-start | bytes 208904 | tf_op jit(solution)/shard_map/cond/branch_0_fun/ppermute | solution.py:345
  16.3 2.0 %collective-permute-start.3 = (bf16[128,256]{1,0:T(8,128)(2,1)S(1)}, bf16[128,256]{1,0:T(8,128)(2,1)S(1)}, u32[]{:S(2)}, u32[]{:S(2)}) collective-permute-start(bf16[128,256]{1,0:T(8,128)(2,1)S(1)} %norm_mine_1.1._.refs_2_.refs_4_), channel_id=1, source_target_pairs={{0,1},{1,0},{2,3},{3,2},{4,5},{5,4},{6,7},{7,6},{8,9},{9,8},{10,11... | collective-permute-start | bytes 196616 | tf_op jit(solution)/shard_map/cond/branch_0_fun/ppermute | solution.py:403
  16.8 1.5 %collective-permute-start.1 = (bf16[128,256]{1,0:T(8,128)(2,1)S(1)}, bf16[128,256]{1,0:T(8,128)(2,1)S(1)}, u32[]{:S(2)}, u32[]{:S(2)}) collective-permute-start(bf16[128,256]{1,0:T(8,128)(2,1)S(1)} %norm_mine_0.1.refs_0_), channel_id=1, source_target_pairs={{0,1},{1,0},{2,3},{3,2},{4,5},{5,4},{6,7},{7,6},{8,9},{9,8},{10,11... | collective-permute-start | bytes 196616 | tf_op jit(solution)/shard_map/cond/branch_0_fun/ppermute | solution.py:403
  20.6 1.3 %collective-permute-start.5 = (bf16[128,256]{1,0:T(8,128)(2,1)S(1)}, bf16[128,256]{1,0:T(8,128)(2,1)S(1)}, u32[]{:S(2)}, u32[]{:S(2)}) collective-permute-start(bf16[128,256]{1,0:T(8,128)(2,1)S(1)} %norm_1.2.refs_6_.mine_ref), channel_id=1, source_target_pairs={{0,1},{1,0},{2,3},{3,2},{4,5},{5,4},{6,7},{7,6},{8,9},{9,8},{10,11... | collective-permute-start | bytes 196616 | tf_op jit(solution)/shard_map/cond/branch_0_fun/ppermute | solution.py:403
  21.0 2.7 %collective-permute-start.4 = (bf16[128,256]{1,0:T(8,128)(2,1)S(1)}, bf16[128,256]{1,0:T(8,128)(2,1)S(1)}, u32[]{:S(2)}, u32[]{:S(2)}) collective-permute-start(bf16[128,256]{1,0:T(8,128)(2,1)S(1)} %norm_0.2.refs_2_.mine_ref), channel_id=1, source_target_pairs={{0,1},{1,0},{2,3},{3,2},{4,5},{5,4},{6,7},{7,6},{8,9},{9,8},{10,11... | collective-permute-start | bytes 196616 | tf_op jit(solution)/shard_map/cond/branch_0_fun/ppermute | solution.py:403
  22.2 6.4 %collective-permute-start.7 = (bf16[128,512]{1,0:T(8,128)(2,1)S(1)}, bf16[128,512]{1,0:T(8,128)(2,1)S(1)}, u32[]{:S(2)}, u32[]{:S(2)}) collective-permute-start(bf16[128,512]{1,0:T(8,128)(2,1)S(1)} %project_far_1.2), channel_id=1, source_target_pairs={{0,2},{1,3},{2,0},{3,1},{4,6},{5,7},{6,4},{7,5},{8,10},{9,11},{10,... | collective-permute-start | bytes 393224 | tf_op jit(solution)/shard_map/cond/branch_0_fun/ppermute | solution.py:421
  24.0 6.6 %collective-permute-start.6 = (bf16[128,512]{1,0:T(8,128)(2,1)S(1)}, bf16[128,512]{1,0:T(8,128)(2,1)S(1)}, u32[]{:S(2)}, u32[]{:S(2)}) collective-permute-start(bf16[128,512]{1,0:T(8,128)(2,1)S(1)} %project_far_0.2), channel_id=1, source_target_pairs={{0,2},{1,3},{2,0},{3,1},{4,6},{5,7},{6,4},{7,5},{8,10},{9,11},{10,... | collective-permute-start | bytes 393224 | tf_op jit(solution)/shard_map/cond/branch_0_fun/ppermute | solution.py:421

commit v8 on v3

--- a/solution.py
+++ b/solution.py
@@ -163,10 +163,11 @@
         sent_ref[at, :] = jnp.where(upper, first, last).astype(BF16)
         total_ref[at, :] = held[MEMBERS].astype(BF16)
         totals.append(through[MEMBERS])
-    total_ref[half * HEAD_DIM :, :] = decays_to_rows(totals)
-
-
-def start_kernel(half, before_ref, through_ref, inside_ref, earlier_ref, _, *outs):
+    if total_ref.shape[0] > half * HEAD_DIM:
+        total_ref[half * HEAD_DIM :, :] = decays_to_rows(totals)
+
+
+def start_kernel(half, before_ref, through_ref, earlier_ref, inside_ref, _, *outs):
     mine_ref, rest_ref, factor_ref, sent_ref = outs
     started = lax.axis_index("seq") >= MEMBERS
     for j in range(half):
@@ -176,7 +177,9 @@
         mine_ref[at, :] = held.astype(BF16)
     rest_ref[...] = inside_ref[...]
     factor_ref[...] = through_ref[8 * half :, :]
-    sent_ref[...] = earlier_ref[...]
+    rows = half * HEAD_DIM
+    sent_ref[:rows, :] = earlier_ref[:rows, :]
+    sent_ref[rows:, :] = jnp.zeros((DECAY_ROWS, HEAD_DIM), BF16)
 
 
 def start_other_kernel(half, rest_ref, factor_ref, earlier_ref, _, out_ref):
@@ -348,7 +351,12 @@
     state = shape(states, BF16)
     before, sent, through, total = call(
         functools.partial(gather_kernel, half, steps),
-        (shape(states, F32), state, shape((heads * 8, HEAD_DIM), F32), message),
+        (
+            shape(states, F32),
+            state,
+            shape((heads * 8, HEAD_DIM), F32),
+            state if devices == 2 * MEMBERS else message,
+        ),
         [VMEM] * len(steps),
         "gather_states",
         scratch=[pltpu.VMEM((MEMBERS,) + message.shape, BF16)],
@@ -367,7 +375,7 @@
         (state, state, shape((half * 8, HEAD_DIM), F32), message),
         [VMEM] * 5,
         "start_states",
-    )(before, through, inside, earlier, own)
+    )(before, through, earlier, inside, own)
 
     chunks = [slice(0, tokens // 2), slice(tokens // 2, tokens)]
     block = (out_weight.shape[0], out_width)

time: 30.4 us -> 30.3 us (level)
    ppermute x5, waiting for transfers between devices: 7.03 us -> 4.2 us  [swap(): return lax.ppermute(piece, 'seq', [(i, i ^ step) for i in range(devices)])]
    ppermute x1, waiting for transfers between devices: 1.35 us -> 4.14 us  [earlier_groups(): lax.ppermute(total, 'seq', [(i, i ^ MEMBERS) for i in range(devices)])]
  transfers between devices with their start and end apart: 13 -> 13, of which waited for: 9 -> 8; matrix products, arithmetic and copies ran while one was open for 0% -> 0% of each run, Pallas kernels for 22% -> 22%
where the time goes in v8:
time: 30.3 us; the launch traced here: 30.1 us
  waiting for transfers between devices  13.2 us (44%)
  starting transfers between devices  9.18 us (30%)
  Pallas kernels  7.57 us (25%)
    ppermute x5, starting transfers between devices, swap(): return lax.ppermute(piece, 'seq', [(i, i ^ step) for i in range(devices)])  5.35 us
    ppermute x2, waiting for transfers between devices, send_far(): return lax.ppermute(part, 'tp', far_pairs)  4.43 us
    ppermute x5, waiting for transfers between devices, swap(): return lax.ppermute(piece, 'seq', [(i, i ^ step) for i in range(devices)])  4.2 us
    ppermute x1, waiting for transfers between devices, earlier_groups(): lax.ppermute(total, 'seq', [(i, i ^ MEMBERS) for i in range(devices)])  4.14 us
    ppermute x2, starting transfers between devices, send_far(): return lax.ppermute(part, 'tp', far_pairs)  2.16 us
    pallas_call x1, Pallas kernels, finish(): call(functools.partial(near_kernel, chunks, passes), shape((tokens, out_w...  1.6 us
    pallas_call x1, Pallas kernels, on_device(): call(functools.partial(state_kernel, half), (message, message) + tuple((s...  1.37 us
    ppermute x4, starting transfers between devices, normed(): return (part, lax.ppermute(part, 'tp', near_pairs))  1.27 us
  transfers between devices with their start and end apart: 13, of which 8 were waited for; matrix products, arithmetic and copies ran while one was open for 0% of the time, Pallas kernels for 22%

profile of v8, /device:TPU:24, one launch (start us, length us, event | category | flops | bytes accessed | tf_op | source)
XLA Modules:
  0.0 30.1 jit_solution(17001005887398810916)
XLA Ops:
  0.0 1.4 %states.1 = (bf16[272,128]{1,0:T(8,128)(2,1)S(1)}, bf16[272,128]{1,0:T(8,128)(2,1)S(1)}, f32[4,256]{1,0:T(4,128)S(1)}, bf16[256,512]{1,0:T(8,128)(2,1)S(1)}, bf1...) custom-call(f32[4,256]{1,0:T(4,128)} %refs_0_.1, bf16[256,512]{1,0:T(8,128)(2,1)} %refs_1_.1, ...), custom_call_target="tpu_custom_call" | custom-call | tf_op jit(solution)/shard_map/states/pallas_call | solution.py:342
  1.4 1.5 %collective-permute-start.11 = (bf16[272,128]{1,0:T(8,128)(2,1)S(1)}, bf16[272,128]{1,0:T(8,128)(2,1)S(1)}, u32[]{:S(2)}, u32[]{:S(2)}) collective-permute-start(bf16[272,128]{1,0:T(8,128)(2,1)S(1)} %get-tuple-element.96), channel_id=1, source_target_pairs={{0,12},{4,8},{8,4},{12,0},{16,28},{20,24},{24,20},{28,16},{1,13},{... | collective-permute-start | bytes 208904 | tf_op jit(solution)/shard_map/ppermute | solution.py:337
  2.9 0.5 %collective-permute-start.12 = (bf16[272,128]{1,0:T(8,128)(2,1)S(1)}, bf16[272,128]{1,0:T(8,128)(2,1)S(1)}, u32[]{:S(2)}, u32[]{:S(2)}) collective-permute-start(bf16[272,128]{1,0:T(8,128)(2,1)S(1)} %get-tuple-element.96), channel_id=1, source_target_pairs={{0,4},{4,0},{8,12},{12,8},{16,20},{20,16},{24,28},{28,24},{1,5},{5... | collective-permute-start | bytes 208904 | tf_op jit(solution)/shard_map/ppermute | solution.py:337
  3.4 1.6 %collective-permute-start.13 = (bf16[272,128]{1,0:T(8,128)(2,1)S(1)}, bf16[272,128]{1,0:T(8,128)(2,1)S(1)}, u32[]{:S(2)}, u32[]{:S(2)}) collective-permute-start(bf16[272,128]{1,0:T(8,128)(2,1)S(1)} %get-tuple-element.97.refs_3_), channel_id=1, source_target_pairs={{0,8},{4,12},{8,0},{12,4},{16,24},{20,28},{24,16},{28,20},{1,9},{5... | collective-permute-start | bytes 208904 | tf_op jit(solution)/shard_map/ppermute | solution.py:337
  4.9 2.1 %collective-permute-done.11.refs_0_ = bf16[272,128]{1,0:T(8,128)(2,1)S(1)} collective-permute-done((bf16[272,128]{1,0:T(8,128)(2,1)S(1)}, bf16[272,128]{1,0:T(8,128)(2,1)S(1)}, u32[]{:S(2)}, u32[]{:S(2)}) %collective-permute-start.11) | collective-permute-done | bytes 69664 | tf_op jit(solution)/shard_map/ppermute | solution.py:337
  7.0 1.4 %collective-permute-done.12.refs_1_ = bf16[272,128]{1,0:T(8,128)(2,1)S(1)} collective-permute-done((bf16[272,128]{1,0:T(8,128)(2,1)S(1)}, bf16[272,128]{1,0:T(8,128)(2,1)S(1)}, u32[]{:S(2)}, u32[]{:S(2)}) %collective-permute-start.12) | collective-permute-done | bytes 69664 | tf_op jit(solution)/shard_map/ppermute | solution.py:337
  8.7 0.4 %collective-permute-start.14 = (bf16[256,128]{1,0:T(8,128)(2,1)S(1)}, bf16[256,128]{1,0:T(8,128)(2,1)S(1)}, u32[]{:S(2)}, u32[]{:S(2)}) collective-permute-start(bf16[256,128]{1,0:T(8,128)(2,1)S(1)} %get-tuple-element.100), channel_id=1, source_target_pairs={{0,16},{4,20},{8,24},{12,28},{16,0},{20,4},{24,8},{28,12},{1,17},{... | collective-permute-start | bytes 196616 | tf_op jit(solution)/shard_map/ppermute | solution.py:300
  9.1 0.7 %collective-permute-start.15 = (bf16[256,128]{1,0:T(8,128)(2,1)S(1)}, bf16[256,128]{1,0:T(8,128)(2,1)S(1)}, u32[]{:S(2)}, u32[]{:S(2)}) collective-permute-start(bf16[256,128]{1,0:T(8,128)(2,1)S(1)} %get-tuple-element.101), channel_id=1, source_target_pairs={{0,4},{4,0},{8,12},{12,8},{16,20},{20,16},{24,28},{28,24},{1,5},{5... | collective-permute-start | bytes 196616 | tf_op jit(solution)/shard_map/ppermute | solution.py:337
  9.7 0.7 %local.1 = (f32[256,512]{1,0:T(8,128)S(1)}, f32[256,4]{1,0:T(8,128)S(1)}) custom-call(f32[4,256]{1,0:T(4,128)S(1)} %get-tuple-element.90.decay_ref, bf16[256,512]{1,0:T(8,128)(2,1)S(1)} %get-tuple-element.89.query_ref, bf16[256,512]{1,0:T(8,128)(2,1)S(1)} %get-tuple-element.91.key_ref, bf16[256,512]{1,0:T(8,128)(2,1)S(1)} %get-tuple-element.92.value_ref), custom_call_target="tpu_custom_call" | custom-call | flops 134217728 | bytes 2000000 | tf_op jit(solution)/shard_map/local/pallas_call | solution.py:366
  10.5 4.1 %collective-permute-done.14.earlier_ref = bf16[256,128]{1,0:T(8,128)(2,1)S(1)} collective-permute-done((bf16[256,128]{1,0:T(8,128)(2,1)S(1)}, bf16[256,128]{1,0:T(8,128)(2,1)S(1)}, u32[]{:S(2)}, u32[]{:S(2)}) %collective-permute-start.14) | collective-permute-done | bytes 65568 | tf_op jit(solution)/shard_map/ppermute | solution.py:300
  14.6 15.4 %conditional.1 = (bf16[256,512]{1,0:T(8,128)(2,1)}) conditional(s32[]{:T(128)} %convert_element_type.3, (bf16[256,512]{1,0:T(8,128)(2,1)S(1)}, f32[256,512]{1,0:T(8,128)S(1)}, f32[256,4]{1,0:T(8,128)S(1)}, f32[1,512]{1,0:T(1,128)S(1)}, bf16[256,128]{1,0:T(8,128)(2,1)S(1)}, /*index=5*/bf16[272,128]{1,0:T(8,128)(2,1)S(1)}, bf16[512,2048]{1,0:T(8,128)(2,1)}, ...), branch_computations={%region_0.0_spmd, %region_1.0_spmd} | conditional | bytes 2375968 | solution.py:469
  14.7 1.1 %collective-permute-start.1 = (bf16[272,128]{1,0:T(8,128)(2,1)S(1)}, bf16[272,128]{1,0:T(8,128)(2,1)S(1)}, u32[]{:S(2)}, u32[]{:S(2)}) collective-permute-start(bf16[272,128]{1,0:T(8,128)(2,1)S(1)} %get-tuple-element.58), channel_id=1, source_target_pairs={{0,4},{4,0},{8,12},{12,8},{16,20},{20,16},{24,28},{28,24},{1,5},{5... | collective-permute-start | bytes 208904 | tf_op jit(solution)/shard_map/cond/branch_0_fun/ppermute | solution.py:337
  16.5 0.6 %collective-permute-start = (bf16[128,256]{1,0:T(8,128)(2,1)S(1)}, bf16[128,256]{1,0:T(8,128)(2,1)S(1)}, u32[]{:S(2)}, u32[]{:S(2)}) collective-permute-start(bf16[128,256]{1,0:T(8,128)(2,1)S(1)} %norm_mine_0.1.refs_0_), channel_id=1, source_target_pairs={{0,1},{1,0},{2,3},{3,2},{4,5},{5,4},{6,7},{7,6},{8,9},{9,8},{10,11... | collective-permute-start | bytes 196616 | tf_op jit(solution)/shard_map/cond/branch_0_fun/ppermute | solution.py:392
  17.0 1.1 %fetch_far.2 = (bf16[512,512]{1,0:T(8,128)(2,1)S(1)}, bf16[512,512]{1,0:T(8,128)(2,1)S(1)}) custom-call(bf16[512,2048]{1,0:T(8,128)(2,1)} %get-tuple-element.49.weight_hbm, bf16[512,2048]{1,0:T(8,128)(2,1)S(1)} %get-tuple-element.50.other_weight_hbm, bf16[128,256]{1,0:T(8,128)(2,1)S(1)} %norm_mine_1.1._.refs_2_.refs_4_), custom_call_target="tpu_custom_call" | custom-call | tf_op jit(solution)/shard_map/cond/branch_0_fun/fetch_far/pallas_call | solution.py:395
  18.1 0.3 %project_far_mine.1._.begun_ref = f32[256,512]{1,0:T(8,128)S(1)} custom-call(bf16[512,512]{1,0:T(8,128)(2,1)S(1)} %get-tuple-element.59.weight_ref, bf16[512,512]{1,0:T(8,128)(2,1)S(1)} %get-tuple-element.60.other_weight_ref, bf16[128,256]{1,0:T(8,128)(2,1)S(1)} %norm_mine_0.1.refs_0_, bf16[128,256]{1,0:T(8,128)(2,1)S(1)} %collective-permute-done.refs_1_, ...), custom_call_target="tpu_custom_call" | custom-call | tf_op jit(solution)/shard_map/cond/branch_0_fun/project_far_mine/pallas_call | solution.py:452
  18.4 0.6 %collective-permute-done.1.earlier_ref = bf16[272,128]{1,0:T(8,128)(2,1)S(1)} collective-permute-done((bf16[272,128]{1,0:T(8,128)(2,1)S(1)}, bf16[272,128]{1,0:T(8,128)(2,1)S(1)}, u32[]{:S(2)}, u32[]{:S(2)}) %collective-permute-start.1) | collective-permute-done | bytes 69664 | tf_op jit(solution)/shard_map/cond/branch_0_fun/ppermute | solution.py:337
  19.7 0.6 %collective-permute-start.3 = (bf16[128,256]{1,0:T(8,128)(2,1)S(1)}, bf16[128,256]{1,0:T(8,128)(2,1)S(1)}, u32[]{:S(2)}, u32[]{:S(2)}) collective-permute-start(bf16[128,256]{1,0:T(8,128)(2,1)S(1)} %norm_0.2.refs_2_.mine_ref), channel_id=1, source_target_pairs={{0,1},{1,0},{2,3},{3,2},{4,5},{5,4},{6,7},{7,6},{8,9},{9,8},{10,11... | collective-permute-start | bytes 196616 | tf_op jit(solution)/shard_map/cond/branch_0_fun/ppermute | solution.py:392
  20.3 0.4 %collective-permute-done.4.refs_7_.other_ref = bf16[128,256]{1,0:T(8,128)(2,1)S(1)} collective-permute-done((bf16[128,256]{1,0:T(8,128)(2,1)S(1)}, bf16[128,256]{1,0:T(8,128)(2,1)S(1)}, u32[]{:S(2)}, u32[]{:S(2)}) %collective-permute-start.4) | collective-permute-done | bytes 65568 | tf_op jit(solution)/shard_map/cond/branch_0_fun/ppermute | solution.py:392
  20.9 1.6 %collective-permute-start.6 = (bf16[128,512]{1,0:T(8,128)(2,1)S(1)}, bf16[128,512]{1,0:T(8,128)(2,1)S(1)}, u32[]{:S(2)}, u32[]{:S(2)}) collective-permute-start(bf16[128,512]{1,0:T(8,128)(2,1)S(1)} %project_far_1.2), channel_id=1, source_target_pairs={{0,2},{1,3},{2,0},{3,1},{4,6},{5,7},{6,4},{7,5},{8,10},{9,11},{10,... | collective-permute-start | bytes 393224 | tf_op jit(solution)/shard_map/cond/branch_0_fun/ppermute | solution.py:410
  22.7 0.6 %collective-permute-start.5 = (bf16[128,512]{1,0:T(8,128)(2,1)S(1)}, bf16[128,512]{1,0:T(8,128)(2,1)S(1)}, u32[]{:S(2)}, u32[]{:S(2)}) collective-permute-start(bf16[128,512]{1,0:T(8,128)(2,1)S(1)} %project_far_0.2), channel_id=1, source_target_pairs={{0,2},{1,3},{2,0},{3,1},{4,6},{5,7},{6,4},{7,5},{8,10},{9,11},{10,... | collective-permute-start | bytes 393224 | tf_op jit(solution)/shard_map/cond/branch_0_fun/ppermute | solution.py:410
  23.3 1.6 %project_near.2.near_ref = f32[256,512]{1,0:T(8,128)S(1)} custom-call(bf16[256,512]{1,0:T(8,128)(2,1)} %get-tuple-element.48.residual_hbm, bf16[512,2048]{1,0:T(8,128)(2,1)} %get-tuple-element.49.weight_hbm, bf16[512,2048]{1,0:T(8,128)(2,1)S(1)} %get-tuple-element.50.other_weight_hbm, bf16[128,256]{1,0:T(8,128)(2,1)S(1)} %norm_mine_0.1.refs_0_, ...), custom_call_target="tpu_custom_call" | custom-call | tf_op jit(solution)/shard_map/cond/branch_0_fun/project_near/pallas_call | solution.py:413
  24.9 2.4 %collective-permute-done.6.refs_1_ = bf16[128,512]{1,0:T(8,128)(2,1)S(1)} collective-permute-done((bf16[128,512]{1,0:T(8,128)(2,1)S(1)}, bf16[128,512]{1,0:T(8,128)(2,1)S(1)}, u32[]{:S(2)}, u32[]{:S(2)}) %collective-permute-start.6) | collective-permute-done | bytes 131104 | tf_op jit(solution)/shard_map/cond/branch_0_fun/ppermute | solution.py:410
  27.3 2.0 %collective-permute-done.5.refs_0_ = bf16[128,512]{1,0:T(8,128)(2,1)S(1)} collective-permute-done((bf16[128,512]{1,0:T(8,128)(2,1)S(1)}, bf16[128,512]{1,0:T(8,128)(2,1)S(1)}, u32[]{:S(2)}, u32[]{:S(2)}) %collective-permute-start.5) | collective-permute-done | bytes 131104 | tf_op jit(solution)/shard_map/cond/branch_0_fun/ppermute | solution.py:410
  29.3 0.7 %add.2 = bf16[256,512]{1,0:T(8,128)(2,1)} custom-call(f32[256,512]{1,0:T(8,128)S(1)} %project_near.2.near_ref, bf16[128,512]{1,0:T(8,128)(2,1)S(1)} %collective-permute-done.5.refs_0_, bf16[128,512]{1,0:T(8,128)(2,1)S(1)} %collective-permute-done.6.refs_1_), custom_call_target="tpu_custom_call" | custom-call | tf_op jit(solution)/shard_map/cond/branch_0_fun/add/pallas_call | solution.py:429
  (18 shorter events, 2.0 us)
Async XLA Ops:
  0.0 14.6 %collective-permute-start.16 = (bf16[512,2048]{1,0:T(8,128)(2,1)}, bf16[512,2048]{1,0:T(8,128)(2,1)S(1)}, u32[]{:S(2)}, u32[]{:S(2)}) collective-permute-start(bf16[512,2048]{1,0:T(8,128)(2,1)} %param.15), channel_id=1, source_target_pairs={{0,1},{1,0},{2,3},{3,2},{4,5},{5,4},{6,7},{7,6},{8,9},{9,8},{10,11... | collective-permute-start | bytes 6291464 | tf_op jit(solution)/shard_map/ppermute | solution.py:339
  1.4 5.7 %collective-permute-start.11 = (bf16[272,128]{1,0:T(8,128)(2,1)S(1)}, bf16[272,128]{1,0:T(8,128)(2,1)S(1)}, u32[]{:S(2)}, u32[]{:S(2)}) collective-permute-start(bf16[272,128]{1,0:T(8,128)(2,1)S(1)} %get-tuple-element.96), channel_id=1, source_target_pairs={{0,12},{4,8},{8,4},{12,0},{16,28},{20,24},{24,20},{28,16},{1,13},{... | collective-permute-start | bytes 208904 | tf_op jit(solution)/shard_map/ppermute | solution.py:337
  2.9 5.6 %collective-permute-start.12 = (bf16[272,128]{1,0:T(8,128)(2,1)S(1)}, bf16[272,128]{1,0:T(8,128)(2,1)S(1)}, u32[]{:S(2)}, u32[]{:S(2)}) collective-permute-start(bf16[272,128]{1,0:T(8,128)(2,1)S(1)} %get-tuple-element.96), channel_id=1, source_target_pairs={{0,4},{4,0},{8,12},{12,8},{16,20},{20,16},{24,28},{28,24},{1,5},{5... | collective-permute-start | bytes 208904 | tf_op jit(solution)/shard_map/ppermute | solution.py:337
  3.4 5.2 %collective-permute-start.13 = (bf16[272,128]{1,0:T(8,128)(2,1)S(1)}, bf16[272,128]{1,0:T(8,128)(2,1)S(1)}, u32[]{:S(2)}, u32[]{:S(2)}) collective-permute-start(bf16[272,128]{1,0:T(8,128)(2,1)S(1)} %get-tuple-element.97.refs_3_), channel_id=1, source_target_pairs={{0,8},{4,12},{8,0},{12,4},{16,24},{20,28},{24,16},{28,20},{1,9},{5... | collective-permute-start | bytes 208904 | tf_op jit(solution)/shard_map/ppermute | solution.py:337
  8.7 5.9 %collective-permute-start.14 = (bf16[256,128]{1,0:T(8,128)(2,1)S(1)}, bf16[256,128]{1,0:T(8,128)(2,1)S(1)}, u32[]{:S(2)}, u32[]{:S(2)}) collective-permute-start(bf16[256,128]{1,0:T(8,128)(2,1)S(1)} %get-tuple-element.100), channel_id=1, source_target_pairs={{0,16},{4,20},{8,24},{12,28},{16,0},{20,4},{24,8},{28,12},{1,17},{... | collective-permute-start | bytes 196616 | tf_op jit(solution)/shard_map/ppermute | solution.py:300
  9.1 5.5 %collective-permute-start.15 = (bf16[256,128]{1,0:T(8,128)(2,1)S(1)}, bf16[256,128]{1,0:T(8,128)(2,1)S(1)}, u32[]{:S(2)}, u32[]{:S(2)}) collective-permute-start(bf16[256,128]{1,0:T(8,128)(2,1)S(1)} %get-tuple-element.101), channel_id=1, source_target_pairs={{0,4},{4,0},{8,12},{12,8},{16,20},{20,16},{24,28},{28,24},{1,5},{5... | collective-permute-start | bytes 196616 | tf_op jit(solution)/shard_map/ppermute | solution.py:337
  14.7 4.4 %collective-permute-start.1 = (bf16[272,128]{1,0:T(8,128)(2,1)S(1)}, bf16[272,128]{1,0:T(8,128)(2,1)S(1)}, u32[]{:S(2)}, u32[]{:S(2)}) collective-permute-start(bf16[272,128]{1,0:T(8,128)(2,1)S(1)} %get-tuple-element.58), channel_id=1, source_target_pairs={{0,4},{4,0},{8,12},{12,8},{16,20},{20,16},{24,28},{28,24},{1,5},{5... | collective-permute-start | bytes 208904 | tf_op jit(solution)/shard_map/cond/branch_0_fun/ppermute | solution.py:337
  16.1 2.0 %collective-permute-start.2 = (bf16[128,256]{1,0:T(8,128)(2,1)S(1)}, bf16[128,256]{1,0:T(8,128)(2,1)S(1)}, u32[]{:S(2)}, u32[]{:S(2)}) collective-permute-start(bf16[128,256]{1,0:T(8,128)(2,1)S(1)} %norm_mine_1.1._.refs_2_.refs_4_), channel_id=1, source_target_pairs={{0,1},{1,0},{2,3},{3,2},{4,5},{5,4},{6,7},{7,6},{8,9},{9,8},{10,11... | collective-permute-start | bytes 196616 | tf_op jit(solution)/shard_map/cond/branch_0_fun/ppermute | solution.py:392
  16.5 1.6 %collective-permute-start = (bf16[128,256]{1,0:T(8,128)(2,1)S(1)}, bf16[128,256]{1,0:T(8,128)(2,1)S(1)}, u32[]{:S(2)}, u32[]{:S(2)}) collective-permute-start(bf16[128,256]{1,0:T(8,128)(2,1)S(1)} %norm_mine_0.1.refs_0_), channel_id=1, source_target_pairs={{0,1},{1,0},{2,3},{3,2},{4,5},{5,4},{6,7},{7,6},{8,9},{9,8},{10,11... | collective-permute-start | bytes 196616 | tf_op jit(solution)/shard_map/cond/branch_0_fun/ppermute | solution.py:392
  19.3 1.3 %collective-permute-start.4 = (bf16[128,256]{1,0:T(8,128)(2,1)S(1)}, bf16[128,256]{1,0:T(8,128)(2,1)S(1)}, u32[]{:S(2)}, u32[]{:S(2)}) collective-permute-start(bf16[128,256]{1,0:T(8,128)(2,1)S(1)} %norm_1.2.refs_6_.mine_ref), channel_id=1, source_target_pairs={{0,1},{1,0},{2,3},{3,2},{4,5},{5,4},{6,7},{7,6},{8,9},{9,8},{10,11... | collective-permute-start | bytes 196616 | tf_op jit(solution)/shard_map/cond/branch_0_fun/ppermute | solution.py:392
  19.7 2.8 %collective-permute-start.3 = (bf16[128,256]{1,0:T(8,128)(2,1)S(1)}, bf16[128,256]{1,0:T(8,128)(2,1)S(1)}, u32[]{:S(2)}, u32[]{:S(2)}) collective-permute-start(bf16[128,256]{1,0:T(8,128)(2,1)S(1)} %norm_0.2.refs_2_.mine_ref), channel_id=1, source_target_pairs={{0,1},{1,0},{2,3},{3,2},{4,5},{5,4},{6,7},{7,6},{8,9},{9,8},{10,11... | collective-permute-start | bytes 196616 | tf_op jit(solution)/shard_map/cond/branch_0_fun/ppermute | solution.py:392
  20.9 6.4 %collective-permute-start.6 = (bf16[128,512]{1,0:T(8,128)(2,1)S(1)}, bf16[128,512]{1,0:T(8,128)(2,1)S(1)}, u32[]{:S(2)}, u32[]{:S(2)}) collective-permute-start(bf16[128,512]{1,0:T(8,128)(2,1)S(1)} %project_far_1.2), channel_id=1, source_target_pairs={{0,2},{1,3},{2,0},{3,1},{4,6},{5,7},{6,4},{7,5},{8,10},{9,11},{10,... | collective-permute-start | bytes 393224 | tf_op jit(solution)/shard_map/cond/branch_0_fun/ppermute | solution.py:410
  22.7 6.6 %collective-permute-start.5 = (bf16[128,512]{1,0:T(8,128)(2,1)S(1)}, bf16[128,512]{1,0:T(8,128)(2,1)S(1)}, u32[]{:S(2)}, u32[]{:S(2)}) collective-permute-start(bf16[128,512]{1,0:T(8,128)(2,1)S(1)} %project_far_0.2), channel_id=1, source_target_pairs={{0,2},{1,3},{2,0},{3,1},{4,6},{5,7},{6,4},{7,5},{8,10},{9,11},{10,... | collective-permute-start | bytes 393224 | tf_op jit(solution)/shard_map/cond/branch_0_fun/ppermute | solution.py:410

commit v9 on v8

--- a/solution.py
+++ b/solution.py
@@ -346,8 +346,8 @@
         "states",
         scratch=[pltpu.SemaphoreType.DMA((5,))],
     )(*(pltpu.with_memory_space_constraint(a, pltpu.HBM) for a in arguments))
-    steps = (3, 1, 2, 0)
-    received = [swap(theirs, 3), swap(theirs, 1), swap(mine, 2), mine]
+    steps = (2, 3, 1, 0)
+    received = [swap(mine, 2), swap(theirs, 3), swap(theirs, 1), mine]
     state = shape(states, BF16)
     before, sent, through, total = call(
         functools.partial(gather_kernel, half, steps),

time: 30.3 us -> 31.8 us (1.050)
  waiting for transfers between devices: 13.2 us -> 15.6 us
  starting transfers between devices: 9.18 us -> 8.2 us
    ppermute x5, waiting for transfers between devices: 4.2 us -> 6.25 us  [swap(): return lax.ppermute(piece, 'seq', [(i, i ^ step) for i in range(devices)])]
    ppermute x5, starting transfers between devices: 5.35 us -> 4.38 us  [swap(): return lax.ppermute(piece, 'seq', [(i, i ^ step) for i in range(devices)])]
    ppermute x1, waiting for transfers between devices: 4.14 us -> 4.53 us  [earlier_groups(): lax.ppermute(total, 'seq', [(i, i ^ MEMBERS) for i in range(devices)])]
  transfers between devices with their start and end apart: 13 -> 13, of which waited for: 8 -> 8; matrix products, arithmetic and copies ran while one was open for 0% -> 0% of each run, Pallas kernels for 22% -> 21%
where the time goes in v9:
time: 31.8 us; the launch traced here: 31.5 us
  waiting for transfers between devices  15.6 us (49%)
  starting transfers between devices  8.2 us (26%)
  Pallas kernels  7.57 us (24%)
    ppermute x5, waiting for transfers between devices, swap(): return lax.ppermute(piece, 'seq', [(i, i ^ step) for i in range(devices)])  6.25 us
    ppermute x1, waiting for transfers between devices, earlier_groups(): lax.ppermute(total, 'seq', [(i, i ^ MEMBERS) for i in range(devices)])  4.53 us
    ppermute x2, waiting for transfers between devices, send_far(): return lax.ppermute(part, 'tp', far_pairs)  4.43 us
    ppermute x5, starting transfers between devices, swap(): return lax.ppermute(piece, 'seq', [(i, i ^ step) for i in range(devices)])  4.38 us
    ppermute x2, starting transfers between devices, send_far(): return lax.ppermute(part, 'tp', far_pairs)  2.16 us
    pallas_call x1, Pallas kernels, finish(): call(functools.partial(near_kernel, chunks, passes), shape((tokens, out_w...  1.6 us
    pallas_call x1, Pallas kernels, on_device(): call(functools.partial(state_kernel, half), (message, message) + tuple((s...  1.37 us
    ppermute x4, starting transfers between devices, normed(): return (part, lax.ppermute(part, 'tp', near_pairs))  1.27 us
  transfers between devices with their start and end apart: 13, of which 8 were waited for; matrix products, arithmetic and copies ran while one was open for 0% of the time, Pallas kernels for 21%

profile of v9, /device:TPU:24, one launch (start us, length us, event | category | flops | bytes accessed | tf_op | source)
XLA Modules:
  0.0 31.5 jit_solution(16781746993371843998)
XLA Ops:
  0.0 1.4 %states.1 = (bf16[272,128]{1,0:T(8,128)(2,1)S(1)}, bf16[272,128]{1,0:T(8,128)(2,1)S(1)}, f32[4,256]{1,0:T(4,128)S(1)}, bf16[256,512]{1,0:T(8,128)(2,1)S(1)}, bf1...) custom-call(f32[4,256]{1,0:T(4,128)} %refs_0_.1, bf16[256,512]{1,0:T(8,128)(2,1)} %refs_1_.1, ...), custom_call_target="tpu_custom_call" | custom-call | tf_op jit(solution)/shard_map/states/pallas_call | solution.py:342
  1.4 0.5 %collective-permute-start.11 = (bf16[272,128]{1,0:T(8,128)(2,1)S(1)}, bf16[272,128]{1,0:T(8,128)(2,1)S(1)}, u32[]{:S(2)}, u32[]{:S(2)}) collective-permute-start(bf16[272,128]{1,0:T(8,128)(2,1)S(1)} %get-tuple-element.96.refs_3_), channel_id=1, source_target_pairs={{0,8},{4,12},{8,0},{12,4},{16,24},{20,28},{24,16},{28,20},{1,9},{5... | collective-permute-start | bytes 208904 | tf_op jit(solution)/shard_map/ppermute | solution.py:337
  1.9 2.5 %collective-permute-start.12 = (bf16[272,128]{1,0:T(8,128)(2,1)S(1)}, bf16[272,128]{1,0:T(8,128)(2,1)S(1)}, u32[]{:S(2)}, u32[]{:S(2)}) collective-permute-start(bf16[272,128]{1,0:T(8,128)(2,1)S(1)} %get-tuple-element.97), channel_id=1, source_target_pairs={{0,12},{4,8},{8,4},{12,0},{16,28},{20,24},{24,20},{28,16},{1,13},{... | collective-permute-start | bytes 208904 | tf_op jit(solution)/shard_map/ppermute | solution.py:337
  4.4 0.5 %collective-permute-start.13 = (bf16[272,128]{1,0:T(8,128)(2,1)S(1)}, bf16[272,128]{1,0:T(8,128)(2,1)S(1)}, u32[]{:S(2)}, u32[]{:S(2)}) collective-permute-start(bf16[272,128]{1,0:T(8,128)(2,1)S(1)} %get-tuple-element.97), channel_id=1, source_target_pairs={{0,4},{4,0},{8,12},{12,8},{16,20},{20,16},{24,28},{28,24},{1,5},{5... | collective-permute-start | bytes 208904 | tf_op jit(solution)/shard_map/ppermute | solution.py:337
  4.9 1.5 %collective-permute-done.11.refs_0_ = bf16[272,128]{1,0:T(8,128)(2,1)S(1)} collective-permute-done((bf16[272,128]{1,0:T(8,128)(2,1)S(1)}, bf16[272,128]{1,0:T(8,128)(2,1)S(1)}, u32[]{:S(2)}, u32[]{:S(2)}) %collective-permute-start.11) | collective-permute-done | bytes 69664 | tf_op jit(solution)/shard_map/ppermute | solution.py:337
  6.5 2.1 %collective-permute-done.12.refs_1_ = bf16[272,128]{1,0:T(8,128)(2,1)S(1)} collective-permute-done((bf16[272,128]{1,0:T(8,128)(2,1)S(1)}, bf16[272,128]{1,0:T(8,128)(2,1)S(1)}, u32[]{:S(2)}, u32[]{:S(2)}) %collective-permute-start.12) | collective-permute-done | bytes 69664 | tf_op jit(solution)/shard_map/ppermute | solution.py:337
  8.6 1.2 %collective-permute-done.13.refs_2_ = bf16[272,128]{1,0:T(8,128)(2,1)S(1)} collective-permute-done((bf16[272,128]{1,0:T(8,128)(2,1)S(1)}, bf16[272,128]{1,0:T(8,128)(2,1)S(1)}, u32[]{:S(2)}, u32[]{:S(2)}) %collective-permute-start.13) | collective-permute-done | bytes 69664 | tf_op jit(solution)/shard_map/ppermute | solution.py:337
  9.9 0.4 %collective-permute-start.14 = (bf16[256,128]{1,0:T(8,128)(2,1)S(1)}, bf16[256,128]{1,0:T(8,128)(2,1)S(1)}, u32[]{:S(2)}, u32[]{:S(2)}) collective-permute-start(bf16[256,128]{1,0:T(8,128)(2,1)S(1)} %get-tuple-element.100), channel_id=1, source_target_pairs={{0,16},{4,20},{8,24},{12,28},{16,0},{20,4},{24,8},{28,12},{1,17},{... | collective-permute-start | bytes 196616 | tf_op jit(solution)/shard_map/ppermute | solution.py:300
  10.3 0.5 %collective-permute-start.15 = (bf16[256,128]{1,0:T(8,128)(2,1)S(1)}, bf16[256,128]{1,0:T(8,128)(2,1)S(1)}, u32[]{:S(2)}, u32[]{:S(2)}) collective-permute-start(bf16[256,128]{1,0:T(8,128)(2,1)S(1)} %get-tuple-element.101), channel_id=1, source_target_pairs={{0,4},{4,0},{8,12},{12,8},{16,20},{20,16},{24,28},{28,24},{1,5},{5... | collective-permute-start | bytes 196616 | tf_op jit(solution)/shard_map/ppermute | solution.py:337
  10.8 0.7 %local.1 = (f32[256,512]{1,0:T(8,128)S(1)}, f32[256,4]{1,0:T(8,128)S(1)}) custom-call(f32[4,256]{1,0:T(4,128)S(1)} %get-tuple-element.90.decay_ref, bf16[256,512]{1,0:T(8,128)(2,1)S(1)} %get-tuple-element.89.query_ref, bf16[256,512]{1,0:T(8,128)(2,1)S(1)} %get-tuple-element.91.key_ref, bf16[256,512]{1,0:T(8,128)(2,1)S(1)} %get-tuple-element.92.value_ref), custom_call_target="tpu_custom_call" | custom-call | flops 134217728 | bytes 2000000 | tf_op jit(solution)/shard_map/local/pallas_call | solution.py:366
  11.5 4.5 %collective-permute-done.14.earlier_ref = bf16[256,128]{1,0:T(8,128)(2,1)S(1)} collective-permute-done((bf16[256,128]{1,0:T(8,128)(2,1)S(1)}, bf16[256,128]{1,0:T(8,128)(2,1)S(1)}, u32[]{:S(2)}, u32[]{:S(2)}) %collective-permute-start.14) | collective-permute-done | bytes 65568 | tf_op jit(solution)/shard_map/ppermute | solution.py:300
  16.1 15.4 %conditional.1 = (bf16[256,512]{1,0:T(8,128)(2,1)}) conditional(s32[]{:T(128)} %convert_element_type.3, (bf16[256,512]{1,0:T(8,128)(2,1)S(1)}, f32[256,512]{1,0:T(8,128)S(1)}, f32[256,4]{1,0:T(8,128)S(1)}, f32[1,512]{1,0:T(1,128)S(1)}, bf16[256,128]{1,0:T(8,128)(2,1)S(1)}, /*index=5*/bf16[272,128]{1,0:T(8,128)(2,1)S(1)}, bf16[512,2048]{1,0:T(8,128)(2,1)}, ...), branch_computations={%region_0.0_spmd, %region_1.0_spmd} | conditional | bytes 2375968 | solution.py:469
  16.1 0.3 %collective-permute-start.1 = (bf16[272,128]{1,0:T(8,128)(2,1)S(1)}, bf16[272,128]{1,0:T(8,128)(2,1)S(1)}, u32[]{:S(2)}, u32[]{:S(2)}) collective-permute-start(bf16[272,128]{1,0:T(8,128)(2,1)S(1)} %get-tuple-element.58), channel_id=1, source_target_pairs={{0,4},{4,0},{8,12},{12,8},{16,20},{20,16},{24,28},{28,24},{1,5},{5... | collective-permute-start | bytes 208904 | tf_op jit(solution)/shard_map/cond/branch_0_fun/ppermute | solution.py:337
  17.1 0.6 %collective-permute-start = (bf16[128,256]{1,0:T(8,128)(2,1)S(1)}, bf16[128,256]{1,0:T(8,128)(2,1)S(1)}, u32[]{:S(2)}, u32[]{:S(2)}) collective-permute-start(bf16[128,256]{1,0:T(8,128)(2,1)S(1)} %norm_mine_0.1.refs_0_), channel_id=1, source_target_pairs={{0,1},{1,0},{2,3},{3,2},{4,5},{5,4},{6,7},{7,6},{8,9},{9,8},{10,11... | collective-permute-start | bytes 196616 | tf_op jit(solution)/shard_map/cond/branch_0_fun/ppermute | solution.py:392
  17.7 1.1 %fetch_far.2 = (bf16[512,512]{1,0:T(8,128)(2,1)S(1)}, bf16[512,512]{1,0:T(8,128)(2,1)S(1)}) custom-call(bf16[512,2048]{1,0:T(8,128)(2,1)} %get-tuple-element.49.weight_hbm, bf16[512,2048]{1,0:T(8,128)(2,1)S(1)} %get-tuple-element.50.other_weight_hbm, bf16[128,256]{1,0:T(8,128)(2,1)S(1)} %norm_mine_1.1._.refs_2_.refs_4_), custom_call_target="tpu_custom_call" | custom-call | tf_op jit(solution)/shard_map/cond/branch_0_fun/fetch_far/pallas_call | solution.py:395
  19.1 1.4 %collective-permute-done.1.earlier_ref = bf16[272,128]{1,0:T(8,128)(2,1)S(1)} collective-permute-done((bf16[272,128]{1,0:T(8,128)(2,1)S(1)}, bf16[272,128]{1,0:T(8,128)(2,1)S(1)}, u32[]{:S(2)}, u32[]{:S(2)}) %collective-permute-start.1) | collective-permute-done | bytes 69664 | tf_op jit(solution)/shard_map/cond/branch_0_fun/ppermute | solution.py:337
  21.2 0.6 %collective-permute-start.3 = (bf16[128,256]{1,0:T(8,128)(2,1)S(1)}, bf16[128,256]{1,0:T(8,128)(2,1)S(1)}, u32[]{:S(2)}, u32[]{:S(2)}) collective-permute-start(bf16[128,256]{1,0:T(8,128)(2,1)S(1)} %norm_0.2.refs_2_.mine_ref), channel_id=1, source_target_pairs={{0,1},{1,0},{2,3},{3,2},{4,5},{5,4},{6,7},{7,6},{8,9},{9,8},{10,11... | collective-permute-start | bytes 196616 | tf_op jit(solution)/shard_map/cond/branch_0_fun/ppermute | solution.py:392
  21.7 0.4 %collective-permute-done.4.refs_7_.other_ref = bf16[128,256]{1,0:T(8,128)(2,1)S(1)} collective-permute-done((bf16[128,256]{1,0:T(8,128)(2,1)S(1)}, bf16[128,256]{1,0:T(8,128)(2,1)S(1)}, u32[]{:S(2)}, u32[]{:S(2)}) %collective-permute-start.4) | collective-permute-done | bytes 65568 | tf_op jit(solution)/shard_map/cond/branch_0_fun/ppermute | solution.py:392
  22.4 1.6 %collective-permute-start.6 = (bf16[128,512]{1,0:T(8,128)(2,1)S(1)}, bf16[128,512]{1,0:T(8,128)(2,1)S(1)}, u32[]{:S(2)}, u32[]{:S(2)}) collective-permute-start(bf16[128,512]{1,0:T(8,128)(2,1)S(1)} %project_far_1.2), channel_id=1, source_target_pairs={{0,2},{1,3},{2,0},{3,1},{4,6},{5,7},{6,4},{7,5},{8,10},{9,11},{10,... | collective-permute-start | bytes 393224 | tf_op jit(solution)/shard_map/cond/branch_0_fun/ppermute | solution.py:410
  24.2 0.6 %collective-permute-start.5 = (bf16[128,512]{1,0:T(8,128)(2,1)S(1)}, bf16[128,512]{1,0:T(8,128)(2,1)S(1)}, u32[]{:S(2)}, u32[]{:S(2)}) collective-permute-start(bf16[128,512]{1,0:T(8,128)(2,1)S(1)} %project_far_0.2), channel_id=1, source_target_pairs={{0,2},{1,3},{2,0},{3,1},{4,6},{5,7},{6,4},{7,5},{8,10},{9,11},{10,... | collective-permute-start | bytes 393224 | tf_op jit(solution)/shard_map/cond/branch_0_fun/ppermute | solution.py:410
  24.8 1.6 %project_near.2.near_ref = f32[256,512]{1,0:T(8,128)S(1)} custom-call(bf16[256,512]{1,0:T(8,128)(2,1)} %get-tuple-element.48.residual_hbm, bf16[512,2048]{1,0:T(8,128)(2,1)} %get-tuple-element.49.weight_hbm, bf16[512,2048]{1,0:T(8,128)(2,1)S(1)} %get-tuple-element.50.other_weight_hbm, bf16[128,256]{1,0:T(8,128)(2,1)S(1)} %norm_mine_0.1.refs_0_, ...), custom_call_target="tpu_custom_call" | custom-call | tf_op jit(solution)/shard_map/cond/branch_0_fun/project_near/pallas_call | solution.py:413
  26.4 2.4 %collective-permute-done.6.refs_1_ = bf16[128,512]{1,0:T(8,128)(2,1)S(1)} collective-permute-done((bf16[128,512]{1,0:T(8,128)(2,1)S(1)}, bf16[128,512]{1,0:T(8,128)(2,1)S(1)}, u32[]{:S(2)}, u32[]{:S(2)}) %collective-permute-start.6) | collective-permute-done | bytes 131104 | tf_op jit(solution)/shard_map/cond/branch_0_fun/ppermute | solution.py:410
  28.8 2.0 %collective-permute-done.5.refs_0_ = bf16[128,512]{1,0:T(8,128)(2,1)S(1)} collective-permute-done((bf16[128,512]{1,0:T(8,128)(2,1)S(1)}, bf16[128,512]{1,0:T(8,128)(2,1)S(1)}, u32[]{:S(2)}, u32[]{:S(2)}) %collective-permute-start.5) | collective-permute-done | bytes 131104 | tf_op jit(solution)/shard_map/cond/branch_0_fun/ppermute | solution.py:410
  30.8 0.7 %add.2 = bf16[256,512]{1,0:T(8,128)(2,1)} custom-call(f32[256,512]{1,0:T(8,128)S(1)} %project_near.2.near_ref, bf16[128,512]{1,0:T(8,128)(2,1)S(1)} %collective-permute-done.5.refs_0_, bf16[128,512]{1,0:T(8,128)(2,1)S(1)} %collective-permute-done.6.refs_1_), custom_call_target="tpu_custom_call" | custom-call | tf_op jit(solution)/shard_map/cond/branch_0_fun/add/pallas_call | solution.py:429
  (18 shorter events, 2.2 us)
Async XLA Ops:
  0.0 16.1 %collective-permute-start.16 = (bf16[512,2048]{1,0:T(8,128)(2,1)}, bf16[512,2048]{1,0:T(8,128)(2,1)S(1)}, u32[]{:S(2)}, u32[]{:S(2)}) collective-permute-start(bf16[512,2048]{1,0:T(8,128)(2,1)} %param.15), channel_id=1, source_target_pairs={{0,1},{1,0},{2,3},{3,2},{4,5},{5,4},{6,7},{7,6},{8,9},{9,8},{10,11... | collective-permute-start | bytes 6291464 | tf_op jit(solution)/shard_map/ppermute | solution.py:339
  1.4 5.1 %collective-permute-start.11 = (bf16[272,128]{1,0:T(8,128)(2,1)S(1)}, bf16[272,128]{1,0:T(8,128)(2,1)S(1)}, u32[]{:S(2)}, u32[]{:S(2)}) collective-permute-start(bf16[272,128]{1,0:T(8,128)(2,1)S(1)} %get-tuple-element.96.refs_3_), channel_id=1, source_target_pairs={{0,8},{4,12},{8,0},{12,4},{16,24},{20,28},{24,16},{28,20},{1,9},{5... | collective-permute-start | bytes 208904 | tf_op jit(solution)/shard_map/ppermute | solution.py:337
  1.9 6.7 %collective-permute-start.12 = (bf16[272,128]{1,0:T(8,128)(2,1)S(1)}, bf16[272,128]{1,0:T(8,128)(2,1)S(1)}, u32[]{:S(2)}, u32[]{:S(2)}) collective-permute-start(bf16[272,128]{1,0:T(8,128)(2,1)S(1)} %get-tuple-element.97), channel_id=1, source_target_pairs={{0,12},{4,8},{8,4},{12,0},{16,28},{20,24},{24,20},{28,16},{1,13},{... | collective-permute-start | bytes 208904 | tf_op jit(solution)/shard_map/ppermute | solution.py:337
  4.4 5.3 %collective-permute-start.13 = (bf16[272,128]{1,0:T(8,128)(2,1)S(1)}, bf16[272,128]{1,0:T(8,128)(2,1)S(1)}, u32[]{:S(2)}, u32[]{:S(2)}) collective-permute-start(bf16[272,128]{1,0:T(8,128)(2,1)S(1)} %get-tuple-element.97), channel_id=1, source_target_pairs={{0,4},{4,0},{8,12},{12,8},{16,20},{20,16},{24,28},{28,24},{1,5},{5... | collective-permute-start | bytes 208904 | tf_op jit(solution)/shard_map/ppermute | solution.py:337
  9.9 6.2 %collective-permute-start.14 = (bf16[256,128]{1,0:T(8,128)(2,1)S(1)}, bf16[256,128]{1,0:T(8,128)(2,1)S(1)}, u32[]{:S(2)}, u32[]{:S(2)}) collective-permute-start(bf16[256,128]{1,0:T(8,128)(2,1)S(1)} %get-tuple-element.100), channel_id=1, source_target_pairs={{0,16},{4,20},{8,24},{12,28},{16,0},{20,4},{24,8},{28,12},{1,17},{... | collective-permute-start | bytes 196616 | tf_op jit(solution)/shard_map/ppermute | solution.py:300
  10.3 5.8 %collective-permute-start.15 = (bf16[256,128]{1,0:T(8,128)(2,1)S(1)}, bf16[256,128]{1,0:T(8,128)(2,1)S(1)}, u32[]{:S(2)}, u32[]{:S(2)}) collective-permute-start(bf16[256,128]{1,0:T(8,128)(2,1)S(1)} %get-tuple-element.101), channel_id=1, source_target_pairs={{0,4},{4,0},{8,12},{12,8},{16,20},{20,16},{24,28},{28,24},{1,5},{5... | collective-permute-start | bytes 196616 | tf_op jit(solution)/shard_map/ppermute | solution.py:337
  16.1 4.4 %collective-permute-start.1 = (bf16[272,128]{1,0:T(8,128)(2,1)S(1)}, bf16[272,128]{1,0:T(8,128)(2,1)S(1)}, u32[]{:S(2)}, u32[]{:S(2)}) collective-permute-start(bf16[272,128]{1,0:T(8,128)(2,1)S(1)} %get-tuple-element.58), channel_id=1, source_target_pairs={{0,4},{4,0},{8,12},{12,8},{16,20},{20,16},{24,28},{28,24},{1,5},{5... | collective-permute-start | bytes 208904 | tf_op jit(solution)/shard_map/cond/branch_0_fun/ppermute | solution.py:337
  16.7 2.0 %collective-permute-start.2 = (bf16[128,256]{1,0:T(8,128)(2,1)S(1)}, bf16[128,256]{1,0:T(8,128)(2,1)S(1)}, u32[]{:S(2)}, u32[]{:S(2)}) collective-permute-start(bf16[128,256]{1,0:T(8,128)(2,1)S(1)} %norm_mine_1.1._.refs_2_.refs_4_), channel_id=1, source_target_pairs={{0,1},{1,0},{2,3},{3,2},{4,5},{5,4},{6,7},{7,6},{8,9},{9,8},{10,11... | collective-permute-start | bytes 196616 | tf_op jit(solution)/shard_map/cond/branch_0_fun/ppermute | solution.py:392
  17.1 1.6 %collective-permute-start = (bf16[128,256]{1,0:T(8,128)(2,1)S(1)}, bf16[128,256]{1,0:T(8,128)(2,1)S(1)}, u32[]{:S(2)}, u32[]{:S(2)}) collective-permute-start(bf16[128,256]{1,0:T(8,128)(2,1)S(1)} %norm_mine_0.1.refs_0_), channel_id=1, source_target_pairs={{0,1},{1,0},{2,3},{3,2},{4,5},{5,4},{6,7},{7,6},{8,9},{9,8},{10,11... | collective-permute-start | bytes 196616 | tf_op jit(solution)/shard_map/cond/branch_0_fun/ppermute | solution.py:392
  20.8 1.3 %collective-permute-start.4 = (bf16[128,256]{1,0:T(8,128)(2,1)S(1)}, bf16[128,256]{1,0:T(8,128)(2,1)S(1)}, u32[]{:S(2)}, u32[]{:S(2)}) collective-permute-start(bf16[128,256]{1,0:T(8,128)(2,1)S(1)} %norm_1.2.refs_6_.mine_ref), channel_id=1, source_target_pairs={{0,1},{1,0},{2,3},{3,2},{4,5},{5,4},{6,7},{7,6},{8,9},{9,8},{10,11... | collective-permute-start | bytes 196616 | tf_op jit(solution)/shard_map/cond/branch_0_fun/ppermute | solution.py:392
  21.2 2.8 %collective-permute-start.3 = (bf16[128,256]{1,0:T(8,128)(2,1)S(1)}, bf16[128,256]{1,0:T(8,128)(2,1)S(1)}, u32[]{:S(2)}, u32[]{:S(2)}) collective-permute-start(bf16[128,256]{1,0:T(8,128)(2,1)S(1)} %norm_0.2.refs_2_.mine_ref), channel_id=1, source_target_pairs={{0,1},{1,0},{2,3},{3,2},{4,5},{5,4},{6,7},{7,6},{8,9},{9,8},{10,11... | collective-permute-start | bytes 196616 | tf_op jit(solution)/shard_map/cond/branch_0_fun/ppermute | solution.py:392
  22.4 6.4 %collective-permute-start.6 = (bf16[128,512]{1,0:T(8,128)(2,1)S(1)}, bf16[128,512]{1,0:T(8,128)(2,1)S(1)}, u32[]{:S(2)}, u32[]{:S(2)}) collective-permute-start(bf16[128,512]{1,0:T(8,128)(2,1)S(1)} %project_far_1.2), channel_id=1, source_target_pairs={{0,2},{1,3},{2,0},{3,1},{4,6},{5,7},{6,4},{7,5},{8,10},{9,11},{10,... | collective-permute-start | bytes 393224 | tf_op jit(solution)/shard_map/cond/branch_0_fun/ppermute | solution.py:410
  24.2 6.6 %collective-permute-start.5 = (bf16[128,512]{1,0:T(8,128)(2,1)S(1)}, bf16[128,512]{1,0:T(8,128)(2,1)S(1)}, u32[]{:S(2)}, u32[]{:S(2)}) collective-permute-start(bf16[128,512]{1,0:T(8,128)(2,1)S(1)} %project_far_0.2), channel_id=1, source_target_pairs={{0,2},{1,3},{2,0},{3,1},{4,6},{5,7},{6,4},{7,5},{8,10},{9,11},{10,... | collective-permute-start | bytes 393224 | tf_op jit(solution)/shard_map/cond/branch_0_fun/ppermute | solution.py:410

commit v10 on v9

--- a/solution.py
+++ b/solution.py
@@ -346,8 +346,8 @@
         "states",
         scratch=[pltpu.SemaphoreType.DMA((5,))],
     )(*(pltpu.with_memory_space_constraint(a, pltpu.HBM) for a in arguments))
-    steps = (2, 3, 1, 0)
-    received = [swap(mine, 2), swap(theirs, 3), swap(theirs, 1), mine]
+    steps = (1, 2, 3, 0)
+    received = [swap(theirs, 1), swap(mine, 2), swap(theirs, 3), mine]
     state = shape(states, BF16)
     before, sent, through, total = call(
         functools.partial(gather_kernel, half, steps),

time: 31.8 us -> 30.8 us (0.969)
  the two profiles are of different devices: /device:TPU:24 before, /device:TPU:16 now
where the time goes in v10:
time: 30.8 us; the launch traced here: 30.6 us
  waiting for transfers between devices  14.3 us (46%)
  starting transfers between devices  8.52 us (28%)
  Pallas kernels  7.58 us (25%)
    ppermute x5, waiting for transfers between devices, swap(): return lax.ppermute(piece, 'seq', [(i, i ^ step) for i in range(devices)])  5.92 us
    ppermute x5, starting transfers between devices, swap(): return lax.ppermute(piece, 'seq', [(i, i ^ step) for i in range(devices)])  4.7 us
    ppermute x2, waiting for transfers between devices, send_far(): return lax.ppermute(part, 'tp', far_pairs)  4.43 us
    ppermute x1, waiting for transfers between devices, earlier_groups(): lax.ppermute(total, 'seq', [(i, i ^ MEMBERS) for i in range(devices)])  3.59 us
    ppermute x2, starting transfers between devices, send_far(): return lax.ppermute(part, 'tp', far_pairs)  2.16 us
    pallas_call x1, Pallas kernels, finish(): call(functools.partial(near_kernel, chunks, passes), shape((tokens, out_w...  1.6 us
    pallas_call x1, Pallas kernels, on_device(): call(functools.partial(state_kernel, half), (message, message) + tuple((s...  1.37 us
    ppermute x4, starting transfers between devices, normed(): return (part, lax.ppermute(part, 'tp', near_pairs))  1.27 us
  transfers between devices with their start and end apart: 13, of which 8 were waited for; matrix products, arithmetic and copies ran while one was open for 0% of the time, Pallas kernels for 21%

profile of v10, /device:TPU:16, one launch (start us, length us, event | category | flops | bytes accessed | tf_op | source)
XLA Modules:
  0.0 30.6 jit_solution(14518712810406552754)
XLA Ops:
  0.0 1.4 %states.1 = (bf16[272,128]{1,0:T(8,128)(2,1)S(1)}, bf16[272,128]{1,0:T(8,128)(2,1)S(1)}, f32[4,256]{1,0:T(4,128)S(1)}, bf16[256,512]{1,0:T(8,128)(2,1)S(1)}, bf1...) custom-call(f32[4,256]{1,0:T(4,128)} %refs_0_.1, bf16[256,512]{1,0:T(8,128)(2,1)} %refs_1_.1, ...), custom_call_target="tpu_custom_call" | custom-call | tf_op jit(solution)/shard_map/states/pallas_call | solution.py:342
  1.4 1.6 %collective-permute-start.11 = (bf16[272,128]{1,0:T(8,128)(2,1)S(1)}, bf16[272,128]{1,0:T(8,128)(2,1)S(1)}, u32[]{:S(2)}, u32[]{:S(2)}) collective-permute-start(bf16[272,128]{1,0:T(8,128)(2,1)S(1)} %get-tuple-element.96), channel_id=1, source_target_pairs={{0,4},{4,0},{8,12},{12,8},{16,20},{20,16},{24,28},{28,24},{1,5},{5... | collective-permute-start | bytes 208904 | tf_op jit(solution)/shard_map/ppermute | solution.py:337
  3.0 1.6 %collective-permute-start.12 = (bf16[272,128]{1,0:T(8,128)(2,1)S(1)}, bf16[272,128]{1,0:T(8,128)(2,1)S(1)}, u32[]{:S(2)}, u32[]{:S(2)}) collective-permute-start(bf16[272,128]{1,0:T(8,128)(2,1)S(1)} %get-tuple-element.97.refs_3_), channel_id=1, source_target_pairs={{0,8},{4,12},{8,0},{12,4},{16,24},{20,28},{24,16},{28,20},{1,9},{5... | collective-permute-start | bytes 208904 | tf_op jit(solution)/shard_map/ppermute | solution.py:337
  4.5 0.4 %collective-permute-start.13 = (bf16[272,128]{1,0:T(8,128)(2,1)S(1)}, bf16[272,128]{1,0:T(8,128)(2,1)S(1)}, u32[]{:S(2)}, u32[]{:S(2)}) collective-permute-start(bf16[272,128]{1,0:T(8,128)(2,1)S(1)} %get-tuple-element.96), channel_id=1, source_target_pairs={{0,12},{4,8},{8,4},{12,0},{16,28},{20,24},{24,20},{28,16},{1,13},{... | collective-permute-start | bytes 208904 | tf_op jit(solution)/shard_map/ppermute | solution.py:337
  4.9 1.1 %collective-permute-done.11.refs_0_ = bf16[272,128]{1,0:T(8,128)(2,1)S(1)} collective-permute-done((bf16[272,128]{1,0:T(8,128)(2,1)S(1)}, bf16[272,128]{1,0:T(8,128)(2,1)S(1)}, u32[]{:S(2)}, u32[]{:S(2)}) %collective-permute-start.11) | collective-permute-done | bytes 69664 | tf_op jit(solution)/shard_map/ppermute | solution.py:337
  6.0 1.6 %collective-permute-done.12.refs_1_ = bf16[272,128]{1,0:T(8,128)(2,1)S(1)} collective-permute-done((bf16[272,128]{1,0:T(8,128)(2,1)S(1)}, bf16[272,128]{1,0:T(8,128)(2,1)S(1)}, u32[]{:S(2)}, u32[]{:S(2)}) %collective-permute-start.12) | collective-permute-done | bytes 69664 | tf_op jit(solution)/shard_map/ppermute | solution.py:337
  7.6 2.1 %collective-permute-done.13.refs_2_ = bf16[272,128]{1,0:T(8,128)(2,1)S(1)} collective-permute-done((bf16[272,128]{1,0:T(8,128)(2,1)S(1)}, bf16[272,128]{1,0:T(8,128)(2,1)S(1)}, u32[]{:S(2)}, u32[]{:S(2)}) %collective-permute-start.13) | collective-permute-done | bytes 69664 | tf_op jit(solution)/shard_map/ppermute | solution.py:337
  9.9 0.4 %collective-permute-start.14 = (bf16[256,128]{1,0:T(8,128)(2,1)S(1)}, bf16[256,128]{1,0:T(8,128)(2,1)S(1)}, u32[]{:S(2)}, u32[]{:S(2)}) collective-permute-start(bf16[256,128]{1,0:T(8,128)(2,1)S(1)} %get-tuple-element.100), channel_id=1, source_target_pairs={{0,16},{4,20},{8,24},{12,28},{16,0},{20,4},{24,8},{28,12},{1,17},{... | collective-permute-start | bytes 196616 | tf_op jit(solution)/shard_map/ppermute | solution.py:300
  10.3 0.5 %collective-permute-start.15 = (bf16[256,128]{1,0:T(8,128)(2,1)S(1)}, bf16[256,128]{1,0:T(8,128)(2,1)S(1)}, u32[]{:S(2)}, u32[]{:S(2)}) collective-permute-start(bf16[256,128]{1,0:T(8,128)(2,1)S(1)} %get-tuple-element.101), channel_id=1, source_target_pairs={{0,4},{4,0},{8,12},{12,8},{16,20},{20,16},{24,28},{28,24},{1,5},{5... | collective-permute-start | bytes 196616 | tf_op jit(solution)/shard_map/ppermute | solution.py:337
  10.8 0.7 %local.1 = (f32[256,512]{1,0:T(8,128)S(1)}, f32[256,4]{1,0:T(8,128)S(1)}) custom-call(f32[4,256]{1,0:T(4,128)S(1)} %get-tuple-element.90.decay_ref, bf16[256,512]{1,0:T(8,128)(2,1)S(1)} %get-tuple-element.89.query_ref, bf16[256,512]{1,0:T(8,128)(2,1)S(1)} %get-tuple-element.91.key_ref, bf16[256,512]{1,0:T(8,128)(2,1)S(1)} %get-tuple-element.92.value_ref), custom_call_target="tpu_custom_call" | custom-call | flops 134217728 | bytes 2000000 | tf_op jit(solution)/shard_map/local/pallas_call | solution.py:366
  11.5 3.6 %collective-permute-done.14.earlier_ref = bf16[256,128]{1,0:T(8,128)(2,1)S(1)} collective-permute-done((bf16[256,128]{1,0:T(8,128)(2,1)S(1)}, bf16[256,128]{1,0:T(8,128)(2,1)S(1)}, u32[]{:S(2)}, u32[]{:S(2)}) %collective-permute-start.14) | collective-permute-done | bytes 65568 | tf_op jit(solution)/shard_map/ppermute | solution.py:300
  15.2 15.4 %conditional.1 = (bf16[256,512]{1,0:T(8,128)(2,1)}) conditional(s32[]{:T(128)} %convert_element_type.3, (bf16[256,512]{1,0:T(8,128)(2,1)S(1)}, f32[256,512]{1,0:T(8,128)S(1)}, f32[256,4]{1,0:T(8,128)S(1)}, f32[1,512]{1,0:T(1,128)S(1)}, bf16[256,128]{1,0:T(8,128)(2,1)S(1)}, /*index=5*/bf16[272,128]{1,0:T(8,128)(2,1)S(1)}, bf16[512,2048]{1,0:T(8,128)(2,1)}, ...), branch_computations={%region_0.0_spmd, %region_1.0_spmd} | conditional | bytes 2375968 | solution.py:469
  15.2 0.6 %collective-permute-start.1 = (bf16[272,128]{1,0:T(8,128)(2,1)S(1)}, bf16[272,128]{1,0:T(8,128)(2,1)S(1)}, u32[]{:S(2)}, u32[]{:S(2)}) collective-permute-start(bf16[272,128]{1,0:T(8,128)(2,1)S(1)} %get-tuple-element.58), channel_id=1, source_target_pairs={{0,4},{4,0},{8,12},{12,8},{16,20},{20,16},{24,28},{28,24},{1,5},{5... | collective-permute-start | bytes 208904 | tf_op jit(solution)/shard_map/cond/branch_0_fun/ppermute | solution.py:337
  16.5 0.6 %collective-permute-start = (bf16[128,256]{1,0:T(8,128)(2,1)S(1)}, bf16[128,256]{1,0:T(8,128)(2,1)S(1)}, u32[]{:S(2)}, u32[]{:S(2)}) collective-permute-start(bf16[128,256]{1,0:T(8,128)(2,1)S(1)} %norm_mine_0.1.refs_0_), channel_id=1, source_target_pairs={{0,1},{1,0},{2,3},{3,2},{4,5},{5,4},{6,7},{7,6},{8,9},{9,8},{10,11... | collective-permute-start | bytes 196616 | tf_op jit(solution)/shard_map/cond/branch_0_fun/ppermute | solution.py:392
  17.0 1.1 %fetch_far.2 = (bf16[512,512]{1,0:T(8,128)(2,1)S(1)}, bf16[512,512]{1,0:T(8,128)(2,1)S(1)}) custom-call(bf16[512,2048]{1,0:T(8,128)(2,1)} %get-tuple-element.49.weight_hbm, bf16[512,2048]{1,0:T(8,128)(2,1)S(1)} %get-tuple-element.50.other_weight_hbm, bf16[128,256]{1,0:T(8,128)(2,1)S(1)} %norm_mine_1.1._.refs_2_.refs_4_), custom_call_target="tpu_custom_call" | custom-call | tf_op jit(solution)/shard_map/cond/branch_0_fun/fetch_far/pallas_call | solution.py:395
  18.4 1.1 %collective-permute-done.1.earlier_ref = bf16[272,128]{1,0:T(8,128)(2,1)S(1)} collective-permute-done((bf16[272,128]{1,0:T(8,128)(2,1)S(1)}, bf16[272,128]{1,0:T(8,128)(2,1)S(1)}, u32[]{:S(2)}, u32[]{:S(2)}) %collective-permute-start.1) | collective-permute-done | bytes 69664 | tf_op jit(solution)/shard_map/cond/branch_0_fun/ppermute | solution.py:337
  20.2 0.6 %collective-permute-start.3 = (bf16[128,256]{1,0:T(8,128)(2,1)S(1)}, bf16[128,256]{1,0:T(8,128)(2,1)S(1)}, u32[]{:S(2)}, u32[]{:S(2)}) collective-permute-start(bf16[128,256]{1,0:T(8,128)(2,1)S(1)} %norm_0.2.refs_2_.mine_ref), channel_id=1, source_target_pairs={{0,1},{1,0},{2,3},{3,2},{4,5},{5,4},{6,7},{7,6},{8,9},{9,8},{10,11... | collective-permute-start | bytes 196616 | tf_op jit(solution)/shard_map/cond/branch_0_fun/ppermute | solution.py:392
  20.8 0.4 %collective-permute-done.4.refs_7_.other_ref = bf16[128,256]{1,0:T(8,128)(2,1)S(1)} collective-permute-done((bf16[128,256]{1,0:T(8,128)(2,1)S(1)}, bf16[128,256]{1,0:T(8,128)(2,1)S(1)}, u32[]{:S(2)}, u32[]{:S(2)}) %collective-permute-start.4) | collective-permute-done | bytes 65568 | tf_op jit(solution)/shard_map/cond/branch_0_fun/ppermute | solution.py:392
  21.4 1.6 %collective-permute-start.6 = (bf16[128,512]{1,0:T(8,128)(2,1)S(1)}, bf16[128,512]{1,0:T(8,128)(2,1)S(1)}, u32[]{:S(2)}, u32[]{:S(2)}) collective-permute-start(bf16[128,512]{1,0:T(8,128)(2,1)S(1)} %project_far_1.2), channel_id=1, source_target_pairs={{0,2},{1,3},{2,0},{3,1},{4,6},{5,7},{6,4},{7,5},{8,10},{9,11},{10,... | collective-permute-start | bytes 393224 | tf_op jit(solution)/shard_map/cond/branch_0_fun/ppermute | solution.py:410
  23.2 0.6 %collective-permute-start.5 = (bf16[128,512]{1,0:T(8,128)(2,1)S(1)}, bf16[128,512]{1,0:T(8,128)(2,1)S(1)}, u32[]{:S(2)}, u32[]{:S(2)}) collective-permute-start(bf16[128,512]{1,0:T(8,128)(2,1)S(1)} %project_far_0.2), channel_id=1, source_target_pairs={{0,2},{1,3},{2,0},{3,1},{4,6},{5,7},{6,4},{7,5},{8,10},{9,11},{10,... | collective-permute-start | bytes 393224 | tf_op jit(solution)/shard_map/cond/branch_0_fun/ppermute | solution.py:410
  23.8 1.6 %project_near.2.near_ref = f32[256,512]{1,0:T(8,128)S(1)} custom-call(bf16[256,512]{1,0:T(8,128)(2,1)} %get-tuple-element.48.residual_hbm, bf16[512,2048]{1,0:T(8,128)(2,1)} %get-tuple-element.49.weight_hbm, bf16[512,2048]{1,0:T(8,128)(2,1)S(1)} %get-tuple-element.50.other_weight_hbm, bf16[128,256]{1,0:T(8,128)(2,1)S(1)} %norm_mine_0.1.refs_0_, ...), custom_call_target="tpu_custom_call" | custom-call | tf_op jit(solution)/shard_map/cond/branch_0_fun/project_near/pallas_call | solution.py:413
  25.4 2.4 %collective-permute-done.6.refs_1_ = bf16[128,512]{1,0:T(8,128)(2,1)S(1)} collective-permute-done((bf16[128,512]{1,0:T(8,128)(2,1)S(1)}, bf16[128,512]{1,0:T(8,128)(2,1)S(1)}, u32[]{:S(2)}, u32[]{:S(2)}) %collective-permute-start.6) | collective-permute-done | bytes 131104 | tf_op jit(solution)/shard_map/cond/branch_0_fun/ppermute | solution.py:410
  27.8 2.0 %collective-permute-done.5.refs_0_ = bf16[128,512]{1,0:T(8,128)(2,1)S(1)} collective-permute-done((bf16[128,512]{1,0:T(8,128)(2,1)S(1)}, bf16[128,512]{1,0:T(8,128)(2,1)S(1)}, u32[]{:S(2)}, u32[]{:S(2)}) %collective-permute-start.5) | collective-permute-done | bytes 131104 | tf_op jit(solution)/shard_map/cond/branch_0_fun/ppermute | solution.py:410
  29.9 0.7 %add.2 = bf16[256,512]{1,0:T(8,128)(2,1)} custom-call(f32[256,512]{1,0:T(8,128)S(1)} %project_near.2.near_ref, bf16[128,512]{1,0:T(8,128)(2,1)S(1)} %collective-permute-done.5.refs_0_, bf16[128,512]{1,0:T(8,128)(2,1)S(1)} %collective-permute-done.6.refs_1_), custom_call_target="tpu_custom_call" | custom-call | tf_op jit(solution)/shard_map/cond/branch_0_fun/add/pallas_call | solution.py:429
  (18 shorter events, 2.2 us)
Async XLA Ops:
  0.0 15.2 %collective-permute-start.16 = (bf16[512,2048]{1,0:T(8,128)(2,1)}, bf16[512,2048]{1,0:T(8,128)(2,1)S(1)}, u32[]{:S(2)}, u32[]{:S(2)}) collective-permute-start(bf16[512,2048]{1,0:T(8,128)(2,1)} %param.15), channel_id=1, source_target_pairs={{0,1},{1,0},{2,3},{3,2},{4,5},{5,4},{6,7},{7,6},{8,9},{9,8},{10,11... | collective-permute-start | bytes 6291464 | tf_op jit(solution)/shard_map/ppermute | solution.py:339
  1.4 4.7 %collective-permute-start.11 = (bf16[272,128]{1,0:T(8,128)(2,1)S(1)}, bf16[272,128]{1,0:T(8,128)(2,1)S(1)}, u32[]{:S(2)}, u32[]{:S(2)}) collective-permute-start(bf16[272,128]{1,0:T(8,128)(2,1)S(1)} %get-tuple-element.96), channel_id=1, source_target_pairs={{0,4},{4,0},{8,12},{12,8},{16,20},{20,16},{24,28},{28,24},{1,5},{5... | collective-permute-start | bytes 208904 | tf_op jit(solution)/shard_map/ppermute | solution.py:337
  3.0 4.6 %collective-permute-start.12 = (bf16[272,128]{1,0:T(8,128)(2,1)S(1)}, bf16[272,128]{1,0:T(8,128)(2,1)S(1)}, u32[]{:S(2)}, u32[]{:S(2)}) collective-permute-start(bf16[272,128]{1,0:T(8,128)(2,1)S(1)} %get-tuple-element.97.refs_3_), channel_id=1, source_target_pairs={{0,8},{4,12},{8,0},{12,4},{16,24},{20,28},{24,16},{28,20},{1,9},{5... | collective-permute-start | bytes 208904 | tf_op jit(solution)/shard_map/ppermute | solution.py:337
  4.5 5.2 %collective-permute-start.13 = (bf16[272,128]{1,0:T(8,128)(2,1)S(1)}, bf16[272,128]{1,0:T(8,128)(2,1)S(1)}, u32[]{:S(2)}, u32[]{:S(2)}) collective-permute-start(bf16[272,128]{1,0:T(8,128)(2,1)S(1)} %get-tuple-element.96), channel_id=1, source_target_pairs={{0,12},{4,8},{8,4},{12,0},{16,28},{20,24},{24,20},{28,16},{1,13},{... | collective-permute-start | bytes 208904 | tf_op jit(solution)/shard_map/ppermute | solution.py:337
  9.9 5.2 %collective-permute-start.14 = (bf16[256,128]{1,0:T(8,128)(2,1)S(1)}, bf16[256,128]{1,0:T(8,128)(2,1)S(1)}, u32[]{:S(2)}, u32[]{:S(2)}) collective-permute-start(bf16[256,128]{1,0:T(8,128)(2,1)S(1)} %get-tuple-element.100), channel_id=1, source_target_pairs={{0,16},{4,20},{8,24},{12,28},{16,0},{20,4},{24,8},{28,12},{1,17},{... | collective-permute-start | bytes 196616 | tf_op jit(solution)/shard_map/ppermute | solution.py:300
  10.3 4.8 %collective-permute-start.15 = (bf16[256,128]{1,0:T(8,128)(2,1)S(1)}, bf16[256,128]{1,0:T(8,128)(2,1)S(1)}, u32[]{:S(2)}, u32[]{:S(2)}) collective-permute-start(bf16[256,128]{1,0:T(8,128)(2,1)S(1)} %get-tuple-element.101), channel_id=1, source_target_pairs={{0,4},{4,0},{8,12},{12,8},{16,20},{20,16},{24,28},{28,24},{1,5},{5... | collective-permute-start | bytes 196616 | tf_op jit(solution)/shard_map/ppermute | solution.py:337
  15.2 4.4 %collective-permute-start.1 = (bf16[272,128]{1,0:T(8,128)(2,1)S(1)}, bf16[272,128]{1,0:T(8,128)(2,1)S(1)}, u32[]{:S(2)}, u32[]{:S(2)}) collective-permute-start(bf16[272,128]{1,0:T(8,128)(2,1)S(1)} %get-tuple-element.58), channel_id=1, source_target_pairs={{0,4},{4,0},{8,12},{12,8},{16,20},{20,16},{24,28},{28,24},{1,5},{5... | collective-permute-start | bytes 208904 | tf_op jit(solution)/shard_map/cond/branch_0_fun/ppermute | solution.py:337
  16.1 2.0 %collective-permute-start.2 = (bf16[128,256]{1,0:T(8,128)(2,1)S(1)}, bf16[128,256]{1,0:T(8,128)(2,1)S(1)}, u32[]{:S(2)}, u32[]{:S(2)}) collective-permute-start(bf16[128,256]{1,0:T(8,128)(2,1)S(1)} %norm_mine_1.1._.refs_2_.refs_4_), channel_id=1, source_target_pairs={{0,1},{1,0},{2,3},{3,2},{4,5},{5,4},{6,7},{7,6},{8,9},{9,8},{10,11... | collective-permute-start | bytes 196616 | tf_op jit(solution)/shard_map/cond/branch_0_fun/ppermute | solution.py:392
  16.5 1.6 %collective-permute-start = (bf16[128,256]{1,0:T(8,128)(2,1)S(1)}, bf16[128,256]{1,0:T(8,128)(2,1)S(1)}, u32[]{:S(2)}, u32[]{:S(2)}) collective-permute-start(bf16[128,256]{1,0:T(8,128)(2,1)S(1)} %norm_mine_0.1.refs_0_), channel_id=1, source_target_pairs={{0,1},{1,0},{2,3},{3,2},{4,5},{5,4},{6,7},{7,6},{8,9},{9,8},{10,11... | collective-permute-start | bytes 196616 | tf_op jit(solution)/shard_map/cond/branch_0_fun/ppermute | solution.py:392
  19.9 1.3 %collective-permute-start.4 = (bf16[128,256]{1,0:T(8,128)(2,1)S(1)}, bf16[128,256]{1,0:T(8,128)(2,1)S(1)}, u32[]{:S(2)}, u32[]{:S(2)}) collective-permute-start(bf16[128,256]{1,0:T(8,128)(2,1)S(1)} %norm_1.2.refs_6_.mine_ref), channel_id=1, source_target_pairs={{0,1},{1,0},{2,3},{3,2},{4,5},{5,4},{6,7},{7,6},{8,9},{9,8},{10,11... | collective-permute-start | bytes 196616 | tf_op jit(solution)/shard_map/cond/branch_0_fun/ppermute | solution.py:392
  20.2 2.8 %collective-permute-start.3 = (bf16[128,256]{1,0:T(8,128)(2,1)S(1)}, bf16[128,256]{1,0:T(8,128)(2,1)S(1)}, u32[]{:S(2)}, u32[]{:S(2)}) collective-permute-start(bf16[128,256]{1,0:T(8,128)(2,1)S(1)} %norm_0.2.refs_2_.mine_ref), channel_id=1, source_target_pairs={{0,1},{1,0},{2,3},{3,2},{4,5},{5,4},{6,7},{7,6},{8,9},{9,8},{10,11... | collective-permute-start | bytes 196616 | tf_op jit(solution)/shard_map/cond/branch_0_fun/ppermute | solution.py:392
  21.4 6.4 %collective-permute-start.6 = (bf16[128,512]{1,0:T(8,128)(2,1)S(1)}, bf16[128,512]{1,0:T(8,128)(2,1)S(1)}, u32[]{:S(2)}, u32[]{:S(2)}) collective-permute-start(bf16[128,512]{1,0:T(8,128)(2,1)S(1)} %project_far_1.2), channel_id=1, source_target_pairs={{0,2},{1,3},{2,0},{3,1},{4,6},{5,7},{6,4},{7,5},{8,10},{9,11},{10,... | collective-permute-start | bytes 393224 | tf_op jit(solution)/shard_map/cond/branch_0_fun/ppermute | solution.py:410
  23.2 6.6 %collective-permute-start.5 = (bf16[128,512]{1,0:T(8,128)(2,1)S(1)}, bf16[128,512]{1,0:T(8,128)(2,1)S(1)}, u32[]{:S(2)}, u32[]{:S(2)}) collective-permute-start(bf16[128,512]{1,0:T(8,128)(2,1)S(1)} %project_far_0.2), channel_id=1, source_target_pairs={{0,2},{1,3},{2,0},{3,1},{4,6},{5,7},{6,4},{7,5},{8,10},{9,11},{10,... | collective-permute-start | bytes 393224 | tf_op jit(solution)/shard_map/cond/branch_0_fun/ppermute | solution.py:410
